TPU v7x, 32 devices: a whole 2x2x4 slice. The times are simulated.
32 devices in a mesh: cell: 32 (over z, y, x, core).
Axes of the slice: x: 2, y: 2, z: 4, core: 2. Of those that a mesh axis runs over, the one named last changes fastest.
Arguments:
- features: bfloat16 [8192, 512], P('cell'), may hold values from -6 to 6
- radial: bfloat16 [8192, 8, 128], P('cell'), may hold values from 0 to 1
- neighbours: int32 [8192, 8], P('cell'), may hold values from 0 to 8191, as said below
- counts: int32 [8192], P('cell'), may hold values from 1 to 8, as said below
- cotangent: bfloat16 [8192, 8, 256], P('cell'), may hold values from -6 to 6
- w_self: bfloat16 [512, 512], replicated, may hold values from -0.25 to 0.25
- w_neighbour: bfloat16 [512, 512], replicated, may hold values from -0.25 to 0.25
- w_radial: bfloat16 [128, 512], replicated, may hold values from -0.5 to 0.5
- w_block: bfloat16 [512, 256], replicated, may hold values from -0.25 to 0.25
Outputs:
- blocks: bfloat16 [8192, 8, 256], P('cell')
- feat_grad: bfloat16 [8192, 512], P('cell')
Inputs may be any that keep to these rules, and one draw needn't show every extreme that they name: `neighbours`: each neighbour index differs from its atom's index by 1 to 128. Only the first counts[i] slots of atom i are live, the rest are padding.
All inputs are finite; a program needn't handle non-finite values.
Results may differ from a plain program's by a relative error of at most 0.013.
Values may be sent and summed in bfloat16 or wider, within the bound.
No kernel may reach another device: no remote copies, remote signals or barrier semaphores. Data moves between devices by JAX's collectives and lax.ppermute only.
A program may use at most 64 MiB of HBM per device.

v0:
```python
import math

import jax
import jax.numpy as jnp
from jax import lax
from jax.sharding import PartitionSpec as P


def extended(block, sides, width):
    for axis, dim in sides:
        count = lax.axis_size(axis)
        forward = [(i, i + 1) for i in range(count - 1)]
        backward = [(target, source) for source, target in forward]
        low = lax.ppermute(
            lax.slice_in_dim(block, block.shape[dim] - width, None, axis=dim), axis, forward
        )
        high = lax.ppermute(lax.slice_in_dim(block, 0, width, axis=dim), axis, backward)
        block = jnp.concatenate([low, block, high], axis=dim)
    return block


def shifted(value, axis, steps):
    count = lax.axis_size(axis)
    initial, last = (max(0, -steps), min(count, count - steps))
    return lax.ppermute(value, axis, [(source, source + steps) for source in range(initial, last)])


def window_pick(table, rows, atoms_per, slot_count, step, width):
    block_total = rows.shape[0] // (atoms_per * slot_count)
    grouped = rows.reshape(block_total, atoms_per * slot_count)
    columns = jnp.arange(width, dtype=jnp.int32)

    def one_block(packed):
        index, ids = packed
        start = index * step
        window = lax.dynamic_slice_in_dim(table, start, width, 0)
        picker = ((ids - start)[:, None] == columns[None, :]).astype(jnp.bfloat16)
        return jnp.dot(picker, window, preferred_element_type=jnp.float32).astype(jnp.bfloat16)

    picked = lax.map(one_block, (jnp.arange(block_total, dtype=jnp.int32), grouped))
    return picked.reshape(-1, table.shape[1])


def window_add(values, rows, total_rows, atoms_per, slot_count, step, width):
    feat_width = values.shape[1]
    block_total = rows.shape[0] // (atoms_per * slot_count)
    grouped = rows.reshape(block_total, atoms_per * slot_count)
    grouped_vals = values.reshape(block_total, atoms_per * slot_count, feat_width)
    columns = jnp.arange(width, dtype=jnp.int32)
    contract = (((0,), (0,)), ((), ()))

    def one_block(carry, packed):
        index, ids, block_vals = packed
        start = index * step
        picker = ((ids - start)[:, None] == columns[None, :]).astype(jnp.bfloat16)
        high = block_vals.astype(jnp.bfloat16)
        low = (block_vals - high.astype(jnp.float32)).astype(jnp.bfloat16)
        added = lax.dot_general(picker, high, contract, preferred_element_type=jnp.float32)
        added = added + lax.dot_general(picker, low, contract, preferred_element_type=jnp.float32)
        window = lax.dynamic_slice_in_dim(carry, start, width, 0)
        carry = lax.dynamic_update_slice_in_dim(carry, window + added, start, 0)
        return (carry, None)

    start_sum = jnp.zeros((total_rows, feat_width), jnp.float32)
    summed, unused = lax.scan(
        one_block, start_sum, (jnp.arange(block_total, dtype=jnp.int32), grouped, grouped_vals)
    )
    return summed


def body(features, radial, neighbours, counts, cotangent, w_self, w_neighbour, w_radial, w_block):
    atoms_here = features.shape[0]
    feat_width = features.shape[1]
    slot_count = neighbours.shape[1]
    block_width = w_block.shape[1]
    radial_width = radial.shape[2]
    margin = atoms_here // 2
    atom_block = math.gcd(atoms_here, 128)
    window_rows = atom_block + 2 * margin
    offset = lax.axis_index("cell") * atoms_here - margin
    local_rows = (neighbours - offset).reshape(-1)
    self_proj = jnp.dot(features, w_self, preferred_element_type=jnp.float32).astype(jnp.bfloat16)
    padded_feat = extended(features, (("cell", 0),), margin)
    padded_proj = jnp.dot(padded_feat, w_neighbour, preferred_element_type=jnp.float32).astype(
        jnp.bfloat16
    )
    gathered = window_pick(padded_proj, local_rows, atom_block, slot_count, atom_block, window_rows)
    gathered = gathered.reshape(atoms_here, slot_count, feat_width)
    radial_flat = radial.reshape(-1, radial_width)
    radial_gate = jnp.dot(radial_flat, w_radial, preferred_element_type=jnp.float32).reshape(
        atoms_here, slot_count, feat_width
    )
    slot_index = jnp.arange(slot_count, dtype=jnp.int32)
    live_mask = (slot_index[None, :] < counts[:, None]).astype(jnp.float32)[:, :, None]
    pre_act = (
        self_proj.astype(jnp.float32)[:, None, :] + gathered.astype(jnp.float32)
    ) * radial_gate
    message = (jax.nn.silu(pre_act) * live_mask).astype(jnp.bfloat16)
    blocks = jnp.dot(
        message.reshape(-1, feat_width), w_block, preferred_element_type=jnp.float32
    ).astype(jnp.bfloat16)
    blocks = blocks.reshape(atoms_here, slot_count, block_width)
    d_message = jnp.dot(
        cotangent.reshape(-1, block_width), w_block.T, preferred_element_type=jnp.float32
    )
    d_message = d_message.reshape(atoms_here, slot_count, feat_width)
    sigmoid_val = jax.nn.sigmoid(pre_act)
    adjoint = (
        d_message * live_mask * (sigmoid_val * (1.0 + pre_act * (1.0 - sigmoid_val))) * radial_gate
    )
    self_adj = jnp.sum(adjoint, axis=1).astype(jnp.bfloat16)
    padded_adj = window_add(
        adjoint.reshape(-1, feat_width),
        local_rows,
        atoms_here + 2 * margin,
        atom_block,
        slot_count,
        atom_block,
        window_rows,
    )
    lower_rim = padded_adj[:margin]
    own_adj = padded_adj[margin : margin + atoms_here]
    upper_rim = padded_adj[margin + atoms_here :]
    from_above = shifted(lower_rim.astype(jnp.bfloat16), "cell", -1).astype(lower_rim.dtype)
    from_below = shifted(upper_rim.astype(jnp.bfloat16), "cell", 1).astype(upper_rim.dtype)
    summed_adj = own_adj + jnp.concatenate([from_below, from_above], axis=0)
    nbr_adj = summed_adj.astype(jnp.bfloat16)
    feat_grad = jnp.dot(self_adj, w_self.T, preferred_element_type=jnp.float32) + jnp.dot(
        nbr_adj, w_neighbour.T, preferred_element_type=jnp.float32
    )
    return (blocks, feat_grad.astype(jnp.bfloat16))


def solution(mesh):
    in_specs = (
        P("cell", None),
        P("cell", None, None),
        P("cell", None),
        P("cell"),
        P("cell", None, None),
        P(),
        P(),
        P(),
        P(),
    )
    out_specs = (P("cell", None, None), P("cell", None))
    return jax.shard_map(body, mesh=mesh, in_specs=in_specs, out_specs=out_specs, check_vma=False)
```

profile of v0, /device:TPU:8, one launch (start us, length us, event | category | flops | bytes accessed | tf_op | source)
XLA Modules:
  0.0 61.1 jit_solution(8874810864672390365)
XLA Ops:
  0.6 1.0 %fusion.49 = (bf16[128,512]{1,0:T(8,128)(2,1)S(1)}, bf16[128,512]{1,0:T(8,128)(2,1)S(1)}) fusion(bf16[256,512]{1,0:T(8,128)(2,1)} %param.13), kind=kLoop, calls=%fused_computation.61 | loop fusion | bytes 524288 | tf_op jit(solution)/shard_map/slice | solution.py:15
  1.7 3.7 %collective-permute-start.1 = (bf16[128,512]{1,0:T(8,128)(2,1)S(1)}, bf16[128,512]{1,0:T(8,128)(2,1)S(1)}, u32[]{:S(2)}, u32[]{:S(2)}) collective-permute-start(bf16[128,512]{1,0:T(8,128)(2,1)S(1)} %get-tuple-element.115), channel_id=1, source_target_pairs={{1,0},{2,1},{3,2},{4,3},{5,4},{6,5},{7,6},{8,7},{9,8},{10,9},{11,1... | collective-permute-start | bytes 393224 | tf_op jit(solution)/shard_map/ppermute | solution.py:17
  5.4 1.9 %collective-permute-start = (bf16[128,512]{1,0:T(8,128)(2,1)S(1)}, bf16[128,512]{1,0:T(8,128)(2,1)}, u32[]{:S(2)}, u32[]{:S(2)}) collective-permute-start(bf16[128,512]{1,0:T(8,128)(2,1)S(1)} %get-tuple-element.114), channel_id=1, source_target_pairs={{0,1},{1,2},{2,3},{3,4},{4,5},{5,6},{6,7},{7,8},{8,9},{9,10},{10,1... | collective-permute-start | bytes 393224 | tf_op jit(solution)/shard_map/ppermute | solution.py:14
  7.3 0.7 %broadcast_subtract_fusion = s32[256,8]{0,1:T(8,128)S(1)} fusion(s32[256,8]{0,1:T(8,128)} %param.15, s32[]{:T(128)S(6)} %sub.41), kind=kLoop, calls=%fused_computation.57 | loop fusion | flops 2048 | bytes 16388 | tf_op jit(solution)/shard_map/sub | solution.py:81
  8.3 1.4 %fusion.29 = f32[256,512]{1,0:T(8,128)S(1)} fusion(bf16[256,512]{1,0:T(8,128)(2,1)} %param.13, bf16[512,512]{1,0:T(8,128)(2,1)} %param.18), kind=kOutput, calls=%fused_computation.38 | convolution fusion | flops 134479872 | bytes 1310720 | tf_op jit(solution)/shard_map/dot_general | solution.py:82
  9.7 0.7 %fusion.45 = f32[256,8]{0,1:T(8,128)S(1)} fusion(s32[256]{0:T(256)} %param.16), kind=kLoop, calls=%fused_computation.56 | loop fusion | flops 4096 | bytes 9216 | tf_op jit(solution)/shard_map/convert_element_type | solution.py:94
  10.4 3.2 %collective-permute-done = bf16[128,512]{1,0:T(8,128)(2,1)} collective-permute-done((bf16[128,512]{1,0:T(8,128)(2,1)S(1)}, bf16[128,512]{1,0:T(8,128)(2,1)}, u32[]{:S(2)}, u32[]{:S(2)}) %collective-permute-start) | collective-permute-done | bytes 131104 | tf_op jit(solution)/shard_map/ppermute | solution.py:14
  13.6 2.2 %convolution_convert_fusion.1 = bf16[512,512]{1,0:T(8,128)(2,1)} fusion(bf16[512,512]{1,0:T(8,128)(2,1)S(1)} %copy-done, bf16[128,512]{1,0:T(8,128)(2,1)S(1)} %collective-permute-done.1, bf16[256,512]{1,0:T(8,128)(2,1)} %param.13, bf16[128,512]{1,0:T(8,128)(2,1)} %collective-permute-done), kind=kOutput, calls=%fused_computation.34 | convolution fusion | flops 270270464 | bytes 1572864 | tf_op jit(solution)/shard_map/dot_general | solution.py:84
  15.8 5.9 %while.22 = (s32[]{:T(128)}, bf16[2,1024,512]{2,1,0:T(8,128)(2,1)S(1)}, s32[2,1024]{1,0:T(2,128)S(1)}, s32[2]{0:T(128)S(1)}, bf16[512,512]{1,0:T(8,128)(2,1)}, /...) while((s32[]{:T(128)}, bf16[2,1024,512]{2,1,0:T(8,128)(2,1)S(1)}, s32[2,1024]{1,0:T(2,128)S(1)}, ...), condition=%wide.region_1.2_spmd.clone, body=%wide.region_0.1_spmd.clone.sunk | while | flops 403571712 | bytes 1454255 | solution.py:40
  17.0 1.8 %fusion.65 = bf16[2,1024,512]{2,1,0:T(8,128)(2,1)S(1)} fusion(bf16[2,1024,512]{2,1,0:T(8,128)(2,1)S(1)} %get-tuple-element.192, s32[]{:T(128)S(6)} %copy.45, s32[1024]{0:T(1024)S(1)} %bitcast.63, bf16[512,512]{1,0:T(8,128)(2,1)} %get-tuple-element.204, s32[]{:T(128)S(6)} %select_n.11), kind=kOutput, calls=%fused_computation.6.clone.1 | convolution fusion | flops 403570688 | bytes 1445896 | tf_op jit(solution)/shard_map/while/body/eval_jaxpr/dot_general | solution.py:38
  19.9 1.8 %fusion.65 = bf16[2,1024,512]{2,1,0:T(8,128)(2,1)S(1)} fusion(bf16[2,1024,512]{2,1,0:T(8,128)(2,1)S(1)} %get-tuple-element.192, s32[]{:T(128)S(6)} %copy.45, s32[1024]{0:T(1024)S(1)} %bitcast.63, bf16[512,512]{1,0:T(8,128)(2,1)} %get-tuple-element.204, s32[]{:T(128)S(6)} %select_n.11), kind=kOutput, calls=%fused_computation.6.clone.1 | convolution fusion | flops 403570688 | bytes 1445896 | tf_op jit(solution)/shard_map/while/body/eval_jaxpr/dot_general | solution.py:38
  22.8 3.0 %multiply_convert_fusion = (bf16[256,8,512]{2,0,1:T(8,128)(2,1)S(1)}, f32[256,8,512]{2,0,1:T(8,128)S(1)}) fusion(f32[256,8,512]{2,1,0:T(8,128)S(1)} %convert.7, f32[256,8]{0,1:T(8,128)S(1)} %fusion.45, f32[256,512]{1,0:T(8,128)S(1)} %fusion.29, bf16[128,512]{1,0:T(8,128)(2,1)S(1)} %copy-done.5, bf16[256,8,128]{2,1,0:T(8,128)(2,1)S(1)} %copy-done.3), kind=kOutput, calls=%fused_computation.28 | convolution fusion | flops 276824064 | bytes 11673600 | tf_op jit(solution)/shard_map/dot_general | solution.py:90
  25.8 2.3 %fusion.25 = bf16[256,8,256]{2,1,0:T(8,128)(2,1)} fusion(bf16[512,256]{1,0:T(8,128)(2,1)S(1)} %copy-done.4, bf16[256,8,512]{2,0,1:T(8,128)(2,1)S(1)} %get-tuple-element.116), kind=kOutput, calls=%fused_computation.33 | convolution fusion | flops 537395200 | bytes 3407872 | tf_op jit(solution)/shard_map/dot_general | solution.py:99
  28.1 4.1 %fusion.50 = (bf16[256,512]{1,0:T(8,128)(2,1)S(1)}, f32[256,8,512]{2,0,1:T(8,128)S(1)}) fusion(f32[256,8,512]{2,0,1:T(8,128)S(1)} %get-tuple-element.117, f32[256,8,512]{2,1,0:T(8,128)S(1)} %convert.7, f32[256,512]{1,0:T(8,128)S(1)} %fusion.29, f32[256,8]{0,1:T(8,128)S(1)} %fusion.45, bf16[512,256]{1,0:T(8,128)(2,1)S(1)} %copy-done.4, ...), kind=kOutput, calls=%fused_computation.62 | convolution fusion | flops 550371328 | bytes 14688256 | tf_op jit(solution)/shard_map/dot_general | solution.py:103
  32.2 4.4 %copy.19 = f32[256,8,512]{2,1,0:T(8,128)} copy(f32[256,8,512]{2,0,1:T(8,128)S(1)} %get-tuple-element.119) | data formatting | bytes 8388608 | tf_op jit(solution)/shard_map/mul | solution.py:109
  36.8 12.8 %while.23 = (s32[]{:T(128)}, f32[512,512]{1,0:T(8,128)S(1)}, s32[2]{0:T(128)S(1)}, s32[2,1024]{1,0:T(2,128)S(1)}, f32[2,1024,512]{2,1,0:T(8,128)}, /*index=5*/s32[]{:T(128)}, s32[1]{0:T(128)}, s32[]{:T(128)}, s32[]{:T(128)}) while((s32[]{:T(128)}, f32[512,512]{1,0:T(8,128)S(1)}, s32[2]{0:T(128)S(1)}, s32[2,1024]{1,0:T(2,128)S(1)}, ...), condition=%wide.region_4.5_spmd.clone, body=%wide.region_3.4_spmd.clone.sunk | while | flops 808584192 | bytes 6308019 | solution.py:65
  38.0 2.5 %fusion.67 = f32[384,512]{1,0:T(8,128)S(1)} fusion(f32[2,1024,512]{2,1,0:T(8,128)} %get-tuple-element.231, s32[]{:T(128)S(6)} %copy.51, s32[1024]{0:T(1024)S(1)} %bitcast.61), kind=kOutput, calls=%fused_computation.15.clone.1 | convolution fusion | flops 405143552 | bytes 2887684 | tf_op jit(solution)/shard_map/while/body/eval_jaxpr/dot_general | solution.py:59
  40.6 2.6 %fusion.68 = f32[512,512]{1,0:T(8,128)S(1)} fusion(f32[512,512]{1,0:T(8,128)S(1)} %get-tuple-element.219, s32[]{:T(128)S(6)} %select_n.12, f32[384,512]{1,0:T(8,128)S(1)} %fusion.67, s32[1024]{0:T(1024)S(1)} %bitcast.62, f32[2,1024,512]{2,1,0:T(8,128)} %get-tuple-element.231, s32[]{:T(128)S(6)} %copy.51), kind=kOutput, calls=%fused_computation.19.clone.1 | convolution fusion | flops 403439616 | bytes 3411976 | tf_op jit(solution)/shard_map/while/body/eval_jaxpr/dot_general | solution.py:58
  44.4 2.5 %fusion.67 = f32[384,512]{1,0:T(8,128)S(1)} fusion(f32[2,1024,512]{2,1,0:T(8,128)} %get-tuple-element.231, s32[]{:T(128)S(6)} %copy.51, s32[1024]{0:T(1024)S(1)} %bitcast.61), kind=kOutput, calls=%fused_computation.15.clone.1 | convolution fusion | flops 405143552 | bytes 2887684 | tf_op jit(solution)/shard_map/while/body/eval_jaxpr/dot_general | solution.py:59
  47.0 2.6 %fusion.68 = f32[512,512]{1,0:T(8,128)S(1)} fusion(f32[512,512]{1,0:T(8,128)S(1)} %get-tuple-element.219, s32[]{:T(128)S(6)} %select_n.12, f32[384,512]{1,0:T(8,128)S(1)} %fusion.67, s32[1024]{0:T(1024)S(1)} %bitcast.62, f32[2,1024,512]{2,1,0:T(8,128)} %get-tuple-element.231, s32[]{:T(128)S(6)} %copy.51), kind=kOutput, calls=%fused_computation.19.clone.1 | convolution fusion | flops 403439616 | bytes 3411976 | tf_op jit(solution)/shard_map/while/body/eval_jaxpr/dot_general | solution.py:58
  49.7 2.3 %collective-permute-start.3 = (bf16[128,512]{1,0:T(8,128)(2,1)S(1)}, bf16[128,512]{1,0:T(8,128)(2,1)S(1)}, u32[]{:S(2)}, u32[]{:S(2)}) collective-permute-start(bf16[128,512]{1,0:T(8,128)(2,1)S(1)} %get-tuple-element.113), channel_id=1, source_target_pairs={{1,0},{2,1},{3,2},{4,3},{5,4},{6,5},{7,6},{8,7},{9,8},{10,9},{11,1... | collective-permute-start | bytes 393224 | tf_op jit(solution)/shard_map/ppermute | solution.py:25
  51.9 2.0 %collective-permute-start.2 = (bf16[128,512]{1,0:T(8,128)(2,1)S(1)}, bf16[128,512]{1,0:T(8,128)(2,1)S(1)}, u32[]{:S(2)}, u32[]{:S(2)}) collective-permute-start(bf16[128,512]{1,0:T(8,128)(2,1)S(1)} %get-tuple-element.112), channel_id=1, source_target_pairs={{0,1},{1,2},{2,3},{3,4},{4,5},{5,6},{6,7},{7,8},{8,9},{9,10},{10,1... | collective-permute-start | bytes 393224 | tf_op jit(solution)/shard_map/ppermute | solution.py:25
  54.5 5.6 %collective-permute-done.2 = bf16[128,512]{1,0:T(8,128)(2,1)S(1)} collective-permute-done((bf16[128,512]{1,0:T(8,128)(2,1)S(1)}, bf16[128,512]{1,0:T(8,128)(2,1)S(1)}, u32[]{:S(2)}, u32[]{:S(2)}) %collective-permute-start.2) | collective-permute-done | bytes 131104 | tf_op jit(solution)/shard_map/ppermute | solution.py:25
  60.0 1.0 %fusion.28 = bf16[256,512]{1,0:T(8,128)(2,1)} fusion(f32[256,512]{1,0:T(8,128)S(1)} %fusion.51, bf16[512,512]{1,0:T(8,128)(2,1)S(1)} %copy-done, f32[512,512]{1,0:T(8,128)S(1)} %get-tuple-element.67, bf16[128,512]{1,0:T(8,128)(2,1)S(1)} %collective-permute-done.3, bf16[128,512]{1,0:T(8,128)(2,1)S(1)} %collective-permute-done.2), kind=kOutput, calls=%fused_computation.36 | convolution fusion | flops 135266304 | bytes 2097152 | tf_op jit(solution)/shard_map/dot_general | solution.py:128
  (32 shorter events, 4.3 us)
Async XLA Ops:
  0.6 12.9 %copy-start = (bf16[512,512]{1,0:T(8,128)(2,1)S(1)}, bf16[512,512]{1,0:T(8,128)(2,1)}, u32[]{:S(2)}) copy-start(bf16[512,512]{1,0:T(8,128)(2,1)} %param.19) | copy-start | bytes 1572868
  1.7 8.7 %collective-permute-start.1 = (bf16[128,512]{1,0:T(8,128)(2,1)S(1)}, bf16[128,512]{1,0:T(8,128)(2,1)S(1)}, u32[]{:S(2)}, u32[]{:S(2)}) collective-permute-start(bf16[128,512]{1,0:T(8,128)(2,1)S(1)} %get-tuple-element.115), channel_id=1, source_target_pairs={{1,0},{2,1},{3,2},{4,3},{5,4},{6,5},{7,6},{8,7},{9,8},{10,9},{11,1... | collective-permute-start | bytes 393224 | tf_op jit(solution)/shard_map/ppermute | solution.py:17
  5.4 8.2 %collective-permute-start = (bf16[128,512]{1,0:T(8,128)(2,1)S(1)}, bf16[128,512]{1,0:T(8,128)(2,1)}, u32[]{:S(2)}, u32[]{:S(2)}) collective-permute-start(bf16[128,512]{1,0:T(8,128)(2,1)S(1)} %get-tuple-element.114), channel_id=1, source_target_pairs={{0,1},{1,2},{2,3},{3,4},{4,5},{5,6},{6,7},{7,8},{8,9},{9,10},{10,1... | collective-permute-start | bytes 393224 | tf_op jit(solution)/shard_map/ppermute | solution.py:14
  21.7 1.0 %copy-start.3 = (bf16[256,8,128]{2,1,0:T(8,128)(2,1)S(1)}, bf16[256,8,128]{2,1,0:T(8,128)(2,1)}, u32[]{:S(2)}) copy-start(bf16[256,8,128]{2,1,0:T(8,128)(2,1)} %param.14) | copy-start | bytes 1572868
  21.7 1.1 %copy-start.5 = (bf16[128,512]{1,0:T(8,128)(2,1)S(1)}, bf16[128,512]{1,0:T(8,128)(2,1)}, u32[]{:S(2)}) copy-start(bf16[128,512]{1,0:T(8,128)(2,1)} %param.20) | copy-start | bytes 393220
  22.8 3.0 %copy-start.4 = (bf16[512,256]{1,0:T(8,128)(2,1)S(1)}, bf16[512,256]{1,0:T(8,128)(2,1)}, u32[]{:S(2)}) copy-start(bf16[512,256]{1,0:T(8,128)(2,1)} %param.21) | copy-start | bytes 786436
  22.8 5.4 %copy-start.2 = (bf16[256,8,256]{2,1,0:T(8,128)(2,1)S(1)}, bf16[256,8,256]{2,1,0:T(8,128)(2,1)}, u32[]{:S(2)}) copy-start(bf16[256,8,256]{2,1,0:T(8,128)(2,1)} %param.17) | copy-start | bytes 3145732
  36.8 17.3 %copy-start.1 = (bf16[512,512]{1,0:T(8,128)(2,1)S(1)}, bf16[512,512]{1,0:T(8,128)(2,1)}, u32[]{:S(2)}) copy-start(bf16[512,512]{1,0:T(8,128)(2,1)} %param.18) | copy-start | bytes 1572868
  49.7 4.8 %collective-permute-start.3 = (bf16[128,512]{1,0:T(8,128)(2,1)S(1)}, bf16[128,512]{1,0:T(8,128)(2,1)S(1)}, u32[]{:S(2)}, u32[]{:S(2)}) collective-permute-start(bf16[128,512]{1,0:T(8,128)(2,1)S(1)} %get-tuple-element.113), channel_id=1, source_target_pairs={{1,0},{2,1},{3,2},{4,3},{5,4},{6,5},{7,6},{8,7},{9,8},{10,9},{11,1... | collective-permute-start | bytes 393224 | tf_op jit(solution)/shard_map/ppermute | solution.py:25
  51.9 8.1 %collective-permute-start.2 = (bf16[128,512]{1,0:T(8,128)(2,1)S(1)}, bf16[128,512]{1,0:T(8,128)(2,1)S(1)}, u32[]{:S(2)}, u32[]{:S(2)}) collective-permute-start(bf16[128,512]{1,0:T(8,128)(2,1)S(1)} %get-tuple-element.112), channel_id=1, source_target_pairs={{0,1},{1,2},{2,3},{3,4},{4,5},{5,6},{6,7},{7,8},{8,9},{9,10},{10,1... | collective-permute-start | bytes 393224 | tf_op jit(solution)/shard_map/ppermute | solution.py:25
where the time goes:
time: 61.6 us; the launch traced here: 61.1 us
  matrix products  28.2 us (46%)
  starting transfers between devices  9.93 us (16%)
  waiting for transfers between devices  8.86 us (14%)
  local copies, waits for them, and re-layouts  8.63 us (14%)
  loops' own time  2.58 us (4%)
  other arithmetic  2.09 us (3%)
  between operations  0.82 us (1%)
    ppermute x2, waiting for transfers between devices, shifted(): lax.ppermute(value, axis, [(source, source + steps) for source in range(i...  5.68 us
    dot_general x2, matrix products, one_block(): lax.dot_general(picker, high, contract, preferred_element_type=jnp.float32)  5.12 us
    dot_general x2, matrix products, one_block(): lax.dot_general(picker, low, contract, preferred_element_type=jnp.float32)  5.08 us
    mul x1, local copies, waits for them, and re-layouts, body(): d_message * live_mask  4.38 us
    ppermute x2, starting transfers between devices, shifted(): lax.ppermute(value, axis, [(source, source + steps) for source in range(i...  4.33 us
    dot_general x1, matrix products, body(): jnp.dot(cotangent.reshape(-1, block_width), w_block.T, preferred_element_...  4.11 us
    ppermute x1, starting transfers between devices, extended(): lax.ppermute(lax.slice_in_dim(block, 0, width, axis=dim), axis, backward)  3.68 us
    dot_general x2, matrix products, one_block(): jnp.dot(picker, window, preferred_element_type=jnp.float32)  3.51 us
  transfers between devices with their start and end apart: 4, of which 3 were waited for; matrix products, arithmetic and copies ran while one was open for 6% of the time, Pallas kernels for 0%

commit v1 on v0

v1 whole, which is shorter than its diff:
```python
import functools

import jax
import jax.numpy as jnp
from jax import lax
from jax.experimental import pallas as pl
from jax.experimental.pallas import tpu as pltpu
from jax.sharding import PartitionSpec as P

BF = jnp.bfloat16
F32 = jnp.float32


def mm(a, b):
    return jnp.dot(a, b, preferred_element_type=F32)


def mm_nt(a, b):
    return lax.dot_general(a, b, (((1,), (1,)), ((), ())), preferred_element_type=F32)


def mm_tn(a, b):
    return lax.dot_general(a, b, (((0,), (0,)), ((), ())), preferred_element_type=F32)


def picker(nbr, count_row, base, half, slots):
    local = nbr - base
    own = (local >= 0) & (local < 2 * half)
    column = jnp.where(own, local, 2 * half + (local & (half - 1)))
    live = lax.broadcasted_iota(jnp.int32, (slots, half), 0) < count_row
    column = jnp.where(live, (column - half).astype(F32), -2.0 * half).astype(BF)
    edges = half * slots
    row = lax.broadcasted_iota(jnp.int32, (edges, half), 0)
    lane = lax.broadcasted_iota(jnp.int32, (edges, half), 1)
    one, zero = jnp.ones((), BF), jnp.zeros((), BF)
    lane_b = lane.astype(F32).astype(BF)
    same_atom = jnp.where(lane_b == (row // slots).astype(F32).astype(BF), one, zero)
    spread = mm_nt(same_atom, column)
    slot_lane = lax.broadcasted_iota(jnp.int32, (edges, slots), 1)
    slot_row = lax.broadcasted_iota(jnp.int32, (edges, slots), 0)
    mine = jnp.where((slot_row & (slots - 1)) == slot_lane, spread, 0.0)
    target = jnp.sum(mine, axis=1, keepdims=True)
    target = jnp.broadcast_to(target, (edges, half)).astype(BF)
    parts = [jnp.where(target == lane_b + BF(half * (j - 1)), one, zero) for j in range(3)]
    parts.append(jnp.where(target > BF(-1.5 * half), same_atom, zero))
    return jnp.concatenate(parts, axis=1)


def activation(pre):
    sig = BF(0.5) * jnp.tanh(BF(0.5) * pre) + BF(0.5)
    message = pre * sig
    slope = sig + message * (BF(1.0) - sig)
    return message, slope


def front_kernel(
    feat_hbm, near_ref, nbr_hbm, cnt_hbm, rad_hbm, cot_hbm, wself_hbm, wnbr_hbm, wrad_hbm, wblk_hbm,
    apick_ref, asum_ref, agate_ref, acot_ref, bpick_ref, bsum_ref, bgate_ref, bdgate_ref,
    wself_ref, wnbr_ref, wblk_ref,
    feat_ref, nbr_ref, cnt_ref, rad_ref, bcot_ref, wrad_ref, table_ref, sems,
    *, slots,
):
    atoms = feat_hbm.shape[0]
    half = atoms // 2
    edges = half * slots
    device = lax.axis_index("cell")
    parity = lax.rem(device, 2)
    base = device * atoms
    near_half, far_half = 1 - parity, parity
    near_off = pl.multiple_of(near_half * half, half)
    far_off = pl.multiple_of(far_half * half, half)
    near_edge = pl.multiple_of(near_half * edges, edges)
    far_edge = pl.multiple_of(far_half * edges, edges)
    pairs = [
        (nbr_hbm, nbr_ref),
        (cnt_hbm, cnt_ref),
        (feat_hbm, feat_ref),
        (wnbr_hbm, wnbr_ref),
        (wself_hbm, wself_ref),
        (wrad_hbm, wrad_ref),
        (rad_hbm, rad_ref),
        (wblk_hbm, wblk_ref),
        (cot_hbm.at[pl.ds(far_edge, edges)], bcot_ref),
        (cot_hbm.at[pl.ds(near_edge, edges)], acot_ref),
    ]
    copies = [pltpu.make_async_copy(src, dst, sems.at[n]) for n, (src, dst) in enumerate(pairs)]
    for copy in copies:
        copy.start()
    copies[0].wait()
    copies[1].wait()
    bpick_ref[...] = picker(
        nbr_ref[:, pl.ds(far_off, half)], cnt_ref[pl.ds(far_half, 1), :], base, half, slots
    )
    apick_ref[...] = picker(
        nbr_ref[:, pl.ds(near_off, half)], cnt_ref[pl.ds(near_half, 1), :], base, half, slots
    )
    copies[2].wait()
    copies[3].wait()
    table_ref[0:atoms, :] = mm(feat_ref[...], wnbr_ref[...]).astype(BF)
    table_ref[atoms : atoms + half, :] = mm(near_ref[pl.ds(far_off, half), :], wnbr_ref[...]).astype(BF)
    copies[4].wait()
    own_self = mm(feat_ref[pl.ds(near_off, half), :], wself_ref[...]).astype(BF)
    far_self = mm(feat_ref[pl.ds(far_off, half), :], wself_ref[...]).astype(BF)
    table_ref[atoms + half : atoms + 2 * half, :] = own_self
    copies[5].wait()
    copies[6].wait()
    bgate = mm(rad_ref[pl.ds(far_edge, edges), :], wrad_ref[...])
    bgate_ref[...] = bgate.astype(BF)
    agate_ref[...] = mm(rad_ref[pl.ds(near_edge, edges), :], wrad_ref[...]).astype(BF)
    bsum_ref[...] = (
        mm(bpick_ref[:, :atoms], table_ref[0:atoms, :]) + mm(bpick_ref[:, atoms + half :], far_self)
    ).astype(BF)
    asum_ref[...] = mm(apick_ref[...], table_ref[...]).astype(BF)
    copies[7].wait()
    copies[8].wait()
    bdgate_ref[...] = (mm_nt(bcot_ref[...], wblk_ref[...]) * bgate).astype(BF)
    copies[9].wait()


def far_kernel(far_ref, wnbr_ref, sum_ref, gate_ref, dgate_ref, pick_ref, msg_ref, adj_ref, rim_ref):
    half = far_ref.shape[0]
    halo = mm(far_ref[...], wnbr_ref[...]).astype(BF)
    pick = pick_ref[:, 2 * half : 3 * half]
    pre = (sum_ref[...] + mm(pick, halo).astype(BF)) * gate_ref[...]
    message, slope = activation(pre)
    msg_ref[...] = message
    adj = dgate_ref[...] * slope
    adj_ref[...] = adj
    rim_ref[...] = mm_tn(pick, adj).astype(BF)


def near_kernel(sum_ref, gate_ref, cot_ref, pick_ref, wblk_ref, order_ref, msg_ref, own_ref, rim_ref):
    half = rim_ref.shape[0]
    message, slope = activation(sum_ref[...] * gate_ref[...])
    msg_ref[...] = message
    adj = mm_nt(cot_ref[...], wblk_ref[...]).astype(BF) * gate_ref[...] * slope
    rim_ref[...] = mm_tn(pick_ref[:, 2 * half : 3 * half], adj).astype(BF)
    own_ref[0 : 2 * half, :] = mm_tn(pick_ref[:, : 2 * half], adj)
    own_ref[2 * half :, :] = mm_tn(pick_ref[:, 3 * half :], adj)


def own_kernel(
    amsg_ref, bmsg_ref, adj_ref, pick_ref, own_ref, wself_ref, wnbr_ref, wblk_ref,
    blocks_hbm, grad_ref,
    ablk_ref, bblk_ref, sems,
):
    edges = bmsg_ref.shape[0]
    half = own_ref.shape[0] // 3
    atoms = 2 * half
    parity = lax.rem(lax.axis_index("cell"), 2)
    near_half = 1 - parity
    near_off = pl.multiple_of(near_half * half, half)
    far_off = pl.multiple_of(parity * half, half)
    near_edge = pl.multiple_of(near_half * edges, edges)
    far_edge = pl.multiple_of(parity * edges, edges)
    ablk_ref[...] = mm(amsg_ref[...], wblk_ref[...]).astype(BF)
    acopy = pltpu.make_async_copy(ablk_ref, blocks_hbm.at[pl.ds(near_edge, edges)], sems.at[0])
    acopy.start()
    bblk_ref[...] = mm(bmsg_ref[...], wblk_ref[...]).astype(BF)
    bcopy = pltpu.make_async_copy(bblk_ref, blocks_hbm.at[pl.ds(far_edge, edges)], sems.at[1])
    bcopy.start()
    total = own_ref[0:atoms, :] + mm_tn(pick_ref[:, :atoms], adj_ref[...])
    mine = mm_tn(pick_ref[:, atoms + half :], adj_ref[...])
    grad_ref[...] = mm_nt(total.astype(BF), wnbr_ref[...])
    grad_ref[pl.ds(near_off, half), :] += mm_nt(own_ref[atoms:, :].astype(BF), wself_ref[...])
    grad_ref[pl.ds(far_off, half), :] += mm_nt(mine.astype(BF), wself_ref[...])
    acopy.wait()
    bcopy.wait()


def last_kernel(grad_ref, near_ref, far_ref, wnbr_ref, out_ref):
    half = far_ref.shape[0]
    parity = lax.rem(lax.axis_index("cell"), 2)
    near_off = pl.multiple_of((1 - parity) * half, half)
    far_off = pl.multiple_of(parity * half, half)
    out_ref[pl.ds(near_off, half), :] = (
        grad_ref[pl.ds(near_off, half), :] + mm_nt(near_ref[...], wnbr_ref[...])
    ).astype(BF)
    out_ref[pl.ds(far_off, half), :] = (
        grad_ref[pl.ds(far_off, half), :] + mm_nt(far_ref[...], wnbr_ref[...])
    ).astype(BF)


VM = pl.BlockSpec(memory_space=pltpu.VMEM)
HB = pl.BlockSpec(memory_space=pltpu.HBM)


def call(kernel, name, inputs, outs, megabytes, scratch=(), in_specs=None, out_specs=None):
    if in_specs is not None:
        inputs = [
            pltpu.with_memory_space_constraint(x, pltpu.HBM) if spec is HB else x
            for x, spec in zip(inputs, in_specs)
        ]
    return pl.pallas_call(
        kernel,
        name=name,
        out_shape=[jax.ShapeDtypeStruct(shape, dtype) for shape, dtype in outs],
        in_specs=in_specs or [VM] * len(inputs),
        out_specs=out_specs or [VM] * len(outs),
        scratch_shapes=list(scratch),
        compiler_params=pltpu.CompilerParams(vmem_limit_bytes=megabytes * 1024 * 1024),
    )(*inputs)


def body(count, features, radial, neighbours, counts, cotangent, w_self, w_neighbour, w_radial, w_block):
    atoms, width = features.shape
    slots = neighbours.shape[1]
    half = atoms // 2
    edges = half * slots
    entries = w_block.shape[1]
    basis = radial.shape[2]
    inside = [(i, i ^ 1) for i in range(count)]
    across = []
    for i in range(1, count - 1, 2):
        across += [(i, i + 1), (i + 1, i)]
    wrapped = across + [(0, count - 1), (count - 1, 0)]
    parity = lax.axis_index("cell") & 1
    near = lax.ppermute(features, "cell", inside)
    far_send = lax.dynamic_slice_in_dim(features, parity * half, half, 0)
    far = lax.ppermute(far_send, "cell", wrapped)
    edge_f = ((edges, width), BF)
    edge_e = ((edges, entries), BF)
    pick_t = ((edges, 4 * half), BF)
    rim_t = ((half, width), BF)
    outs = [
        pick_t, edge_f, edge_f, edge_e, pick_t, edge_f, edge_f, edge_f,
        ((width, width), BF), ((width, width), BF), ((width, entries), BF),
    ]
    apick, asum, agate, acot, bpick, bsum, bgate, bdgate, wself_v, wnbr_v, wblk_v = call(
        functools.partial(front_kernel, slots=slots),
        "front",
        (
            features, near, neighbours.T, counts.reshape(2, half),
            radial.reshape(atoms * slots, basis), cotangent.reshape(atoms * slots, entries),
            w_self, w_neighbour, w_radial, w_block,
        ),
        outs,
        20,
        scratch=[
            pltpu.VMEM((atoms, width), BF),
            pltpu.VMEM((slots, atoms), jnp.int32),
            pltpu.VMEM((2, half), jnp.int32),
            pltpu.VMEM((2 * edges, basis), BF),
            pltpu.VMEM((edges, entries), BF),
            pltpu.VMEM((basis, width), BF),
            pltpu.VMEM((4 * half, width), BF),
            pltpu.SemaphoreType.DMA((10,)),
        ],
        in_specs=[HB, VM] + [HB] * 8,
    )
    bmsg, badj, far_rim = call(
        far_kernel,
        "far",
        (far, wnbr_v, bsum, bgate, bdgate, bpick),
        [edge_f, edge_f, rim_t],
        16,
    )
    far_back = lax.ppermute(far_rim, "cell", across)
    amsg, own, near_rim = call(
        near_kernel,
        "near",
        (asum, agate, acot, apick, wblk_v, far_rim),
        [edge_f, ((3 * half, width), F32), rim_t],
        16,
    )
    near_back = lax.ppermute(near_rim, "cell", inside)
    blocks, grad = call(
        own_kernel,
        "own",
        (amsg, bmsg, badj, bpick, own, wself_v, wnbr_v, wblk_v),
        [((2 * edges, entries), BF), ((atoms, width), F32)],
        16,
        scratch=[
            pltpu.VMEM((edges, entries), BF),
            pltpu.VMEM((edges, entries), BF),
            pltpu.SemaphoreType.DMA((2,)),
        ],
        out_specs=[HB, VM],
    )
    (feat_grad,) = call(last_kernel, "last", (grad, near_back, far_back, wnbr_v), [((atoms, width), BF)], 8)
    return blocks.reshape(atoms, slots, entries), feat_grad


def solution(mesh):
    in_specs = (
        P("cell", None),
        P("cell", None, None),
        P("cell", None),
        P("cell"),
        P("cell", None, None),
        P(),
        P(),
        P(),
        P(),
    )
    out_specs = (P("cell", None, None), P("cell", None))
    return jax.shard_map(
        functools.partial(body, mesh.shape["cell"]),
        mesh=mesh, in_specs=in_specs, out_specs=out_specs, check_vma=False,
    )
```

time: 61.6 us -> 23.2 us (0.38)
  the two profiles are of different devices: /device:TPU:8 before, /device:TPU:1 now
where the time goes in v1:
time: 23.2 us; the launch traced here: 22.9 us
  Pallas kernels  10.2 us (44%)
  starting transfers between devices  9.2 us (40%)
  waiting for transfers between devices  1.92 us (8%)
  local copies, waits for them, and re-layouts  0.91 us (4%)
  between operations  0.69 us (3%)
    pallas_call x5, Pallas kernels, call(): pl.pallas_call(kernel, name=name, out_shape=[jax.ShapeDtypeStruct(shape,...  10.2 us
    ppermute x1, starting transfers between devices, body(): near_back = lax.ppermute(near_rim, 'cell', inside)  4.54 us
    ppermute x1, starting transfers between devices, body(): far = lax.ppermute(far_send, 'cell', wrapped)  2.63 us
    ppermute x1, waiting for transfers between devices, body(): far_back = lax.ppermute(far_rim, 'cell', across)  1.91 us
    ppermute x1, starting transfers between devices, body(): far_back = lax.ppermute(far_rim, 'cell', across)  1.91 us
    dynamic_slice x1, local copies, waits for them, and re-layouts, body(): far_send = lax.dynamic_slice_in_dim(features, parity * half, half, 0)  0.91 us
  transfers between devices with their start and end apart: 4, of which 1 were waited for; matrix products, arithmetic and copies ran while one was open for 4% of the time, Pallas kernels for 29%

profile of v1, /device:TPU:1, one launch (start us, length us, event | category | flops | bytes accessed | tf_op | source)
XLA Modules:
  0.0 22.9 jit_solution(10619257102286063872)
XLA Ops:
  0.6 0.1 collective-permute-start
  0.8 0.9 %constant_dynamic-slice_fusion = bf16[128,512]{1,0:T(8,128)(2,1)S(1)} fusion(bf16[256,512]{1,0:T(8,128)(2,1)} %feat_hbm.1, s32[]{:T(128)S(6)} %select_n.3), kind=kLoop, calls=%fused_computation | loop fusion | bytes 262148 | tf_op jit(solution)/shard_map/dynamic_slice | solution.py:219
  1.7 2.6 %collective-permute-start.1 = (bf16[128,512]{1,0:T(8,128)(2,1)S(1)}, bf16[128,512]{1,0:T(8,128)(2,1)S(1)}, u32[]{:S(2)}, u32[]{:S(2)}) collective-permute-start(bf16[128,512]{1,0:T(8,128)(2,1)S(1)} %constant_dynamic-slice_fusion), channel_id=1, source_target_pairs={{1,2},{2,1},{3,4},{4,3},{5,6},{6,5},{7,8},{8,7},{9,10},{10,9},{11,... | collective-permute-start | bytes 393224 | tf_op jit(solution)/shard_map/ppermute | solution.py:220
  4.3 0.0 collective-permute-done.near_ref
  4.3 4.3 %front.1 = (bf16[1024,512]{1,0:T(8,128)(2,1)S(1)}, bf16[1024,512]{1,0:T(8,128)(2,1)S(1)}, bf16[1024,512]{1,0:T(8,128)(2,1)S(1)}, bf16[1024,256]{1,0:T(8,128)(2,1...) custom-call(bf16[256,512]{1,0:T(8,128)(2,1)} %feat_hbm.1, ...), custom_call_target="tpu_custom_call" | custom-call | tf_op jit(solution)/shard_map/front/pallas_call | solution.py:194
  8.6 0.0 collective-permute-done.1.far_ref
  8.6 1.1 %far.1 = (bf16[1024,512]{1,0:T(8,128)(2,1)S(1)}, bf16[1024,512]{1,0:T(8,128)(2,1)S(1)}, bf16[128,512]{1,0:T(8,128)(2,1)S(1)}) custom-call(bf16[128,512]{1,0:T(8,128)(2,1)S(1)} %collective-permute-done.1.far_ref, bf16[512,512]{1,0:T(8,128)(2,1)S(1)} %get-tuple-element.26.wnbr_ref, bf16[1024,512]{1,0:T(8,128)(2,1)S(1)} %get-tuple-element.27.sum_ref, ...), custom_call_target="tpu_custom_call" | custom-call | tf_op jit(solution)/shard_map/far/pallas_call | solution.py:194
  9.7 1.3 %near.1 = (bf16[1024,512]{1,0:T(8,128)(2,1)S(1)}, f32[384,512]{1,0:T(8,128)S(1)}, bf16[128,512]{1,0:T(8,128)(2,1)S(1)}) custom-call(bf16[1024,512]{1,0:T(8,128)(2,1)S(1)} %get-tuple-element.21.sum_ref, bf16[1024,512]{1,0:T(8,128)(2,1)S(1)} %get-tuple-element.22.gate_ref, bf16[1024,256]{1,0:T(8,128)(2,1)S(1)} %get-tuple-element.23.cot_ref, ...), custom_call_target="tpu_custom_call" | custom-call | tf_op jit(solution)/shard_map/near/pallas_call | solution.py:194
  10.9 4.5 %collective-permute-start.2 = (bf16[128,512]{1,0:T(8,128)(2,1)S(1)}, bf16[128,512]{1,0:T(8,128)(2,1)S(1)}, u32[]{:S(2)}, u32[]{:S(2)}) collective-permute-start(bf16[128,512]{1,0:T(8,128)(2,1)S(1)} %get-tuple-element.39), channel_id=1, source_target_pairs={{0,1},{1,0},{2,3},{3,2},{4,5},{5,4},{6,7},{7,6},{8,9},{9,8},{10,11... | collective-permute-start | bytes 393224 | tf_op jit(solution)/shard_map/ppermute | solution.py:266
  15.5 1.9 %collective-permute-start.3 = (bf16[128,512]{1,0:T(8,128)(2,1)S(1)}, bf16[128,512]{1,0:T(8,128)(2,1)S(1)}, u32[]{:S(2)}, u32[]{:S(2)}) collective-permute-start(bf16[128,512]{1,0:T(8,128)(2,1)S(1)} %get-tuple-element.31.order_ref), channel_id=1, source_target_pairs={{1,2},{2,1},{3,4},{4,3},{5,6},{6,5},{7,8},{8,7},{9,10},{10,9},{11,... | collective-permute-start | bytes 393224 | tf_op jit(solution)/shard_map/ppermute | solution.py:258
  17.4 2.4 %own.1 = (bf16[2048,256]{1,0:T(8,128)(2,1)}, f32[256,512]{1,0:T(8,128)S(1)}) custom-call(bf16[1024,512]{1,0:T(8,128)(2,1)S(1)} %get-tuple-element.32.amsg_ref, bf16[1024,512]{1,0:T(8,128)(2,1)S(1)} %get-tuple-element.33.bmsg_ref, bf16[1024,512]{1,0:T(8,128)(2,1)S(1)} %get-tuple-element.34.adj_ref, bf16[1024,512]{1,0:T(8,128)(2,1)S(1)} %get-tuple-element.30.pick_ref, ...), custom_call_target="tpu_custom_call" | custom-call | tf_op jit(solution)/shard_map/own/pallas_call | solution.py:194
  19.8 0.0 collective-permute-done.2.near_ref
  19.8 1.9 %collective-permute-done.3.far_ref = bf16[128,512]{1,0:T(8,128)(2,1)S(1)} collective-permute-done((bf16[128,512]{1,0:T(8,128)(2,1)S(1)}, bf16[128,512]{1,0:T(8,128)(2,1)S(1)}, u32[]{:S(2)}, u32[]{:S(2)}) %collective-permute-start.3) | collective-permute-done | bytes 131104 | tf_op jit(solution)/shard_map/ppermute | solution.py:258
  21.8 1.2 %last.1 = bf16[256,512]{1,0:T(8,128)(2,1)} custom-call(f32[256,512]{1,0:T(8,128)S(1)} %get-tuple-element.38.grad_ref, bf16[128,512]{1,0:T(8,128)(2,1)S(1)} %collective-permute-done.2.near_ref, bf16[128,512]{1,0:T(8,128)(2,1)S(1)} %collective-permute-done.3.far_ref, bf16[512,512]{1,0:T(8,128)(2,1)S(1)} %get-tuple-element.26.wnbr_ref), custom_call_target="tpu_custom_call" | custom-call | tf_op jit(solution)/shard_map/last/pallas_call | solution.py:194
Async XLA Ops:
  0.6 3.7 %collective-permute-start = (bf16[256,512]{1,0:T(8,128)(2,1)}, bf16[256,512]{1,0:T(8,128)(2,1)S(1)}, u32[]{:S(2)}, u32[]{:S(2)}) collective-permute-start(bf16[256,512]{1,0:T(8,128)(2,1)} %feat_hbm.1), channel_id=1, source_target_pairs={{0,1},{1,0},{2,3},{3,2},{4,5},{5,4},{6,7},{7,6},{8,9},{9,8},{10,11... | collective-permute-start | bytes 786440 | tf_op jit(solution)/shard_map/ppermute | solution.py:218
  1.7 6.9 %collective-permute-start.1 = (bf16[128,512]{1,0:T(8,128)(2,1)S(1)}, bf16[128,512]{1,0:T(8,128)(2,1)S(1)}, u32[]{:S(2)}, u32[]{:S(2)}) collective-permute-start(bf16[128,512]{1,0:T(8,128)(2,1)S(1)} %constant_dynamic-slice_fusion), channel_id=1, source_target_pairs={{1,2},{2,1},{3,4},{4,3},{5,6},{6,5},{7,8},{8,7},{9,10},{10,9},{11,... | collective-permute-start | bytes 393224 | tf_op jit(solution)/shard_map/ppermute | solution.py:220
  10.9 8.9 %collective-permute-start.2 = (bf16[128,512]{1,0:T(8,128)(2,1)S(1)}, bf16[128,512]{1,0:T(8,128)(2,1)S(1)}, u32[]{:S(2)}, u32[]{:S(2)}) collective-permute-start(bf16[128,512]{1,0:T(8,128)(2,1)S(1)} %get-tuple-element.39), channel_id=1, source_target_pairs={{0,1},{1,0},{2,3},{3,2},{4,5},{5,4},{6,7},{7,6},{8,9},{9,8},{10,11... | collective-permute-start | bytes 393224 | tf_op jit(solution)/shard_map/ppermute | solution.py:266
  15.5 6.3 %collective-permute-start.3 = (bf16[128,512]{1,0:T(8,128)(2,1)S(1)}, bf16[128,512]{1,0:T(8,128)(2,1)S(1)}, u32[]{:S(2)}, u32[]{:S(2)}) collective-permute-start(bf16[128,512]{1,0:T(8,128)(2,1)S(1)} %get-tuple-element.31.order_ref), channel_id=1, source_target_pairs={{1,2},{2,1},{3,4},{4,3},{5,6},{6,5},{7,8},{8,7},{9,10},{10,9},{11,... | collective-permute-start | bytes 393224 | tf_op jit(solution)/shard_map/ppermute | solution.py:258

commit v2 on v1

v2 whole, which is shorter than its diff:
```python
import functools

import jax
import jax.numpy as jnp
from jax import lax
from jax.experimental import pallas as pl
from jax.experimental.pallas import tpu as pltpu
from jax.sharding import PartitionSpec as P

BF = jnp.bfloat16
F32 = jnp.float32


def mm(a, b):
    return jnp.dot(a, b, preferred_element_type=F32)


def mm_nt(a, b):
    return lax.dot_general(a, b, (((1,), (1,)), ((), ())), preferred_element_type=F32)


def mm_tn(a, b):
    return lax.dot_general(a, b, (((0,), (0,)), ((), ())), preferred_element_type=F32)


def halves(half):
    parity = lax.rem(lax.axis_index("cell"), 2)
    near, far = 1 - parity, parity
    return near, far, pl.multiple_of(near * half, half), pl.multiple_of(far * half, half)


def picker(nbr, count_row, base, half, slots):
    local = nbr - base
    own = (local >= 0) & (local < 2 * half)
    target = jnp.where(own, local, 2 * half + (local & (half - 1)))
    live = lax.broadcasted_iota(jnp.int32, (slots, half), 0) < count_row
    target = jnp.where(live, (target - half).astype(F32), -2.0 * half).astype(BF)
    edges = half * slots
    row = lax.broadcasted_iota(jnp.int32, (edges, half), 0)
    lane = lax.broadcasted_iota(jnp.int32, (edges, half), 1)
    one, zero = jnp.ones((), BF), jnp.zeros((), BF)
    lane_b = lane.astype(F32).astype(BF)
    same_atom = jnp.where(lane_b == (row // slots).astype(F32).astype(BF), one, zero)
    spread = mm_nt(same_atom, target)
    slot_lane = lax.broadcasted_iota(jnp.int32, (edges, slots), 1)
    slot_row = lax.broadcasted_iota(jnp.int32, (edges, slots), 0)
    mine = jnp.where((slot_row & (slots - 1)) == slot_lane, spread, 0.0)
    target = jnp.sum(mine, axis=1, keepdims=True)
    target = jnp.broadcast_to(target, (edges, half)).astype(BF)
    low, high, halo = [
        jnp.where(target == lane_b + BF(half * (j - 1)), one, zero) for j in range(3)
    ]
    mine = jnp.where(target > BF(-1.5 * half), same_atom, zero)
    return jnp.concatenate([low, high, mine, halo], axis=1)


def activation(total, half_gate, half_dgate):
    h = total * half_gate
    t = jnp.tanh(h)
    ht = h * t
    return h + ht, half_dgate * (t + BF(1.0)) * (h - ht + BF(1.0))


def head_kernel(feat_hbm, nbr_hbm, cnt_hbm, send_ref, nbr_ref, cnt_ref, sems):
    half = send_ref.shape[0]
    _, _, _, far_off = halves(half)
    pairs = [
        (feat_hbm.at[pl.ds(far_off, half)], send_ref),
        (nbr_hbm, nbr_ref),
        (cnt_hbm, cnt_ref),
    ]
    copies = [pltpu.make_async_copy(src, dst, sems.at[n]) for n, (src, dst) in enumerate(pairs)]
    for copy in copies:
        copy.start()
    for copy in copies:
        copy.wait()


def front_kernel(
    nbr_ref, cnt_ref, feat_hbm, rad_hbm, cot_hbm, wself_hbm, wnbr_hbm, wrad_hbm, wblk_hbm,
    pick_ref, sum_ref, gate_ref, dgate_ref, self_ref, wself_ref, wnbr_ref, wblk_ref,
    feat_ref, rad_ref, cot_ref, wrad_ref, sems,
    *, slots,
):
    atoms = feat_hbm.shape[0]
    half = atoms // 2
    edges = half * slots
    base = lax.axis_index("cell") * atoms
    pairs = [
        (feat_hbm, feat_ref),
        (wnbr_hbm, wnbr_ref),
        (wrad_hbm, wrad_ref),
        (rad_hbm, rad_ref),
        (wblk_hbm, wblk_ref),
        (cot_hbm, cot_ref),
        (wself_hbm, wself_ref),
    ]
    copies = [pltpu.make_async_copy(src, dst, sems.at[n]) for n, (src, dst) in enumerate(pairs)]
    for copy in copies:
        copy.start()
    for n in range(2):
        pick_ref[n * edges : (n + 1) * edges, :] = picker(
            nbr_ref[:, n * half : (n + 1) * half], cnt_ref[n : n + 1, :], base, half, slots
        )
    for copy in copies[:2]:
        copy.wait()
    own = mm(feat_ref[...], wnbr_ref[...]).astype(BF)
    sum_ref[...] = mm(pick_ref[:, :atoms], own).astype(BF)
    for copy in copies[2:]:
        copy.wait()
    self_ref[...] = mm(feat_ref[...], wself_ref[...]).astype(BF)
    half_wrad = wrad_ref[...] * BF(0.5)
    step = edges // 2
    for n in range(4):
        rows = slice(n * step, (n + 1) * step)
        gate = mm(rad_ref[rows, :], half_wrad).astype(BF)
        gate_ref[rows, :] = gate
        dgate_ref[rows, :] = mm_nt(cot_ref[rows, :], wblk_ref[...]).astype(BF) * gate


def side(halo, half_index, refs, msg_ref, adj_ref, rim_ref):
    self_ref, sum_ref, gate_ref, dgate_ref, pick_ref = refs
    half = rim_ref.shape[0]
    edges = msg_ref.shape[0]
    table = jnp.concatenate(
        [self_ref[pl.ds(pl.multiple_of(half_index * half, half), half), :], halo], axis=0
    )
    step = edges // 2
    first = pl.multiple_of(half_index * edges, edges)
    parts = [
        mm(pick_ref[pl.ds(first + n * step, step), 2 * half :], table).astype(BF) for n in range(2)
    ]
    for n in range(2):
        rows = pl.ds(first + n * step, step)
        message, adj = activation(
            sum_ref[rows, :] + parts[n], gate_ref[rows, :], dgate_ref[rows, :]
        )
        msg_ref[n * step : (n + 1) * step, :] = message
        adj_ref[n * step : (n + 1) * step, :] = adj
    rim_ref[...] = mm_tn(pick_ref[pl.ds(first, edges), 3 * half :], adj_ref[...]).astype(BF)


def near_kernel(
    near_ref, wnbr_ref, self_ref, sum_ref, gate_ref, dgate_ref, pick_ref, order_ref,
    msg_ref, adj_ref, rim_ref,
):
    half = rim_ref.shape[0]
    near, _, _, far_off = halves(half)
    halo = mm(near_ref[pl.ds(far_off, half), :], wnbr_ref[...]).astype(BF)
    side(halo, near, (self_ref, sum_ref, gate_ref, dgate_ref, pick_ref), msg_ref, adj_ref, rim_ref)


def far_kernel(
    far_ref, wnbr_ref, self_ref, sum_ref, gate_ref, dgate_ref, pick_ref, msg_ref, adj_ref, rim_ref
):
    _, far, _, _ = halves(rim_ref.shape[0])
    halo = mm(far_ref[...], wnbr_ref[...]).astype(BF)
    side(halo, far, (self_ref, sum_ref, gate_ref, dgate_ref, pick_ref), msg_ref, adj_ref, rim_ref)


def own_kernel(
    nearmsg_ref, farmsg_ref, nearadj_ref, faradj_ref, pick_ref, wself_ref, wnbr_ref, wblk_ref,
    blocks_hbm, grad_ref,
    nearblk_ref, farblk_ref, selfsum_ref, sems,
):
    edges = farmsg_ref.shape[0]
    atoms = grad_ref.shape[0]
    half = atoms // 2
    near, far, near_off, far_off = halves(half)
    near_edge = pl.multiple_of(near * edges, edges)
    far_edge = pl.multiple_of(far * edges, edges)
    farblk_ref[...] = mm(farmsg_ref[...], wblk_ref[...]).astype(BF)
    far_copy = pltpu.make_async_copy(farblk_ref, blocks_hbm.at[pl.ds(far_edge, edges)], sems.at[0])
    far_copy.start()
    nearblk_ref[...] = mm(nearmsg_ref[...], wblk_ref[...]).astype(BF)
    near_copy = pltpu.make_async_copy(
        nearblk_ref, blocks_hbm.at[pl.ds(near_edge, edges)], sems.at[1]
    )
    near_copy.start()
    near_back = mm_tn(pick_ref[pl.ds(near_edge, edges), : atoms + half], nearadj_ref[...])
    far_back = mm_tn(pick_ref[pl.ds(far_edge, edges), : atoms + half], faradj_ref[...])
    selfsum_ref[pl.ds(near_off, half), :] = near_back[atoms:].astype(BF)
    selfsum_ref[pl.ds(far_off, half), :] = far_back[atoms:].astype(BF)
    total = (near_back[:atoms] + far_back[:atoms]).astype(BF)
    grad_ref[...] = mm_nt(total, wnbr_ref[...]) + mm_nt(selfsum_ref[...], wself_ref[...])
    near_copy.wait()
    far_copy.wait()


def last_kernel(far_ref, near_ref, grad_ref, wnbr_ref, out_hbm, fout_ref, nout_ref, sem):
    half = near_ref.shape[0]
    _, _, near_off, far_off = halves(half)
    fout_ref[...] = (grad_ref[pl.ds(far_off, half), :] + mm_nt(far_ref[...], wnbr_ref[...])).astype(BF)
    c0 = pltpu.make_async_copy(fout_ref, out_hbm.at[pl.ds(far_off, half)], sem.at[0])
    c0.start()
    nout_ref[...] = (grad_ref[pl.ds(near_off, half), :] + mm_nt(near_ref[...], wnbr_ref[...])).astype(BF)
    c1 = pltpu.make_async_copy(nout_ref, out_hbm.at[pl.ds(near_off, half)], sem.at[1])
    c1.start()
    c0.wait()
    c1.wait()


VM = pl.BlockSpec(memory_space=pltpu.VMEM)
HB = pl.BlockSpec(memory_space=pltpu.HBM)


def call(kernel, name, inputs, outs, megabytes, scratch=(), in_specs=None, out_specs=None, aliases=None):
    in_specs = in_specs or [VM] * len(inputs)
    inputs = [
        pltpu.with_memory_space_constraint(x, pltpu.HBM) if spec is HB else x
        for x, spec in zip(inputs, in_specs)
    ]
    return pl.pallas_call(
        kernel,
        name=name,
        out_shape=[jax.ShapeDtypeStruct(shape, dtype) for shape, dtype in outs],
        in_specs=in_specs,
        out_specs=out_specs or [VM] * len(outs),
        scratch_shapes=list(scratch),
        input_output_aliases=aliases or {},
        compiler_params=pltpu.CompilerParams(vmem_limit_bytes=megabytes * 1024 * 1024),
    )(*inputs)


def body(count, features, radial, neighbours, counts, cotangent, w_self, w_neighbour, w_radial, w_block):
    atoms, width = features.shape
    slots = neighbours.shape[1]
    half = atoms // 2
    edges = half * slots
    entries = w_block.shape[1]
    basis = radial.shape[2]
    inside = [(i, i ^ 1) for i in range(count)]
    across = []
    for i in range(1, count - 1, 2):
        across += [(i, i + 1), (i + 1, i)]
    wrapped = across + [(0, count - 1), (count - 1, 0)]
    dma = pltpu.SemaphoreType.DMA
    edge_t = ((edges, width), BF)
    both_t = ((2 * edges, width), BF)
    rim_t = ((half, width), BF)
    grad_t = ((atoms, width), BF)
    far_send, nbr, cnt = call(
        head_kernel,
        "head",
        (features, neighbours.T, counts.reshape(2, half)),
        [rim_t, ((slots, atoms), jnp.int32), ((2, half), jnp.int32)],
        4,
        scratch=[dma((3,))],
        in_specs=[HB] * 3,
    )
    far = lax.ppermute(far_send, "cell", wrapped)
    near = lax.ppermute(features, "cell", inside)
    pick, total, gate, dgate, selfs, wself_v, wnbr_v, wblk_v = call(
        functools.partial(front_kernel, slots=slots),
        "front",
        (
            nbr, cnt, features,
            radial.reshape(atoms * slots, basis), cotangent.reshape(atoms * slots, entries),
            w_self, w_neighbour, w_radial, w_block,
        ),
        [
            ((2 * edges, 4 * half), BF), both_t, both_t, both_t, grad_t,
            ((width, width), BF), ((width, width), BF), ((width, entries), BF),
        ],
        20,
        scratch=[
            pltpu.VMEM((atoms, width), BF),
            pltpu.VMEM((2 * edges, basis), BF),
            pltpu.VMEM((2 * edges, entries), BF),
            pltpu.VMEM((basis, width), BF),
            dma((7,)),
        ],
        in_specs=[VM, VM] + [HB] * 7,
    )
    refs = (selfs, total, gate, dgate, pick)
    side_t = [edge_t, edge_t, rim_t]
    far_msg, far_adj, far_rim = call(far_kernel, "far", (far, wnbr_v) + refs, side_t, 12)
    far_back = lax.ppermute(far_rim, "cell", across)
    near_msg, near_adj, near_rim = call(
        near_kernel, "near", (near, wnbr_v) + refs + (far_rim,), side_t, 12
    )
    near_back = lax.ppermute(near_rim, "cell", inside)
    blocks, grad = call(
        own_kernel,
        "own",
        (near_msg, far_msg, near_adj, far_adj, pick, wself_v, wnbr_v, wblk_v),
        [((2 * edges, entries), BF), ((atoms, width), F32)],
        16,
        scratch=[
            pltpu.VMEM((edges, entries), BF),
            pltpu.VMEM((edges, entries), BF),
            pltpu.VMEM((atoms, width), BF),
            dma((2,)),
        ],
        out_specs=[HB, VM],
    )
    (feat_grad,) = call(
        last_kernel,
        "last",
        (far_back, near_back, grad, wnbr_v),
        [grad_t],
        4,
        scratch=[pltpu.VMEM((half, width), BF), pltpu.VMEM((half, width), BF), dma((2,))],
        out_specs=[HB],
    )
    return blocks.reshape(atoms, slots, entries), feat_grad


def solution(mesh):
    in_specs = (
        P("cell", None),
        P("cell", None, None),
        P("cell", None),
        P("cell"),
        P("cell", None, None),
        P(),
        P(),
        P(),
        P(),
    )
    out_specs = (P("cell", None, None), P("cell", None))
    return jax.shard_map(
        functools.partial(body, mesh.shape["cell"]),
        mesh=mesh, in_specs=in_specs, out_specs=out_specs, check_vma=False,
    )
```

time: 23.2 us -> 19.4 us (0.84)
  waiting for transfers between devices: 1.92 us -> 0.01 us
  starting transfers between devices: 9.2 us -> 7.98 us
  local copies, waits for them, and re-layouts: 0.91 us -> 0 us
  Pallas kernels: 10.2 us -> 10.5 us
    ppermute x1, starting transfers between devices: 4.54 us -> 2.51 us  [body(): near_back = lax.ppermute(near_rim, 'cell', inside)]
    ppermute x1, waiting for transfers between devices: 1.91 us -> 0.01 us  [body(): far_back = lax.ppermute(far_rim, 'cell', across)]
    dynamic_slice x1 -> x0, local copies, waits for them, and re-layouts: 0.91 us -> none  [body(): far_send = lax.dynamic_slice_in_dim(features, parity * half, half, 0)]
    ppermute x1, starting transfers between devices: 1.91 us -> 2.72 us  [body(): far_back = lax.ppermute(far_rim, 'cell', across)]
    pallas_call x5 -> x6, Pallas kernels: 10.2 us -> 10.5 us  [call(): pl.pallas_call(kernel, name=name, out_shape=[jax.ShapeDtypeStruct(shape,...]
  transfers between devices with their start and end apart: 4 -> 4, of which waited for: 1 -> 0; matrix products, arithmetic and copies ran while one was open for 4% -> 0% of each run, Pallas kernels for 29% -> 49%
where the time goes in v2:
time: 19.4 us; the launch traced here: 19.2 us
  Pallas kernels  10.5 us (54%)
  starting transfers between devices  7.98 us (41%)
  between operations  0.71 us (4%)
    pallas_call x6, Pallas kernels, call(): pl.pallas_call(kernel, name=name, out_shape=[jax.ShapeDtypeStruct(shape,...  10.5 us
    ppermute x1, starting transfers between devices, body(): far_back = lax.ppermute(far_rim, 'cell', across)  2.72 us
    ppermute x1, starting transfers between devices, body(): far = lax.ppermute(far_send, 'cell', wrapped)  2.64 us
    ppermute x1, starting transfers between devices, body(): near_back = lax.ppermute(near_rim, 'cell', inside)  2.51 us
  transfers between devices with their start and end apart: 4, of which 0 were waited for; matrix products, arithmetic and copies ran while one was open for 0% of the time, Pallas kernels for 49%

profile of v2, /device:TPU:1, one launch (start us, length us, event | category | flops | bytes accessed | tf_op | source)
XLA Modules:
  0.0 19.2 jit_solution(10534411024683713069)
XLA Ops:
  0.6 0.1 collective-permute-start
  0.8 0.9 %head.1 = (bf16[128,512]{1,0:T(8,128)(2,1)S(1)}, s32[8,256]{1,0:T(8,128)S(1)}, s32[2,128]{1,0:T(2,128)S(1)}) custom-call(bf16[256,512]{1,0:T(8,128)(2,1)} %feat_hbm.3, s32[8,256]{1,0:T(8,128)} %bitcast.7, s32[2,128]{1,0:T(2,128)} %bitcast.8), custom_call_target="tpu_custom_call" | custom-call | tf_op jit(solution)/shard_map/head/pallas_call | solution.py:213
  1.7 2.6 %collective-permute-start.1 = (bf16[128,512]{1,0:T(8,128)(2,1)S(1)}, bf16[128,512]{1,0:T(8,128)(2,1)S(1)}, u32[]{:S(2)}, u32[]{:S(2)}) collective-permute-start(bf16[128,512]{1,0:T(8,128)(2,1)S(1)} %get-tuple-element.29), channel_id=1, source_target_pairs={{1,2},{2,1},{3,4},{4,3},{5,6},{6,5},{7,8},{8,7},{9,10},{10,9},{11,... | collective-permute-start | bytes 393224 | tf_op jit(solution)/shard_map/ppermute | solution.py:251
  4.3 3.6 %front.1 = (bf16[2048,512]{1,0:T(8,128)(2,1)S(1)}, bf16[2048,512]{1,0:T(8,128)(2,1)S(1)}, bf16[2048,512]{1,0:T(8,128)(2,1)S(1)}, bf16[2048,512]{1,0:T(8,128)(2,1...) custom-call(s32[8,256]{1,0:T(8,128)S(1)} %get-tuple-element.21.nbr_r, ...), custom_call_target="tpu_custom_call" | custom-call | tf_op jit(solution)/shard_map/front/pallas_call | solution.py:213
  7.9 0.0 collective-permute-done.1.far_ref
  7.9 1.1 %far.1 = (bf16[1024,512]{1,0:T(8,128)(2,1)S(1)}, bf16[1024,512]{1,0:T(8,128)(2,1)S(1)}, bf16[128,512]{1,0:T(8,128)(2,1)S(1)}) custom-call(bf16[128,512]{1,0:T(8,128)(2,1)S(1)} %collective-permute-done.1.far_ref, bf16[512,512]{1,0:T(8,128)(2,1)S(1)} %get-tuple-element.23.wnbr_ref, bf16[256,512]{1,0:T(8,128)(2,1)S(1)} %get-tuple-element.24.self_ref, ...), custom_call_target="tpu_custom_call" | custom-call | tf_op jit(solution)/shard_map/far/pallas_call | solution.py:213
  9.0 2.7 %collective-permute-start.2 = (bf16[128,512]{1,0:T(8,128)(2,1)S(1)}, bf16[128,512]{1,0:T(8,128)(2,1)S(1)}, u32[]{:S(2)}, u32[]{:S(2)}) collective-permute-start(bf16[128,512]{1,0:T(8,128)(2,1)S(1)} %get-tuple-element.30.order_ref), channel_id=1, source_target_pairs={{1,2},{2,1},{3,4},{4,3},{5,6},{6,5},{7,8},{8,7},{9,10},{10,9},{11,... | collective-permute-start | bytes 393224 | tf_op jit(solution)/shard_map/ppermute | solution.py:278
  11.7 0.0 collective-permute-done.near_ref
  11.7 1.1 %near.1 = (bf16[1024,512]{1,0:T(8,128)(2,1)S(1)}, bf16[1024,512]{1,0:T(8,128)(2,1)S(1)}, bf16[128,512]{1,0:T(8,128)(2,1)S(1)}) custom-call(bf16[256,512]{1,0:T(8,128)(2,1)S(1)} %collective-permute-done.near_ref, bf16[512,512]{1,0:T(8,128)(2,1)S(1)} %get-tuple-element.23.wnbr_ref, bf16[256,512]{1,0:T(8,128)(2,1)S(1)} %get-tuple-element.24.self_ref, ...), custom_call_target="tpu_custom_call" | custom-call | tf_op jit(solution)/shard_map/near/pallas_call | solution.py:213
  12.8 2.5 %collective-permute-start.3 = (bf16[128,512]{1,0:T(8,128)(2,1)S(1)}, bf16[128,512]{1,0:T(8,128)(2,1)S(1)}, u32[]{:S(2)}, u32[]{:S(2)}) collective-permute-start(bf16[128,512]{1,0:T(8,128)(2,1)S(1)} %get-tuple-element.38), channel_id=1, source_target_pairs={{0,1},{1,0},{2,3},{3,2},{4,5},{5,4},{6,7},{7,6},{8,9},{9,8},{10,11... | collective-permute-start | bytes 393224 | tf_op jit(solution)/shard_map/ppermute | solution.py:282
  15.3 2.7 %own.1 = (bf16[2048,256]{1,0:T(8,128)(2,1)}, f32[256,512]{1,0:T(8,128)S(1)}) custom-call(bf16[1024,512]{1,0:T(8,128)(2,1)S(1)} %get-tuple-element.31.nearmsg_ref, bf16[1024,512]{1,0:T(8,128)(2,1)S(1)} %get-tuple-element.32.farmsg_ref, bf16[1024,512]{1,0:T(8,128)(2,1)S(1)} %get-tuple-element.33.nearadj_ref, ...), custom_call_target="tpu_custom_call" | custom-call | tf_op jit(solution)/shard_map/own/pallas_call | solution.py:213
  18.0 0.0 collective-permute-done.2.far_ref
  18.1 0.0 collective-permute-done.3.near_ref
  18.1 1.2 %last.1 = bf16[256,512]{1,0:T(8,128)(2,1)} custom-call(bf16[128,512]{1,0:T(8,128)(2,1)S(1)} %collective-permute-done.2.far_ref, bf16[128,512]{1,0:T(8,128)(2,1)S(1)} %collective-permute-done.3.near_ref, f32[256,512]{1,0:T(8,128)S(1)} %get-tuple-element.39.grad_ref, bf16[512,512]{1,0:T(8,128)(2,1)S(1)} %get-tuple-element.23.wnbr_ref), custom_call_target="tpu_custom_call" | custom-call | tf_op jit(solution)/shard_map/last/pallas_call | solution.py:213
Async XLA Ops:
  0.6 11.1 %collective-permute-start = (bf16[256,512]{1,0:T(8,128)(2,1)}, bf16[256,512]{1,0:T(8,128)(2,1)S(1)}, u32[]{:S(2)}, u32[]{:S(2)}) collective-permute-start(bf16[256,512]{1,0:T(8,128)(2,1)} %feat_hbm.3), channel_id=1, source_target_pairs={{0,1},{1,0},{2,3},{3,2},{4,5},{5,4},{6,7},{7,6},{8,9},{9,8},{10,11... | collective-permute-start | bytes 786440 | tf_op jit(solution)/shard_map/ppermute | solution.py:252
  1.7 6.2 %collective-permute-start.1 = (bf16[128,512]{1,0:T(8,128)(2,1)S(1)}, bf16[128,512]{1,0:T(8,128)(2,1)S(1)}, u32[]{:S(2)}, u32[]{:S(2)}) collective-permute-start(bf16[128,512]{1,0:T(8,128)(2,1)S(1)} %get-tuple-element.29), channel_id=1, source_target_pairs={{1,2},{2,1},{3,4},{4,3},{5,6},{6,5},{7,8},{8,7},{9,10},{10,9},{11,... | collective-permute-start | bytes 393224 | tf_op jit(solution)/shard_map/ppermute | solution.py:251
  9.0 9.0 %collective-permute-start.2 = (bf16[128,512]{1,0:T(8,128)(2,1)S(1)}, bf16[128,512]{1,0:T(8,128)(2,1)S(1)}, u32[]{:S(2)}, u32[]{:S(2)}) collective-permute-start(bf16[128,512]{1,0:T(8,128)(2,1)S(1)} %get-tuple-element.30.order_ref), channel_id=1, source_target_pairs={{1,2},{2,1},{3,4},{4,3},{5,6},{6,5},{7,8},{8,7},{9,10},{10,9},{11,... | collective-permute-start | bytes 393224 | tf_op jit(solution)/shard_map/ppermute | solution.py:278
  12.8 5.2 %collective-permute-start.3 = (bf16[128,512]{1,0:T(8,128)(2,1)S(1)}, bf16[128,512]{1,0:T(8,128)(2,1)S(1)}, u32[]{:S(2)}, u32[]{:S(2)}) collective-permute-start(bf16[128,512]{1,0:T(8,128)(2,1)S(1)} %get-tuple-element.38), channel_id=1, source_target_pairs={{0,1},{1,0},{2,3},{3,2},{4,5},{5,4},{6,7},{7,6},{8,9},{9,8},{10,11... | collective-permute-start | bytes 393224 | tf_op jit(solution)/shard_map/ppermute | solution.py:282

commit v3 on v2

--- a/solution.py
+++ b/solution.py
@@ -61,11 +61,12 @@
     return h + ht, half_dgate * (t + BF(1.0)) * (h - ht + BF(1.0))
 
 
-def head_kernel(feat_hbm, nbr_hbm, cnt_hbm, send_ref, nbr_ref, cnt_ref, sems):
-    half = send_ref.shape[0]
-    _, _, _, far_off = halves(half)
+def head_kernel(feat_hbm, nbr_hbm, cnt_hbm, far_ref, near_ref, nbr_ref, cnt_ref, sems):
+    half = far_ref.shape[0]
+    _, _, near_off, far_off = halves(half)
     pairs = [
-        (feat_hbm.at[pl.ds(far_off, half)], send_ref),
+        (feat_hbm.at[pl.ds(far_off, half)], far_ref),
+        (feat_hbm.at[pl.ds(near_off, half)], near_ref),
         (nbr_hbm, nbr_ref),
         (cnt_hbm, cnt_ref),
     ]
@@ -77,45 +78,24 @@
 
 
 def front_kernel(
-    nbr_ref, cnt_ref, feat_hbm, rad_hbm, cot_hbm, wself_hbm, wnbr_hbm, wrad_hbm, wblk_hbm,
-    pick_ref, sum_ref, gate_ref, dgate_ref, self_ref, wself_ref, wnbr_ref, wblk_ref,
-    feat_ref, rad_ref, cot_ref, wrad_ref, sems,
+    nbr_ref, cnt_ref, feat_ref, rad_ref, cot_ref, wself_ref, wnbr_ref, wrad_ref, wblk_ref,
+    pick_ref, sum_ref, gate_ref, dgate_ref, self_ref,
     *, slots,
 ):
-    atoms = feat_hbm.shape[0]
+    atoms = feat_ref.shape[0]
     half = atoms // 2
     edges = half * slots
     base = lax.axis_index("cell") * atoms
-    pairs = [
-        (feat_hbm, feat_ref),
-        (wnbr_hbm, wnbr_ref),
-        (wrad_hbm, wrad_ref),
-        (rad_hbm, rad_ref),
-        (wblk_hbm, wblk_ref),
-        (cot_hbm, cot_ref),
-        (wself_hbm, wself_ref),
-    ]
-    copies = [pltpu.make_async_copy(src, dst, sems.at[n]) for n, (src, dst) in enumerate(pairs)]
-    for copy in copies:
-        copy.start()
     for n in range(2):
         pick_ref[n * edges : (n + 1) * edges, :] = picker(
             nbr_ref[:, n * half : (n + 1) * half], cnt_ref[n : n + 1, :], base, half, slots
         )
-    for copy in copies[:2]:
-        copy.wait()
     own = mm(feat_ref[...], wnbr_ref[...]).astype(BF)
+    self_ref[...] = mm(feat_ref[...], wself_ref[...]).astype(BF)
+    gate = mm(rad_ref[...], wrad_ref[...] * BF(0.5))
+    gate_ref[...] = gate.astype(BF)
     sum_ref[...] = mm(pick_ref[:, :atoms], own).astype(BF)
-    for copy in copies[2:]:
-        copy.wait()
-    self_ref[...] = mm(feat_ref[...], wself_ref[...]).astype(BF)
-    half_wrad = wrad_ref[...] * BF(0.5)
-    step = edges // 2
-    for n in range(4):
-        rows = slice(n * step, (n + 1) * step)
-        gate = mm(rad_ref[rows, :], half_wrad).astype(BF)
-        gate_ref[rows, :] = gate
-        dgate_ref[rows, :] = mm_nt(cot_ref[rows, :], wblk_ref[...]).astype(BF) * gate
+    dgate_ref[...] = (mm_nt(cot_ref[...], wblk_ref[...]) * gate).astype(BF)
 
 
 def side(halo, half_index, refs, msg_ref, adj_ref, rim_ref):
@@ -141,17 +121,17 @@
 
 
 def near_kernel(
-    near_ref, wnbr_ref, self_ref, sum_ref, gate_ref, dgate_ref, pick_ref, order_ref,
-    msg_ref, adj_ref, rim_ref,
+    near_ref, wnbr_ref, self_ref, sum_ref, gate_ref, dgate_ref, pick_ref, msg_ref, adj_ref, rim_ref
 ):
     half = rim_ref.shape[0]
-    near, _, _, far_off = halves(half)
-    halo = mm(near_ref[pl.ds(far_off, half), :], wnbr_ref[...]).astype(BF)
+    near, _, _, _ = halves(half)
+    halo = mm(near_ref[...], wnbr_ref[...]).astype(BF)
     side(halo, near, (self_ref, sum_ref, gate_ref, dgate_ref, pick_ref), msg_ref, adj_ref, rim_ref)
 
 
 def far_kernel(
-    far_ref, wnbr_ref, self_ref, sum_ref, gate_ref, dgate_ref, pick_ref, msg_ref, adj_ref, rim_ref
+    far_ref, wnbr_ref, self_ref, sum_ref, gate_ref, dgate_ref, pick_ref, order_ref,
+    msg_ref, adj_ref, rim_ref,
 ):
     _, far, _, _ = halves(rim_ref.shape[0])
     halo = mm(far_ref[...], wnbr_ref[...]).astype(BF)
@@ -177,12 +157,16 @@
         nearblk_ref, blocks_hbm.at[pl.ds(near_edge, edges)], sems.at[1]
     )
     near_copy.start()
-    near_back = mm_tn(pick_ref[pl.ds(near_edge, edges), : atoms + half], nearadj_ref[...])
-    far_back = mm_tn(pick_ref[pl.ds(far_edge, edges), : atoms + half], faradj_ref[...])
-    selfsum_ref[pl.ds(near_off, half), :] = near_back[atoms:].astype(BF)
-    selfsum_ref[pl.ds(far_off, half), :] = far_back[atoms:].astype(BF)
-    total = (near_back[:atoms] + far_back[:atoms]).astype(BF)
-    grad_ref[...] = mm_nt(total, wnbr_ref[...]) + mm_nt(selfsum_ref[...], wself_ref[...])
+
+    @pl.when(lax.axis_index("cell") >= 0)
+    def _():
+        near_back = mm_tn(pick_ref[pl.ds(near_edge, edges), : atoms + half], nearadj_ref[...])
+        far_back = mm_tn(pick_ref[pl.ds(far_edge, edges), : atoms + half], faradj_ref[...])
+        selfsum_ref[pl.ds(near_off, half), :] = near_back[atoms:].astype(BF)
+        selfsum_ref[pl.ds(far_off, half), :] = far_back[atoms:].astype(BF)
+        total = (near_back[:atoms] + far_back[:atoms]).astype(BF)
+        grad_ref[...] = mm_nt(total, wnbr_ref[...]) + mm_nt(selfsum_ref[...], wself_ref[...])
+
     near_copy.wait()
     far_copy.wait()
 
@@ -204,7 +188,7 @@
 HB = pl.BlockSpec(memory_space=pltpu.HBM)
 
 
-def call(kernel, name, inputs, outs, megabytes, scratch=(), in_specs=None, out_specs=None, aliases=None):
+def call(kernel, name, inputs, outs, megabytes, scratch=(), in_specs=None, out_specs=None, flops=0):
     in_specs = in_specs or [VM] * len(inputs)
     inputs = [
         pltpu.with_memory_space_constraint(x, pltpu.HBM) if spec is HB else x
@@ -217,7 +201,7 @@
         in_specs=in_specs,
         out_specs=out_specs or [VM] * len(outs),
         scratch_shapes=list(scratch),
-        input_output_aliases=aliases or {},
+        cost_estimate=pl.CostEstimate(flops=flops, bytes_accessed=0, transcendentals=0),
         compiler_params=pltpu.CompilerParams(vmem_limit_bytes=megabytes * 1024 * 1024),
     )(*inputs)
 
@@ -239,18 +223,19 @@
     both_t = ((2 * edges, width), BF)
     rim_t = ((half, width), BF)
     grad_t = ((atoms, width), BF)
-    far_send, nbr, cnt = call(
+    far_send, near_send, nbr, cnt = call(
         head_kernel,
         "head",
         (features, neighbours.T, counts.reshape(2, half)),
-        [rim_t, ((slots, atoms), jnp.int32), ((2, half), jnp.int32)],
+        [rim_t, rim_t, ((slots, atoms), jnp.int32), ((2, half), jnp.int32)],
         4,
-        scratch=[dma((3,))],
+        scratch=[dma((4,))],
         in_specs=[HB] * 3,
+        flops=10**12,
     )
     far = lax.ppermute(far_send, "cell", wrapped)
-    near = lax.ppermute(features, "cell", inside)
-    pick, total, gate, dgate, selfs, wself_v, wnbr_v, wblk_v = call(
+    near = lax.ppermute(near_send, "cell", inside)
+    pick, total, gate, dgate, selfs = call(
         functools.partial(front_kernel, slots=slots),
         "front",
         (
@@ -258,32 +243,22 @@
             radial.reshape(atoms * slots, basis), cotangent.reshape(atoms * slots, entries),
             w_self, w_neighbour, w_radial, w_block,
         ),
-        [
-            ((2 * edges, 4 * half), BF), both_t, both_t, both_t, grad_t,
-            ((width, width), BF), ((width, width), BF), ((width, entries), BF),
-        ],
-        20,
-        scratch=[
-            pltpu.VMEM((atoms, width), BF),
-            pltpu.VMEM((2 * edges, basis), BF),
-            pltpu.VMEM((2 * edges, entries), BF),
-            pltpu.VMEM((basis, width), BF),
-            dma((7,)),
-        ],
-        in_specs=[VM, VM] + [HB] * 7,
+        [((2 * edges, 4 * half), BF), both_t, both_t, both_t, grad_t],
+        16,
     )
     refs = (selfs, total, gate, dgate, pick)
     side_t = [edge_t, edge_t, rim_t]
-    far_msg, far_adj, far_rim = call(far_kernel, "far", (far, wnbr_v) + refs, side_t, 12)
+    near_msg, near_adj, near_rim = call(near_kernel, "near", (near, w_neighbour) + refs, side_t, 12)
+    far_msg, far_adj, far_rim = call(
+        far_kernel, "far", (far, w_neighbour) + refs + (near_rim,), side_t, 12
+    )
+    near_rim, far_rim = lax.optimization_barrier((near_rim, far_rim))
+    near_back = lax.ppermute(near_rim, "cell", inside)
     far_back = lax.ppermute(far_rim, "cell", across)
-    near_msg, near_adj, near_rim = call(
-        near_kernel, "near", (near, wnbr_v) + refs + (far_rim,), side_t, 12
-    )
-    near_back = lax.ppermute(near_rim, "cell", inside)
     blocks, grad = call(
         own_kernel,
         "own",
-        (near_msg, far_msg, near_adj, far_adj, pick, wself_v, wnbr_v, wblk_v),
+        (near_msg, far_msg, near_adj, far_adj, pick, w_self, w_neighbour, w_block),
         [((2 * edges, entries), BF), ((atoms, width), F32)],
         16,
         scratch=[
@@ -297,7 +272,7 @@
     (feat_grad,) = call(
         last_kernel,
         "last",
-        (far_back, near_back, grad, wnbr_v),
+        (far_back, near_back, grad, w_neighbour),
         [grad_t],
         4,
         scratch=[pltpu.VMEM((half, width), BF), pltpu.VMEM((half, width), BF), dma((2,))],

time: 19.4 us -> 19.3 us (level)
  the two profiles are of different devices: /device:TPU:1 before, /device:TPU:23 now
where the time goes in v3:
time: 19.3 us; the launch traced here: 19.1 us
  Pallas kernels  8.92 us (46%)
  starting transfers between devices  5.17 us (27%)
  waiting for transfers between devices  4.23 us (22%)
  between operations  0.78 us (4%)
    pallas_call x6, Pallas kernels, call(): pl.pallas_call(kernel, name=name, out_shape=[jax.ShapeDtypeStruct(shape,...  8.92 us
    ppermute x1, starting transfers between devices, body(): far_back = lax.ppermute(far_rim, 'cell', across)  3.19 us
    ppermute x1, waiting for transfers between devices, body(): far_back = lax.ppermute(far_rim, 'cell', across)  2.68 us
    ppermute x1, waiting for transfers between devices, body(): far = lax.ppermute(far_send, 'cell', wrapped)  1.55 us
    ppermute x1, starting transfers between devices, body(): far = lax.ppermute(far_send, 'cell', wrapped)  1.17 us
    ppermute x1, starting transfers between devices, body(): near = lax.ppermute(near_send, 'cell', inside)  0.74 us
  transfers between devices with their start and end apart: 4, of which 2 were waited for; matrix products, arithmetic and copies ran while one was open for 0% of the time, Pallas kernels for 29%

profile of v3, /device:TPU:23, one launch (start us, length us, event | category | flops | bytes accessed | tf_op | source)
XLA Modules:
  0.0 19.1 jit_solution(7892118691339305148)
XLA Ops:
  0.6 0.0 copy-start
  0.6 0.0 copy-start.1
  0.7 0.0 copy-start.2
  0.7 0.0 copy-start.3
  0.7 0.0 copy-start.4
  0.7 0.0 copy-start.5
  0.7 0.0 copy-start.6
  0.7 1.2 %head.1 = (bf16[128,512]{1,0:T(8,128)(2,1)S(1)}, bf16[128,512]{1,0:T(8,128)(2,1)S(1)}, s32[8,256]{1,0:T(8,128)S(1)}, s32[2,128]{1,0:T(2,128)S(1)}) custom-call(bf16[256,512]{1,0:T(8,128)(2,1)} %feat_ref.1, s32[8,256]{1,0:T(8,128)} %bitcast.8, s32[2,128]{1,0:T(2,128)} %bitcast.9), custom_call_target="tpu_custom_call" | custom-call | flops 999999995904 | tf_op jit(solution)/shard_map/head/pallas_call | solution.py:197
  1.9 0.7 %collective-permute-start = (bf16[128,512]{1,0:T(8,128)(2,1)S(1)}, bf16[128,512]{1,0:T(8,128)(2,1)S(1)}, u32[]{:S(2)}, u32[]{:S(2)}) collective-permute-start(bf16[128,512]{1,0:T(8,128)(2,1)S(1)} %get-tuple-element.21), channel_id=1, source_target_pairs={{0,1},{1,0},{2,3},{3,2},{4,5},{5,4},{6,7},{7,6},{8,9},{9,8},{10,11... | collective-permute-start | bytes 393224 | tf_op jit(solution)/shard_map/ppermute | solution.py:237
  2.6 1.2 %collective-permute-start.1 = (bf16[128,512]{1,0:T(8,128)(2,1)S(1)}, bf16[128,512]{1,0:T(8,128)(2,1)S(1)}, u32[]{:S(2)}, u32[]{:S(2)}) collective-permute-start(bf16[128,512]{1,0:T(8,128)(2,1)S(1)} %get-tuple-element.30), channel_id=1, source_target_pairs={{1,2},{2,1},{3,4},{4,3},{5,6},{6,5},{7,8},{8,7},{9,10},{10,9},{11,... | collective-permute-start | bytes 393224 | tf_op jit(solution)/shard_map/ppermute | solution.py:236
  3.8 0.0 copy-done
  3.8 0.0 copy-done.1
  3.8 0.0 copy-done.2
  3.8 2.3 %front.1 = (bf16[2048,512]{1,0:T(8,128)(2,1)S(1)}, bf16[2048,512]{1,0:T(8,128)(2,1)S(1)}, bf16[2048,512]{1,0:T(8,128)(2,1)S(1)}, bf16[2048,512]{1,0:T(8,128)(2,1)S(1)}, bf16[256,512]{1,0:T(8,128)(2,1)S(1)}) custom-call(s32[8,256]{1,0:T(8,128)S(1)} %get-tuple-element.22.nbr_ref, s32[2,128]{1,0:T(2,128)S(1)} %get-tuple-element.23.cnt_ref, ...), custom_call_target="tpu_custom_call" | custom-call | tf_op jit(solution)/shard_map/front/pallas_call | solution.py:197
  6.2 0.0 collective-permute-done.near_ref
  6.2 1.1 %near.1 = (bf16[1024,512]{1,0:T(8,128)(2,1)S(1)}, bf16[1024,512]{1,0:T(8,128)(2,1)S(1)}, bf16[128,512]{1,0:T(8,128)(2,1)S(1)}) custom-call(bf16[128,512]{1,0:T(8,128)(2,1)S(1)} %collective-permute-done.near_ref, bf16[512,512]{1,0:T(8,128)(2,1)S(1)} %copy-done, bf16[256,512]{1,0:T(8,128)(2,1)S(1)} %get-tuple-element.24.self_ref, ...), custom_call_target="tpu_custom_call" | custom-call | tf_op jit(solution)/shard_map/near/pallas_call | solution.py:197
  7.3 1.6 %collective-permute-done.1.far_ref = bf16[128,512]{1,0:T(8,128)(2,1)S(1)} collective-permute-done((bf16[128,512]{1,0:T(8,128)(2,1)S(1)}, bf16[128,512]{1,0:T(8,128)(2,1)S(1)}, u32[]{:S(2)}, u32[]{:S(2)}) %collective-permute-start.1) | collective-permute-done | bytes 131104 | tf_op jit(solution)/shard_map/ppermute | solution.py:236
  8.8 1.1 %far.1 = (bf16[1024,512]{1,0:T(8,128)(2,1)S(1)}, bf16[1024,512]{1,0:T(8,128)(2,1)S(1)}, bf16[128,512]{1,0:T(8,128)(2,1)S(1)}) custom-call(bf16[128,512]{1,0:T(8,128)(2,1)S(1)} %collective-permute-done.1.far_ref, bf16[512,512]{1,0:T(8,128)(2,1)S(1)} %copy-done, bf16[256,512]{1,0:T(8,128)(2,1)S(1)} %get-tuple-element.24.self_ref, ...), custom_call_target="tpu_custom_call" | custom-call | tf_op jit(solution)/shard_map/far/pallas_call | solution.py:197
  9.9 3.2 %collective-permute-start.2 = (bf16[128,512]{1,0:T(8,128)(2,1)S(1)}, bf16[128,512]{1,0:T(8,128)(2,1)S(1)}, u32[]{:S(2)}, u32[]{:S(2)}) collective-permute-start(bf16[128,512]{1,0:T(8,128)(2,1)S(1)} %get-tuple-element.37), channel_id=1, source_target_pairs={{1,2},{2,1},{3,4},{4,3},{5,6},{6,5},{7,8},{8,7},{9,10},{10,9},{11,... | collective-permute-start | bytes 393224 | tf_op jit(solution)/shard_map/ppermute | solution.py:257
  13.1 0.1 collective-permute-start.3
  13.2 2.1 %own.1 = (bf16[2048,256]{1,0:T(8,128)(2,1)}, f32[256,512]{1,0:T(8,128)S(1)}) custom-call(bf16[1024,512]{1,0:T(8,128)(2,1)S(1)} %get-tuple-element.29.nearmsg_ref, bf16[1024,512]{1,0:T(8,128)(2,1)S(1)} %get-tuple-element.32.farmsg_ref, bf16[1024,512]{1,0:T(8,128)(2,1)S(1)} %get-tuple-element.33.nearadj_ref, ...), custom_call_target="tpu_custom_call" | custom-call | tf_op jit(solution)/shard_map/own/pallas_call | solution.py:197
  15.3 2.7 %collective-permute-done.2.far_ref = bf16[128,512]{1,0:T(8,128)(2,1)S(1)} collective-permute-done((bf16[128,512]{1,0:T(8,128)(2,1)S(1)}, bf16[128,512]{1,0:T(8,128)(2,1)S(1)}, u32[]{:S(2)}, u32[]{:S(2)}) %collective-permute-start.2) | collective-permute-done | bytes 131104 | tf_op jit(solution)/shard_map/ppermute | solution.py:257
  18.0 0.0 collective-permute-done.3.near_ref
  18.0 1.2 %last.1 = bf16[256,512]{1,0:T(8,128)(2,1)} custom-call(bf16[128,512]{1,0:T(8,128)(2,1)S(1)} %collective-permute-done.2.far_ref, bf16[128,512]{1,0:T(8,128)(2,1)S(1)} %collective-permute-done.3.near_ref, f32[256,512]{1,0:T(8,128)S(1)} %get-tuple-element.39.grad_ref, bf16[512,512]{1,0:T(8,128)(2,1)S(1)} %copy-done), custom_call_target="tpu_custom_call" | custom-call | tf_op jit(solution)/shard_map/last/pallas_call | solution.py:197
  (4 shorter events, 0.0 us)
Async XLA Ops:
  0.6 3.2 %copy-start = (bf16[512,512]{1,0:T(8,128)(2,1)S(1)}, bf16[512,512]{1,0:T(8,128)(2,1)}, u32[]{:S(2)}) copy-start(bf16[512,512]{1,0:T(8,128)(2,1)} %wnbr_ref.9) | copy-start | bytes 1572868
  0.6 3.2 %copy-start.1 = (bf16[512,512]{1,0:T(8,128)(2,1)S(1)}, bf16[512,512]{1,0:T(8,128)(2,1)}, u32[]{:S(2)}) copy-start(bf16[512,512]{1,0:T(8,128)(2,1)} %wself_ref.3) | copy-start | bytes 1572868
  0.7 3.1 %copy-start.2 = (bf16[256,8,256]{2,1,0:T(8,128)(2,1)S(1)}, bf16[256,8,256]{2,1,0:T(8,128)(2,1)}, u32[]{:S(2)}) copy-start(bf16[256,8,256]{2,1,0:T(8,128)(2,1)} %param.13) | copy-start | bytes 3145732
  0.7 3.1 %copy-start.3 = (bf16[512,256]{1,0:T(8,128)(2,1)S(1)}, bf16[512,256]{1,0:T(8,128)(2,1)}, u32[]{:S(2)}) copy-start(bf16[512,256]{1,0:T(8,128)(2,1)} %wblk_ref.3) | copy-start | bytes 786436
  0.7 3.1 %copy-start.4 = (bf16[256,8,128]{2,1,0:T(8,128)(2,1)S(1)}, bf16[256,8,128]{2,1,0:T(8,128)(2,1)}, u32[]{:S(2)}) copy-start(bf16[256,8,128]{2,1,0:T(8,128)(2,1)} %param.10) | copy-start | bytes 1572868
  0.7 3.1 %copy-start.5 = (bf16[256,512]{1,0:T(8,128)(2,1)S(1)}, bf16[256,512]{1,0:T(8,128)(2,1)}, u32[]{:S(2)}) copy-start(bf16[256,512]{1,0:T(8,128)(2,1)} %feat_ref.1) | copy-start | bytes 786436
  0.7 3.1 %copy-start.6 = (bf16[128,512]{1,0:T(8,128)(2,1)S(1)}, bf16[128,512]{1,0:T(8,128)(2,1)}, u32[]{:S(2)}) copy-start(bf16[128,512]{1,0:T(8,128)(2,1)} %wrad_ref.1) | copy-start | bytes 393220
  1.9 4.3 %collective-permute-start = (bf16[128,512]{1,0:T(8,128)(2,1)S(1)}, bf16[128,512]{1,0:T(8,128)(2,1)S(1)}, u32[]{:S(2)}, u32[]{:S(2)}) collective-permute-start(bf16[128,512]{1,0:T(8,128)(2,1)S(1)} %get-tuple-element.21), channel_id=1, source_target_pairs={{0,1},{1,0},{2,3},{3,2},{4,5},{5,4},{6,7},{7,6},{8,9},{9,8},{10,11... | collective-permute-start | bytes 393224 | tf_op jit(solution)/shard_map/ppermute | solution.py:237
  2.6 6.2 %collective-permute-start.1 = (bf16[128,512]{1,0:T(8,128)(2,1)S(1)}, bf16[128,512]{1,0:T(8,128)(2,1)S(1)}, u32[]{:S(2)}, u32[]{:S(2)}) collective-permute-start(bf16[128,512]{1,0:T(8,128)(2,1)S(1)} %get-tuple-element.30), channel_id=1, source_target_pairs={{1,2},{2,1},{3,4},{4,3},{5,6},{6,5},{7,8},{8,7},{9,10},{10,9},{11,... | collective-permute-start | bytes 393224 | tf_op jit(solution)/shard_map/ppermute | solution.py:236
  9.9 8.1 %collective-permute-start.2 = (bf16[128,512]{1,0:T(8,128)(2,1)S(1)}, bf16[128,512]{1,0:T(8,128)(2,1)S(1)}, u32[]{:S(2)}, u32[]{:S(2)}) collective-permute-start(bf16[128,512]{1,0:T(8,128)(2,1)S(1)} %get-tuple-element.37), channel_id=1, source_target_pairs={{1,2},{2,1},{3,4},{4,3},{5,6},{6,5},{7,8},{8,7},{9,10},{10,9},{11,... | collective-permute-start | bytes 393224 | tf_op jit(solution)/shard_map/ppermute | solution.py:257
  13.1 4.9 %collective-permute-start.3 = (bf16[128,512]{1,0:T(8,128)(2,1)S(1)}, bf16[128,512]{1,0:T(8,128)(2,1)S(1)}, u32[]{:S(2)}, u32[]{:S(2)}) collective-permute-start(bf16[128,512]{1,0:T(8,128)(2,1)S(1)} %get-tuple-element.38.order_ref), channel_id=1, source_target_pairs={{0,1},{1,0},{2,3},{3,2},{4,5},{5,4},{6,7},{7,6},{8,9},{9,8},{10,11... | collective-permute-start | bytes 393224 | tf_op jit(solution)/shard_map/ppermute | solution.py:256

commit v4 on v3

--- a/solution.py
+++ b/solution.py
@@ -77,25 +77,37 @@
         copy.wait()
 
 
+def prepare(half_index, own, refs, outs, slots):
+    nbr_ref, cnt_ref, rad_ref, cot_ref, wrad_ref, wblk_ref = refs
+    pick_ref, sum_ref, gate_ref, dgate_ref = outs
+    edges = pick_ref.shape[0]
+    half = edges // slots
+    off = pl.multiple_of(half_index * half, half)
+    rows = pl.ds(pl.multiple_of(half_index * edges, edges), edges)
+    pick_ref[...] = picker(
+        nbr_ref[:, pl.ds(off, half)],
+        cnt_ref[pl.ds(half_index, 1), :],
+        lax.axis_index("cell") * (2 * half),
+        half,
+        slots,
+    )
+    gate = mm(rad_ref[rows, :], wrad_ref[...] * BF(0.5))
+    gate_ref[...] = gate.astype(BF)
+    sum_ref[...] = mm(pick_ref[:, : 2 * half], own).astype(BF)
+    dgate_ref[...] = (mm_nt(cot_ref[rows, :], wblk_ref[...]) * gate).astype(BF)
+
+
 def front_kernel(
-    nbr_ref, cnt_ref, feat_ref, rad_ref, cot_ref, wself_ref, wnbr_ref, wrad_ref, wblk_ref,
-    pick_ref, sum_ref, gate_ref, dgate_ref, self_ref,
+    nbr_ref, cnt_ref, rad_ref, cot_ref, wrad_ref, wblk_ref, feat_ref, wself_ref, wnbr_ref,
+    pick_ref, sum_ref, gate_ref, dgate_ref, self_ref, own_ref,
     *, slots,
 ):
-    atoms = feat_ref.shape[0]
-    half = atoms // 2
-    edges = half * slots
-    base = lax.axis_index("cell") * atoms
-    for n in range(2):
-        pick_ref[n * edges : (n + 1) * edges, :] = picker(
-            nbr_ref[:, n * half : (n + 1) * half], cnt_ref[n : n + 1, :], base, half, slots
-        )
+    _, far, _, _ = halves(feat_ref.shape[0] // 2)
     own = mm(feat_ref[...], wnbr_ref[...]).astype(BF)
+    own_ref[...] = own
     self_ref[...] = mm(feat_ref[...], wself_ref[...]).astype(BF)
-    gate = mm(rad_ref[...], wrad_ref[...] * BF(0.5))
-    gate_ref[...] = gate.astype(BF)
-    sum_ref[...] = mm(pick_ref[:, :atoms], own).astype(BF)
-    dgate_ref[...] = (mm_nt(cot_ref[...], wblk_ref[...]) * gate).astype(BF)
+    refs = (nbr_ref, cnt_ref, rad_ref, cot_ref, wrad_ref, wblk_ref)
+    prepare(far, own, refs, (pick_ref, sum_ref, gate_ref, dgate_ref), slots)
 
 
 def side(halo, half_index, refs, msg_ref, adj_ref, rim_ref):
@@ -106,32 +118,30 @@
         [self_ref[pl.ds(pl.multiple_of(half_index * half, half), half), :], halo], axis=0
     )
     step = edges // 2
-    first = pl.multiple_of(half_index * edges, edges)
-    parts = [
-        mm(pick_ref[pl.ds(first + n * step, step), 2 * half :], table).astype(BF) for n in range(2)
-    ]
-    for n in range(2):
-        rows = pl.ds(first + n * step, step)
-        message, adj = activation(
-            sum_ref[rows, :] + parts[n], gate_ref[rows, :], dgate_ref[rows, :]
-        )
-        msg_ref[n * step : (n + 1) * step, :] = message
-        adj_ref[n * step : (n + 1) * step, :] = adj
-    rim_ref[...] = mm_tn(pick_ref[pl.ds(first, edges), 3 * half :], adj_ref[...]).astype(BF)
+    chunks = [slice(n * step, (n + 1) * step) for n in range(2)]
+    parts = [mm(pick_ref[rows, 2 * half :], table).astype(BF) for rows in chunks]
+    for rows, part in zip(chunks, parts):
+        message, adj = activation(sum_ref[rows, :] + part, gate_ref[rows, :], dgate_ref[rows, :])
+        msg_ref[rows, :] = message
+        adj_ref[rows, :] = adj
+    rim_ref[...] = mm_tn(pick_ref[:, 3 * half :], adj_ref[...]).astype(BF)
 
 
 def near_kernel(
-    near_ref, wnbr_ref, self_ref, sum_ref, gate_ref, dgate_ref, pick_ref, msg_ref, adj_ref, rim_ref
+    nbr_ref, cnt_ref, rad_ref, cot_ref, wrad_ref, wblk_ref, near_ref, wnbr_ref, self_ref, own_ref, order_ref,
+    msg_ref, adj_ref, rim_ref, pick_ref,
+    sum_ref, gate_ref, dgate_ref,
+    *, slots,
 ):
-    half = rim_ref.shape[0]
-    near, _, _, _ = halves(half)
+    near, _, _, _ = halves(rim_ref.shape[0])
+    refs = (nbr_ref, cnt_ref, rad_ref, cot_ref, wrad_ref, wblk_ref)
+    prepare(near, own_ref[...], refs, (pick_ref, sum_ref, gate_ref, dgate_ref), slots)
     halo = mm(near_ref[...], wnbr_ref[...]).astype(BF)
     side(halo, near, (self_ref, sum_ref, gate_ref, dgate_ref, pick_ref), msg_ref, adj_ref, rim_ref)
 
 
 def far_kernel(
-    far_ref, wnbr_ref, self_ref, sum_ref, gate_ref, dgate_ref, pick_ref, order_ref,
-    msg_ref, adj_ref, rim_ref,
+    far_ref, wnbr_ref, self_ref, sum_ref, gate_ref, dgate_ref, pick_ref, msg_ref, adj_ref, rim_ref
 ):
     _, far, _, _ = halves(rim_ref.shape[0])
     halo = mm(far_ref[...], wnbr_ref[...]).astype(BF)
@@ -139,7 +149,7 @@
 
 
 def own_kernel(
-    nearmsg_ref, farmsg_ref, nearadj_ref, faradj_ref, pick_ref, wself_ref, wnbr_ref, wblk_ref,
+    nearmsg_ref, farmsg_ref, nearadj_ref, faradj_ref, nearpick_ref, farpick_ref, wself_ref, wnbr_ref, wblk_ref,
     blocks_hbm, grad_ref,
     nearblk_ref, farblk_ref, selfsum_ref, sems,
 ):
@@ -160,8 +170,8 @@
 
     @pl.when(lax.axis_index("cell") >= 0)
     def _():
-        near_back = mm_tn(pick_ref[pl.ds(near_edge, edges), : atoms + half], nearadj_ref[...])
-        far_back = mm_tn(pick_ref[pl.ds(far_edge, edges), : atoms + half], faradj_ref[...])
+        near_back = mm_tn(nearpick_ref[:, : atoms + half], nearadj_ref[...])
+        far_back = mm_tn(farpick_ref[:, : atoms + half], faradj_ref[...])
         selfsum_ref[pl.ds(near_off, half), :] = near_back[atoms:].astype(BF)
         selfsum_ref[pl.ds(far_off, half), :] = far_back[atoms:].astype(BF)
         total = (near_back[:atoms] + far_back[:atoms]).astype(BF)
@@ -220,7 +230,6 @@
     wrapped = across + [(0, count - 1), (count - 1, 0)]
     dma = pltpu.SemaphoreType.DMA
     edge_t = ((edges, width), BF)
-    both_t = ((2 * edges, width), BF)
     rim_t = ((half, width), BF)
     grad_t = ((atoms, width), BF)
     far_send, near_send, nbr, cnt = call(
@@ -233,32 +242,38 @@
         in_specs=[HB] * 3,
         flops=10**12,
     )
-    far = lax.ppermute(far_send, "cell", wrapped)
+    far = lax.ppermute(far_send, "cell", across)
     near = lax.ppermute(near_send, "cell", inside)
-    pick, total, gate, dgate, selfs = call(
+    pick_t = ((edges, 4 * half), BF)
+    edge_refs = (
+        nbr, cnt, radial.reshape(atoms * slots, basis), cotangent.reshape(atoms * slots, entries),
+        w_radial, w_block,
+    )
+    far_pick, total, gate, dgate, selfs, own = call(
         functools.partial(front_kernel, slots=slots),
         "front",
-        (
-            nbr, cnt, features,
-            radial.reshape(atoms * slots, basis), cotangent.reshape(atoms * slots, entries),
-            w_self, w_neighbour, w_radial, w_block,
-        ),
-        [((2 * edges, 4 * half), BF), both_t, both_t, both_t, grad_t],
+        edge_refs + (features, w_self, w_neighbour),
+        [pick_t, edge_t, edge_t, edge_t, grad_t, grad_t],
         16,
     )
-    refs = (selfs, total, gate, dgate, pick)
     side_t = [edge_t, edge_t, rim_t]
-    near_msg, near_adj, near_rim = call(near_kernel, "near", (near, w_neighbour) + refs, side_t, 12)
     far_msg, far_adj, far_rim = call(
-        far_kernel, "far", (far, w_neighbour) + refs + (near_rim,), side_t, 12
-    )
-    near_rim, far_rim = lax.optimization_barrier((near_rim, far_rim))
+        far_kernel, "far", (far, w_neighbour, selfs, total, gate, dgate, far_pick), side_t, 12
+    )
+    far_back = lax.ppermute(far_rim, "cell", wrapped)
+    near_msg, near_adj, near_rim, near_pick = call(
+        functools.partial(near_kernel, slots=slots),
+        "near",
+        edge_refs + (near, w_neighbour, selfs, own, far_msg),
+        side_t + [pick_t],
+        16,
+        scratch=[pltpu.VMEM((edges, width), BF)] * 3,
+    )
     near_back = lax.ppermute(near_rim, "cell", inside)
-    far_back = lax.ppermute(far_rim, "cell", across)
     blocks, grad = call(
         own_kernel,
         "own",
-        (near_msg, far_msg, near_adj, far_adj, pick, w_self, w_neighbour, w_block),
+        (near_msg, far_msg, near_adj, far_adj, near_pick, far_pick, w_self, w_neighbour, w_block),
         [((2 * edges, entries), BF), ((atoms, width), F32)],
         16,
         scratch=[

time: 19.3 us -> 19.1 us (0.990)
  the two profiles are of different devices: /device:TPU:23 before, /device:TPU:9 now
where the time goes in v4:
time: 19.1 us; the launch traced here: 18.9 us
  Pallas kernels  8.88 us (46%)
  starting transfers between devices  7.95 us (42%)
  waiting for transfers between devices  1.31 us (7%)
  between operations  0.78 us (4%)
    pallas_call x6, Pallas kernels, call(): pl.pallas_call(kernel, name=name, out_shape=[jax.ShapeDtypeStruct(shape,...  8.88 us
    ppermute x1, starting transfers between devices, body(): far = lax.ppermute(far_send, 'cell', across)  3.68 us
    ppermute x1, starting transfers between devices, body(): near_back = lax.ppermute(near_rim, 'cell', inside)  2.54 us
    ppermute x1, waiting for transfers between devices, body(): far = lax.ppermute(far_send, 'cell', across)  1.3 us
    ppermute x1, starting transfers between devices, body(): far_back = lax.ppermute(far_rim, 'cell', wrapped)  0.99 us
    ppermute x1, starting transfers between devices, body(): near = lax.ppermute(near_send, 'cell', inside)  0.74 us
  transfers between devices with their start and end apart: 4, of which 1 were waited for; matrix products, arithmetic and copies ran while one was open for 0% of the time, Pallas kernels for 35%

profile of v4, /device:TPU:9, one launch (start us, length us, event | category | flops | bytes accessed | tf_op | source)
XLA Modules:
  0.0 18.9 jit_solution(15459083206742943272)
XLA Ops:
  0.6 0.0 copy-start
  0.6 0.0 copy-start.1
  0.7 0.0 copy-start.2
  0.7 0.0 copy-start.3
  0.7 0.0 copy-start.4
  0.7 0.0 copy-start.5
  0.7 0.0 copy-start.6
  0.7 1.2 %head.1 = (bf16[128,512]{1,0:T(8,128)(2,1)S(1)}, bf16[128,512]{1,0:T(8,128)(2,1)S(1)}, s32[8,256]{1,0:T(8,128)S(1)}, s32[2,128]{1,0:T(2,128)S(1)}) custom-call(bf16[256,512]{1,0:T(8,128)(2,1)} %feat_ref.1, s32[8,256]{1,0:T(8,128)} %bitcast.10, s32[2,128]{1,0:T(2,128)} %bitcast.11), custom_call_target="tpu_custom_call" | custom-call | flops 999999995904 | tf_op jit(solution)/shard_map/head/pallas_call | solution.py:207
  1.9 3.7 %collective-permute-start.1 = (bf16[128,512]{1,0:T(8,128)(2,1)S(1)}, bf16[128,512]{1,0:T(8,128)(2,1)S(1)}, u32[]{:S(2)}, u32[]{:S(2)}) collective-permute-start(bf16[128,512]{1,0:T(8,128)(2,1)S(1)} %get-tuple-element.26), channel_id=1, source_target_pairs={{1,2},{2,1},{3,4},{4,3},{5,6},{6,5},{7,8},{8,7},{9,10},{10,9},{11,... | collective-permute-start | bytes 393224 | tf_op jit(solution)/shard_map/ppermute | solution.py:245
  5.6 0.7 %collective-permute-start = (bf16[128,512]{1,0:T(8,128)(2,1)S(1)}, bf16[128,512]{1,0:T(8,128)(2,1)S(1)}, u32[]{:S(2)}, u32[]{:S(2)}) collective-permute-start(bf16[128,512]{1,0:T(8,128)(2,1)S(1)} %get-tuple-element.23), channel_id=1, source_target_pairs={{0,1},{1,0},{2,3},{3,2},{4,5},{5,4},{6,7},{7,6},{8,9},{9,8},{10,11... | collective-permute-start | bytes 393224 | tf_op jit(solution)/shard_map/ppermute | solution.py:246
  6.3 0.0 copy-done
  6.3 0.0 copy-done.1
  6.3 0.0 copy-done.2
  6.4 1.4 %front.1 = (bf16[1024,512]{1,0:T(8,128)(2,1)S(1)}, bf16[1024,512]{1,0:T(8,128)(2,1)S(1)}, bf16[1024,512]{1,0:T(8,128)(2,1)S(1)}, bf16[1024,512]{1,0:T(8,128)(2,1...) custom-call(s32[8,256]{1,0:T(8,128)S(1)} %get-tuple-element.21.nbr_ref, ...), custom_call_target="tpu_custom_call" | custom-call | tf_op jit(solution)/shard_map/front/pallas_call | solution.py:207
  7.7 1.3 %collective-permute-done.1.far_ref = bf16[128,512]{1,0:T(8,128)(2,1)S(1)} collective-permute-done((bf16[128,512]{1,0:T(8,128)(2,1)S(1)}, bf16[128,512]{1,0:T(8,128)(2,1)S(1)}, u32[]{:S(2)}, u32[]{:S(2)}) %collective-permute-start.1) | collective-permute-done | bytes 131104 | tf_op jit(solution)/shard_map/ppermute | solution.py:245
  9.0 1.0 %far.1 = (bf16[1024,512]{1,0:T(8,128)(2,1)S(1)}, bf16[1024,512]{1,0:T(8,128)(2,1)S(1)}, bf16[128,512]{1,0:T(8,128)(2,1)S(1)}) custom-call(bf16[128,512]{1,0:T(8,128)(2,1)S(1)} %collective-permute-done.1.far_ref, bf16[512,512]{1,0:T(8,128)(2,1)S(1)} %copy-done, bf16[256,512]{1,0:T(8,128)(2,1)S(1)} %get-tuple-element.24.self_ref, ...), custom_call_target="tpu_custom_call" | custom-call | tf_op jit(solution)/shard_map/far/pallas_call | solution.py:207
  10.1 1.0 %collective-permute-start.2 = (bf16[128,512]{1,0:T(8,128)(2,1)S(1)}, bf16[128,512]{1,0:T(8,128)(2,1)S(1)}, u32[]{:S(2)}, u32[]{:S(2)}) collective-permute-start(bf16[128,512]{1,0:T(8,128)(2,1)S(1)} %get-tuple-element.37), channel_id=1, source_target_pairs={{1,2},{2,1},{3,4},{4,3},{5,6},{6,5},{7,8},{8,7},{9,10},{10,9},{11,... | collective-permute-start | bytes 393224 | tf_op jit(solution)/shard_map/ppermute | solution.py:263
  11.0 0.0 collective-permute-done.near_ref
  11.0 2.0 %near.1 = (bf16[1024,512]{1,0:T(8,128)(2,1)S(1)}, bf16[1024,512]{1,0:T(8,128)(2,1)S(1)}, bf16[128,512]{1,0:T(8,128)(2,1)S(1)}, bf16[1024,512]{1,0:T(8,128)(2,1)S(1)}) custom-call(s32[8,256]{1,0:T(8,128)S(1)} %get-tuple-element.21.nbr_ref, s32[2,128]{1,0:T(2,128)S(1)} %get-tuple-element.22.cnt_ref, bf16[2048,128]{1,0:T(8,128)(2,1)S(1)} %bitcast.8, ...), custom_call_target="tpu_custom_call" | custom-call | tf_op jit(solution)/shard_map/near/pallas_call | solution.py:207
  13.1 2.5 %collective-permute-start.3 = (bf16[128,512]{1,0:T(8,128)(2,1)S(1)}, bf16[128,512]{1,0:T(8,128)(2,1)S(1)}, u32[]{:S(2)}, u32[]{:S(2)}) collective-permute-start(bf16[128,512]{1,0:T(8,128)(2,1)S(1)} %get-tuple-element.38), channel_id=1, source_target_pairs={{0,1},{1,0},{2,3},{3,2},{4,5},{5,4},{6,7},{7,6},{8,9},{9,8},{10,11... | collective-permute-start | bytes 393224 | tf_op jit(solution)/shard_map/ppermute | solution.py:272
  15.6 2.2 %own.1 = (bf16[2048,256]{1,0:T(8,128)(2,1)}, f32[256,512]{1,0:T(8,128)S(1)}) custom-call(bf16[1024,512]{1,0:T(8,128)(2,1)S(1)} %get-tuple-element.32.nearmsg_ref, bf16[1024,512]{1,0:T(8,128)(2,1)S(1)} %get-tuple-element.31.order_ref.farmsg_ref, bf16[1024,512]{1,0:T(8,128)(2,1)S(1)} %get-tuple-element.33.nearadj_ref, ...), custom_call_target="tpu_custom_call" | custom-call | tf_op jit(solution)/shard_map/own/pallas_call | solution.py:207
  17.8 0.0 collective-permute-done.2.far_ref
  17.8 0.0 collective-permute-done.3.near_ref
  17.8 1.1 %last.1 = bf16[256,512]{1,0:T(8,128)(2,1)} custom-call(bf16[128,512]{1,0:T(8,128)(2,1)S(1)} %collective-permute-done.2.far_ref, bf16[128,512]{1,0:T(8,128)(2,1)S(1)} %collective-permute-done.3.near_ref, f32[256,512]{1,0:T(8,128)S(1)} %get-tuple-element.39.grad_ref, bf16[512,512]{1,0:T(8,128)(2,1)S(1)} %copy-done), custom_call_target="tpu_custom_call" | custom-call | tf_op jit(solution)/shard_map/last/pallas_call | solution.py:207
  (4 shorter events, 0.0 us)
Async XLA Ops:
  0.6 5.7 %copy-start = (bf16[512,512]{1,0:T(8,128)(2,1)S(1)}, bf16[512,512]{1,0:T(8,128)(2,1)}, u32[]{:S(2)}) copy-start(bf16[512,512]{1,0:T(8,128)(2,1)} %wnbr_ref.9) | copy-start | bytes 1572868
  0.6 5.7 %copy-start.1 = (bf16[256,8,256]{2,1,0:T(8,128)(2,1)S(1)}, bf16[256,8,256]{2,1,0:T(8,128)(2,1)}, u32[]{:S(2)}) copy-start(bf16[256,8,256]{2,1,0:T(8,128)(2,1)} %param.13) | copy-start | bytes 3145732
  0.7 5.7 %copy-start.2 = (bf16[512,256]{1,0:T(8,128)(2,1)S(1)}, bf16[512,256]{1,0:T(8,128)(2,1)}, u32[]{:S(2)}) copy-start(bf16[512,256]{1,0:T(8,128)(2,1)} %wblk_ref.5) | copy-start | bytes 786436
  0.7 5.7 %copy-start.3 = (bf16[256,8,128]{2,1,0:T(8,128)(2,1)S(1)}, bf16[256,8,128]{2,1,0:T(8,128)(2,1)}, u32[]{:S(2)}) copy-start(bf16[256,8,128]{2,1,0:T(8,128)(2,1)} %param.10) | copy-start | bytes 1572868
  0.7 5.7 %copy-start.4 = (bf16[512,512]{1,0:T(8,128)(2,1)S(1)}, bf16[512,512]{1,0:T(8,128)(2,1)}, u32[]{:S(2)}) copy-start(bf16[512,512]{1,0:T(8,128)(2,1)} %wself_ref.3) | copy-start | bytes 1572868
  0.7 5.7 %copy-start.5 = (bf16[128,512]{1,0:T(8,128)(2,1)S(1)}, bf16[128,512]{1,0:T(8,128)(2,1)}, u32[]{:S(2)}) copy-start(bf16[128,512]{1,0:T(8,128)(2,1)} %wrad_ref.3) | copy-start | bytes 393220
  0.7 5.7 %copy-start.6 = (bf16[256,512]{1,0:T(8,128)(2,1)S(1)}, bf16[256,512]{1,0:T(8,128)(2,1)}, u32[]{:S(2)}) copy-start(bf16[256,512]{1,0:T(8,128)(2,1)} %feat_ref.1) | copy-start | bytes 786436
  1.9 7.1 %collective-permute-start.1 = (bf16[128,512]{1,0:T(8,128)(2,1)S(1)}, bf16[128,512]{1,0:T(8,128)(2,1)S(1)}, u32[]{:S(2)}, u32[]{:S(2)}) collective-permute-start(bf16[128,512]{1,0:T(8,128)(2,1)S(1)} %get-tuple-element.26), channel_id=1, source_target_pairs={{1,2},{2,1},{3,4},{4,3},{5,6},{6,5},{7,8},{8,7},{9,10},{10,9},{11,... | collective-permute-start | bytes 393224 | tf_op jit(solution)/shard_map/ppermute | solution.py:245
  5.6 5.5 %collective-permute-start = (bf16[128,512]{1,0:T(8,128)(2,1)S(1)}, bf16[128,512]{1,0:T(8,128)(2,1)S(1)}, u32[]{:S(2)}, u32[]{:S(2)}) collective-permute-start(bf16[128,512]{1,0:T(8,128)(2,1)S(1)} %get-tuple-element.23), channel_id=1, source_target_pairs={{0,1},{1,0},{2,3},{3,2},{4,5},{5,4},{6,7},{7,6},{8,9},{9,8},{10,11... | collective-permute-start | bytes 393224 | tf_op jit(solution)/shard_map/ppermute | solution.py:246
  10.1 7.7 %collective-permute-start.2 = (bf16[128,512]{1,0:T(8,128)(2,1)S(1)}, bf16[128,512]{1,0:T(8,128)(2,1)S(1)}, u32[]{:S(2)}, u32[]{:S(2)}) collective-permute-start(bf16[128,512]{1,0:T(8,128)(2,1)S(1)} %get-tuple-element.37), channel_id=1, source_target_pairs={{1,2},{2,1},{3,4},{4,3},{5,6},{6,5},{7,8},{8,7},{9,10},{10,9},{11,... | collective-permute-start | bytes 393224 | tf_op jit(solution)/shard_map/ppermute | solution.py:263
  13.1 4.7 %collective-permute-start.3 = (bf16[128,512]{1,0:T(8,128)(2,1)S(1)}, bf16[128,512]{1,0:T(8,128)(2,1)S(1)}, u32[]{:S(2)}, u32[]{:S(2)}) collective-permute-start(bf16[128,512]{1,0:T(8,128)(2,1)S(1)} %get-tuple-element.38), channel_id=1, source_target_pairs={{0,1},{1,0},{2,3},{3,2},{4,5},{5,4},{6,7},{7,6},{8,9},{9,8},{10,11... | collective-permute-start | bytes 393224 | tf_op jit(solution)/shard_map/ppermute | solution.py:272

commit v5 on v4

--- a/solution.py
+++ b/solution.py
@@ -21,6 +21,34 @@
 
 def mm_tn(a, b):
     return lax.dot_general(a, b, (((0,), (0,)), ((), ())), preferred_element_type=F32)
+
+
+def swaps(pairs):
+    return [edge for a, b in pairs for edge in ((a, b), (b, a))]
+
+
+def in_first(device):
+    return ((device + 1) // 2 + 1) // 4 % 2 == 0
+
+
+def chip_swaps(count):
+    across = [(i, i + 1) for i in range(1, count - 1, 2)]
+    if count < 16 or count % 8:
+        return swaps(across), swaps(across)
+    both = []
+    for first in (True, False):
+        pairs = [pair for pair in across if in_first(pair[0]) == first]
+        busy = {device for pair in pairs for device in pair}
+        rest = [device for device in range(count) if device not in busy]
+        both.append(swaps(pairs + list(zip(rest[::2], rest[1::2]))))
+    return both
+
+
+def from_across(count, first_ref, second_ref):
+    device = lax.axis_index("cell")
+    value = jnp.where(in_first(device), first_ref[...], second_ref[...])
+    inner = (device > 0) & (device < count - 1)
+    return jnp.where(inner, value, jnp.zeros_like(value))
 
 
 def halves(half):
@@ -128,7 +156,7 @@
 
 
 def near_kernel(
-    nbr_ref, cnt_ref, rad_ref, cot_ref, wrad_ref, wblk_ref, near_ref, wnbr_ref, self_ref, own_ref, order_ref,
+    nbr_ref, cnt_ref, rad_ref, cot_ref, wrad_ref, wblk_ref, near_ref, wnbr_ref, self_ref, own_ref,
     msg_ref, adj_ref, rim_ref, pick_ref,
     sum_ref, gate_ref, dgate_ref,
     *, slots,
@@ -141,10 +169,12 @@
 
 
 def far_kernel(
-    far_ref, wnbr_ref, self_ref, sum_ref, gate_ref, dgate_ref, pick_ref, msg_ref, adj_ref, rim_ref
+    second_ref, first_ref, wnbr_ref, self_ref, sum_ref, gate_ref, dgate_ref, pick_ref, order_ref,
+    msg_ref, adj_ref, rim_ref,
+    *, count,
 ):
     _, far, _, _ = halves(rim_ref.shape[0])
-    halo = mm(far_ref[...], wnbr_ref[...]).astype(BF)
+    halo = mm(from_across(count, first_ref, second_ref), wnbr_ref[...]).astype(BF)
     side(halo, far, (self_ref, sum_ref, gate_ref, dgate_ref, pick_ref), msg_ref, adj_ref, rim_ref)
 
 
@@ -181,17 +211,19 @@
     far_copy.wait()
 
 
-def last_kernel(far_ref, near_ref, grad_ref, wnbr_ref, out_hbm, fout_ref, nout_ref, sem):
+def last_kernel(second_ref, first_ref, near_ref, grad_ref, wnbr_ref, out_hbm, out_ref, sem, *, count):
     half = near_ref.shape[0]
     _, _, near_off, far_off = halves(half)
-    fout_ref[...] = (grad_ref[pl.ds(far_off, half), :] + mm_nt(far_ref[...], wnbr_ref[...])).astype(BF)
-    c0 = pltpu.make_async_copy(fout_ref, out_hbm.at[pl.ds(far_off, half)], sem.at[0])
-    c0.start()
-    nout_ref[...] = (grad_ref[pl.ds(near_off, half), :] + mm_nt(near_ref[...], wnbr_ref[...])).astype(BF)
-    c1 = pltpu.make_async_copy(nout_ref, out_hbm.at[pl.ds(near_off, half)], sem.at[1])
-    c1.start()
-    c0.wait()
-    c1.wait()
+    rims = jnp.concatenate([from_across(count, first_ref, second_ref), near_ref[...]], axis=0)
+    grads = jnp.concatenate(
+        [grad_ref[pl.ds(far_off, half), :], grad_ref[pl.ds(near_off, half), :]], axis=0
+    )
+    total = (grads + mm_nt(rims, wnbr_ref[...])).astype(BF)
+    out_ref[pl.ds(far_off, half), :] = total[:half]
+    out_ref[pl.ds(near_off, half), :] = total[half:]
+    copy = pltpu.make_async_copy(out_ref, out_hbm, sem)
+    copy.start()
+    copy.wait()
 
 
 VM = pl.BlockSpec(memory_space=pltpu.VMEM)
@@ -224,10 +256,7 @@
     entries = w_block.shape[1]
     basis = radial.shape[2]
     inside = [(i, i ^ 1) for i in range(count)]
-    across = []
-    for i in range(1, count - 1, 2):
-        across += [(i, i + 1), (i + 1, i)]
-    wrapped = across + [(0, count - 1), (count - 1, 0)]
+    first, second = chip_swaps(count)
     dma = pltpu.SemaphoreType.DMA
     edge_t = ((edges, width), BF)
     rim_t = ((half, width), BF)
@@ -242,7 +271,8 @@
         in_specs=[HB] * 3,
         flops=10**12,
     )
-    far = lax.ppermute(far_send, "cell", across)
+    far_first = lax.ppermute(far_send, "cell", first)
+    far_second = lax.ppermute(far_send, "cell", second)
     near = lax.ppermute(near_send, "cell", inside)
     pick_t = ((edges, 4 * half), BF)
     edge_refs = (
@@ -257,19 +287,24 @@
         16,
     )
     side_t = [edge_t, edge_t, rim_t]
-    far_msg, far_adj, far_rim = call(
-        far_kernel, "far", (far, w_neighbour, selfs, total, gate, dgate, far_pick), side_t, 12
-    )
-    far_back = lax.ppermute(far_rim, "cell", wrapped)
     near_msg, near_adj, near_rim, near_pick = call(
         functools.partial(near_kernel, slots=slots),
         "near",
-        edge_refs + (near, w_neighbour, selfs, own, far_msg),
+        edge_refs + (near, w_neighbour, selfs, own),
         side_t + [pick_t],
         16,
         scratch=[pltpu.VMEM((edges, width), BF)] * 3,
     )
     near_back = lax.ppermute(near_rim, "cell", inside)
+    far_msg, far_adj, far_rim = call(
+        functools.partial(far_kernel, count=count),
+        "far",
+        (far_second, far_first, w_neighbour, selfs, total, gate, dgate, far_pick, near_msg),
+        side_t,
+        12,
+    )
+    far_back_second = lax.ppermute(far_rim, "cell", second)
+    far_back_first = lax.ppermute(far_rim, "cell", first)
     blocks, grad = call(
         own_kernel,
         "own",
@@ -285,12 +320,12 @@
         out_specs=[HB, VM],
     )
     (feat_grad,) = call(
-        last_kernel,
+        functools.partial(last_kernel, count=count),
         "last",
-        (far_back, near_back, grad, w_neighbour),
+        (far_back_second, far_back_first, near_back, grad, w_neighbour),
         [grad_t],
         4,
-        scratch=[pltpu.VMEM((half, width), BF), pltpu.VMEM((half, width), BF), dma((2,))],
+        scratch=[pltpu.VMEM((atoms, width), BF), dma],
         out_specs=[HB],
     )
     return blocks.reshape(atoms, slots, entries), feat_grad

time: 19.1 us -> 18.4 us (0.963)
  the two profiles are of different devices: /device:TPU:9 before, /device:TPU:29 now
where the time goes in v5:
time: 18.4 us; the launch traced here: 18.2 us
  Pallas kernels  8.66 us (47%)
  waiting for transfers between devices  4.64 us (25%)
  starting transfers between devices  4.09 us (22%)
  between operations  0.78 us (4%)
    pallas_call x6, Pallas kernels, call(): pl.pallas_call(kernel, name=name, out_shape=[jax.ShapeDtypeStruct(shape,...  8.66 us
    ppermute x1, waiting for transfers between devices, body(): far_back_first = lax.ppermute(far_rim, 'cell', first)  3.12 us
    ppermute x1, starting transfers between devices, body(): far_back_second = lax.ppermute(far_rim, 'cell', second)  1.57 us
    ppermute x1, waiting for transfers between devices, body(): far_first = lax.ppermute(far_send, 'cell', first)  1.52 us
    ppermute x1, starting transfers between devices, body(): far_first = lax.ppermute(far_send, 'cell', first)  1.17 us
    ppermute x1, starting transfers between devices, body(): near = lax.ppermute(near_send, 'cell', inside)  0.74 us
    ppermute x1, starting transfers between devices, body(): far_second = lax.ppermute(far_send, 'cell', second)  0.43 us
  transfers between devices with their start and end apart: 6, of which 2 were waited for; matrix products, arithmetic and copies ran while one was open for 0% of the time, Pallas kernels for 35%

profile of v5, /device:TPU:29, one launch (start us, length us, event | category | flops | bytes accessed | tf_op | source)
XLA Modules:
  0.0 18.2 jit_solution(16120485381025060185)
XLA Ops:
  0.6 0.0 copy-start
  0.6 0.0 copy-start.1
  0.7 0.0 copy-start.2
  0.7 0.0 copy-start.3
  0.7 0.0 copy-start.4
  0.7 0.0 copy-start.5
  0.7 1.2 %head.1 = (bf16[128,512]{1,0:T(8,128)(2,1)S(1)}, bf16[128,512]{1,0:T(8,128)(2,1)S(1)}, s32[8,256]{1,0:T(8,128)S(1)}, s32[2,128]{1,0:T(2,128)S(1)}) custom-call(bf16[256,512]{1,0:T(8,128)(2,1)} %feat_ref.1, s32[8,256]{1,0:T(8,128)} %bitcast.10, s32[2,128]{1,0:T(2,128)} %bitcast.11), custom_call_target="tpu_custom_call" | custom-call | flops 999999995904 | tf_op jit(solution)/shard_map/head/pallas_call | solution.py:239
  1.9 0.7 %collective-permute-start = (bf16[128,512]{1,0:T(8,128)(2,1)S(1)}, bf16[128,512]{1,0:T(8,128)(2,1)S(1)}, u32[]{:S(2)}, u32[]{:S(2)}) collective-permute-start(bf16[128,512]{1,0:T(8,128)(2,1)S(1)} %get-tuple-element.23), channel_id=1, source_target_pairs={{0,1},{1,0},{2,3},{3,2},{4,5},{5,4},{6,7},{7,6},{8,9},{9,8},{10,11... | collective-permute-start | bytes 393224 | tf_op jit(solution)/shard_map/ppermute | solution.py:276
  2.6 1.2 %collective-permute-start.2 = (bf16[128,512]{1,0:T(8,128)(2,1)S(1)}, bf16[128,512]{1,0:T(8,128)(2,1)S(1)}, u32[]{:S(2)}, u32[]{:S(2)}) collective-permute-start(bf16[128,512]{1,0:T(8,128)(2,1)S(1)} %get-tuple-element.27), channel_id=1, source_target_pairs={{1,2},{2,1},{3,4},{4,3},{13,14},{14,13},{15,16},{16,15},{17,18},{1... | collective-permute-start | bytes 393224 | tf_op jit(solution)/shard_map/ppermute | solution.py:274
  3.8 0.4 %collective-permute-start.1 = (bf16[128,512]{1,0:T(8,128)(2,1)S(1)}, bf16[128,512]{1,0:T(8,128)(2,1)S(1)}, u32[]{:S(2)}, u32[]{:S(2)}) collective-permute-start(bf16[128,512]{1,0:T(8,128)(2,1)S(1)} %get-tuple-element.27), channel_id=1, source_target_pairs={{5,6},{6,5},{7,8},{8,7},{9,10},{10,9},{11,12},{12,11},{21,22},{22,... | collective-permute-start | bytes 393224 | tf_op jit(solution)/shard_map/ppermute | solution.py:275
  4.3 1.4 %front.1 = (bf16[1024,512]{1,0:T(8,128)(2,1)S(1)}, bf16[1024,512]{1,0:T(8,128)(2,1)S(1)}, bf16[1024,512]{1,0:T(8,128)(2,1)S(1)}, bf16[1024,512]{1,0:T(8,128)(2,1...) custom-call(s32[8,256]{1,0:T(8,128)S(1)} %get-tuple-element.21.nbr_ref, ...), custom_call_target="tpu_custom_call" | custom-call | tf_op jit(solution)/shard_map/front/pallas_call | solution.py:239
  5.6 0.0 collective-permute-done.near_ref
  5.6 1.9 %near.1 = (bf16[1024,512]{1,0:T(8,128)(2,1)S(1)}, bf16[1024,512]{1,0:T(8,128)(2,1)S(1)}, bf16[128,512]{1,0:T(8,128)(2,1)S(1)}, bf16[1024,512]{1,0:T(8,128)(2,1)S(1)}) custom-call(s32[8,256]{1,0:T(8,128)S(1)} %get-tuple-element.21.nbr_ref, s32[2,128]{1,0:T(2,128)S(1)} %get-tuple-element.22.cnt_ref, bf16[2048,128]{1,0:T(8,128)(2,1)S(1)} %bitcast.8, ...), custom_call_target="tpu_custom_call" | custom-call | tf_op jit(solution)/shard_map/near/pallas_call | solution.py:239
  7.6 0.1 collective-permute-start.5
  7.7 1.5 %collective-permute-done.2.first_ref = bf16[128,512]{1,0:T(8,128)(2,1)S(1)} collective-permute-done((bf16[128,512]{1,0:T(8,128)(2,1)S(1)}, bf16[128,512]{1,0:T(8,128)(2,1)S(1)}, u32[]{:S(2)}, u32[]{:S(2)}) %collective-permute-start.2) | collective-permute-done | bytes 131104 | tf_op jit(solution)/shard_map/ppermute | solution.py:274
  9.2 0.0 collective-permute-done.1.second_ref
  9.2 1.0 %far.1 = (bf16[1024,512]{1,0:T(8,128)(2,1)S(1)}, bf16[1024,512]{1,0:T(8,128)(2,1)S(1)}, bf16[128,512]{1,0:T(8,128)(2,1)S(1)}) custom-call(bf16[128,512]{1,0:T(8,128)(2,1)S(1)} %collective-permute-done.1.second_ref, bf16[128,512]{1,0:T(8,128)(2,1)S(1)} %collective-permute-done.2.first_ref, bf16[512,512]{1,0:T(8,128)(2,1)S(1)} %copy-done, ...), custom_call_target="tpu_custom_call" | custom-call | tf_op jit(solution)/shard_map/far/pallas_call | solution.py:239
  10.3 0.1 collective-permute-start.4
  10.3 1.6 %collective-permute-start.3 = (bf16[128,512]{1,0:T(8,128)(2,1)S(1)}, bf16[128,512]{1,0:T(8,128)(2,1)S(1)}, u32[]{:S(2)}, u32[]{:S(2)}) collective-permute-start(bf16[128,512]{1,0:T(8,128)(2,1)S(1)} %get-tuple-element.37), channel_id=1, source_target_pairs={{5,6},{6,5},{7,8},{8,7},{9,10},{10,9},{11,12},{12,11},{21,22},{22,... | collective-permute-start | bytes 393224 | tf_op jit(solution)/shard_map/ppermute | solution.py:306
  11.9 2.1 %own.1 = (bf16[2048,256]{1,0:T(8,128)(2,1)}, f32[256,512]{1,0:T(8,128)S(1)}) custom-call(bf16[1024,512]{1,0:T(8,128)(2,1)S(1)} %get-tuple-element.26.order_ref.nearmsg_ref, bf16[1024,512]{1,0:T(8,128)(2,1)S(1)} %get-tuple-element.32.farmsg_ref, bf16[1024,512]{1,0:T(8,128)(2,1)S(1)} %get-tuple-element.33.nearadj_ref, ...), custom_call_target="tpu_custom_call" | custom-call | tf_op jit(solution)/shard_map/own/pallas_call | solution.py:239
  14.0 0.0 collective-permute-done.5.near_ref
  14.0 3.1 %collective-permute-done.4.first_ref = bf16[128,512]{1,0:T(8,128)(2,1)S(1)} collective-permute-done((bf16[128,512]{1,0:T(8,128)(2,1)S(1)}, bf16[128,512]{1,0:T(8,128)(2,1)S(1)}, u32[]{:S(2)}, u32[]{:S(2)}) %collective-permute-start.4) | collective-permute-done | bytes 131104 | tf_op jit(solution)/shard_map/ppermute | solution.py:307
  17.2 0.0 collective-permute-done.3.second_ref
  17.2 1.1 %last.1 = bf16[256,512]{1,0:T(8,128)(2,1)} custom-call(bf16[128,512]{1,0:T(8,128)(2,1)S(1)} %collective-permute-done.3.second_ref, bf16[128,512]{1,0:T(8,128)(2,1)S(1)} %collective-permute-done.4.first_ref, bf16[128,512]{1,0:T(8,128)(2,1)S(1)} %collective-permute-done.5.near_ref, f32[256,512]{1,0:T(8,128)S(1)} %get-tuple-element.39.grad_ref, ...), custom_call_target="tpu_custom_call" | custom-call | tf_op jit(solution)/shard_map/last/pallas_call | solution.py:239
  (8 shorter events, 0.0 us)
Async XLA Ops:
  0.6 3.6 %copy-start = (bf16[512,512]{1,0:T(8,128)(2,1)S(1)}, bf16[512,512]{1,0:T(8,128)(2,1)}, u32[]{:S(2)}) copy-start(bf16[512,512]{1,0:T(8,128)(2,1)} %wnbr_ref.9) | copy-start | bytes 1572868
  0.6 3.6 %copy-start.1 = (bf16[256,8,256]{2,1,0:T(8,128)(2,1)S(1)}, bf16[256,8,256]{2,1,0:T(8,128)(2,1)}, u32[]{:S(2)}) copy-start(bf16[256,8,256]{2,1,0:T(8,128)(2,1)} %param.13) | copy-start | bytes 3145732
  0.7 3.6 %copy-start.2 = (bf16[512,256]{1,0:T(8,128)(2,1)S(1)}, bf16[512,256]{1,0:T(8,128)(2,1)}, u32[]{:S(2)}) copy-start(bf16[512,256]{1,0:T(8,128)(2,1)} %wblk_ref.5) | copy-start | bytes 786436
  0.7 3.6 %copy-start.3 = (bf16[256,8,128]{2,1,0:T(8,128)(2,1)S(1)}, bf16[256,8,128]{2,1,0:T(8,128)(2,1)}, u32[]{:S(2)}) copy-start(bf16[256,8,128]{2,1,0:T(8,128)(2,1)} %param.10) | copy-start | bytes 1572868
  0.7 3.6 %copy-start.4 = (bf16[512,512]{1,0:T(8,128)(2,1)S(1)}, bf16[512,512]{1,0:T(8,128)(2,1)}, u32[]{:S(2)}) copy-start(bf16[512,512]{1,0:T(8,128)(2,1)} %wself_ref.3) | copy-start | bytes 1572868
  0.7 3.6 %copy-start.5 = (bf16[128,512]{1,0:T(8,128)(2,1)S(1)}, bf16[128,512]{1,0:T(8,128)(2,1)}, u32[]{:S(2)}) copy-start(bf16[128,512]{1,0:T(8,128)(2,1)} %wrad_ref.3) | copy-start | bytes 393220
  0.7 3.6 %copy-start.6 = (bf16[256,512]{1,0:T(8,128)(2,1)S(1)}, bf16[256,512]{1,0:T(8,128)(2,1)}, u32[]{:S(2)}) copy-start(bf16[256,512]{1,0:T(8,128)(2,1)} %feat_ref.1) | copy-start | bytes 786436
  1.9 3.8 %collective-permute-start = (bf16[128,512]{1,0:T(8,128)(2,1)S(1)}, bf16[128,512]{1,0:T(8,128)(2,1)S(1)}, u32[]{:S(2)}, u32[]{:S(2)}) collective-permute-start(bf16[128,512]{1,0:T(8,128)(2,1)S(1)} %get-tuple-element.23), channel_id=1, source_target_pairs={{0,1},{1,0},{2,3},{3,2},{4,5},{5,4},{6,7},{7,6},{8,9},{9,8},{10,11... | collective-permute-start | bytes 393224 | tf_op jit(solution)/shard_map/ppermute | solution.py:276
  2.6 6.6 %collective-permute-start.2 = (bf16[128,512]{1,0:T(8,128)(2,1)S(1)}, bf16[128,512]{1,0:T(8,128)(2,1)S(1)}, u32[]{:S(2)}, u32[]{:S(2)}) collective-permute-start(bf16[128,512]{1,0:T(8,128)(2,1)S(1)} %get-tuple-element.27), channel_id=1, source_target_pairs={{1,2},{2,1},{3,4},{4,3},{13,14},{14,13},{15,16},{16,15},{17,18},{1... | collective-permute-start | bytes 393224 | tf_op jit(solution)/shard_map/ppermute | solution.py:274
  3.8 5.4 %collective-permute-start.1 = (bf16[128,512]{1,0:T(8,128)(2,1)S(1)}, bf16[128,512]{1,0:T(8,128)(2,1)S(1)}, u32[]{:S(2)}, u32[]{:S(2)}) collective-permute-start(bf16[128,512]{1,0:T(8,128)(2,1)S(1)} %get-tuple-element.27), channel_id=1, source_target_pairs={{5,6},{6,5},{7,8},{8,7},{9,10},{10,9},{11,12},{12,11},{21,22},{22,... | collective-permute-start | bytes 393224 | tf_op jit(solution)/shard_map/ppermute | solution.py:275
  7.6 6.4 %collective-permute-start.5 = (bf16[128,512]{1,0:T(8,128)(2,1)S(1)}, bf16[128,512]{1,0:T(8,128)(2,1)S(1)}, u32[]{:S(2)}, u32[]{:S(2)}) collective-permute-start(bf16[128,512]{1,0:T(8,128)(2,1)S(1)} %get-tuple-element.38), channel_id=1, source_target_pairs={{0,1},{1,0},{2,3},{3,2},{4,5},{5,4},{6,7},{7,6},{8,9},{9,8},{10,11... | collective-permute-start | bytes 393224 | tf_op jit(solution)/shard_map/ppermute | solution.py:298
  10.3 6.9 %collective-permute-start.4 = (bf16[128,512]{1,0:T(8,128)(2,1)S(1)}, bf16[128,512]{1,0:T(8,128)(2,1)S(1)}, u32[]{:S(2)}, u32[]{:S(2)}) collective-permute-start(bf16[128,512]{1,0:T(8,128)(2,1)S(1)} %get-tuple-element.37), channel_id=1, source_target_pairs={{1,2},{2,1},{3,4},{4,3},{13,14},{14,13},{15,16},{16,15},{17,18},{1... | collective-permute-start | bytes 393224 | tf_op jit(solution)/shard_map/ppermute | solution.py:307
  10.3 6.8 %collective-permute-start.3 = (bf16[128,512]{1,0:T(8,128)(2,1)S(1)}, bf16[128,512]{1,0:T(8,128)(2,1)S(1)}, u32[]{:S(2)}, u32[]{:S(2)}) collective-permute-start(bf16[128,512]{1,0:T(8,128)(2,1)S(1)} %get-tuple-element.37), channel_id=1, source_target_pairs={{5,6},{6,5},{7,8},{8,7},{9,10},{10,9},{11,12},{12,11},{21,22},{22,... | collective-permute-start | bytes 393224 | tf_op jit(solution)/shard_map/ppermute | solution.py:306

commit v6 on v5

--- a/solution.py
+++ b/solution.py
@@ -82,11 +82,12 @@
     return jnp.concatenate([low, high, mine, halo], axis=1)
 
 
-def activation(total, half_gate, half_dgate):
-    h = total * half_gate
-    t = jnp.tanh(h)
-    ht = h * t
-    return h + ht, half_dgate * (t + BF(1.0)) * (h - ht + BF(1.0))
+def activation(total, gate, dgate):
+    v = total * gate
+    e = jnp.exp(jnp.minimum(-v, BF(80.0)))
+    s = pl.reciprocal(e + BF(1.0), approx=True)
+    message = v * s
+    return message, dgate * s * (message * e + BF(1.0))
 
 
 def head_kernel(feat_hbm, nbr_hbm, cnt_hbm, far_ref, near_ref, nbr_ref, cnt_ref, sems):
@@ -119,7 +120,7 @@
         half,
         slots,
     )
-    gate = mm(rad_ref[rows, :], wrad_ref[...] * BF(0.5))
+    gate = mm(rad_ref[rows, :], wrad_ref[...])
     gate_ref[...] = gate.astype(BF)
     sum_ref[...] = mm(pick_ref[:, : 2 * half], own).astype(BF)
     dgate_ref[...] = (mm_nt(cot_ref[rows, :], wblk_ref[...]) * gate).astype(BF)

time: 18.4 us -> 18.5 us (level)
  Pallas kernels: 8.66 us -> 8.97 us
    pallas_call x6, Pallas kernels: 8.66 us -> 8.97 us  [call(): pl.pallas_call(kernel, name=name, out_shape=[jax.ShapeDtypeStruct(shape,...]
  transfers between devices with their start and end apart: 6 -> 6, of which waited for: 2 -> 2; matrix products, arithmetic and copies ran while one was open for 0% -> 0% of each run, Pallas kernels for 35% -> 37%
where the time goes in v6:
time: 18.5 us; the launch traced here: 18.4 us
  Pallas kernels  8.97 us (48%)
  waiting for transfers between devices  4.53 us (24%)
  starting transfers between devices  4.08 us (22%)
  between operations  0.78 us (4%)
    pallas_call x6, Pallas kernels, call(): pl.pallas_call(kernel, name=name, out_shape=[jax.ShapeDtypeStruct(shape,...  8.97 us
    ppermute x1, waiting for transfers between devices, body(): far_back_first = lax.ppermute(far_rim, 'cell', first)  3.12 us
    ppermute x1, starting transfers between devices, body(): far_back_second = lax.ppermute(far_rim, 'cell', second)  1.57 us
    ppermute x1, waiting for transfers between devices, body(): far_first = lax.ppermute(far_send, 'cell', first)  1.4 us
    ppermute x1, starting transfers between devices, body(): far_first = lax.ppermute(far_send, 'cell', first)  1.17 us
    ppermute x1, starting transfers between devices, body(): near = lax.ppermute(near_send, 'cell', inside)  0.74 us
    ppermute x1, starting transfers between devices, body(): far_second = lax.ppermute(far_send, 'cell', second)  0.43 us
  transfers between devices with their start and end apart: 6, of which 2 were waited for; matrix products, arithmetic and copies ran while one was open for 0% of the time, Pallas kernels for 37%

profile of v6, /device:TPU:29, one launch (start us, length us, event | category | flops | bytes accessed | tf_op | source)
XLA Modules:
  0.0 18.4 jit_solution(4565266465579799842)
XLA Ops:
  0.6 0.0 copy-start
  0.6 0.0 copy-start.1
  0.7 0.0 copy-start.2
  0.7 0.0 copy-start.3
  0.7 0.0 copy-start.4
  0.7 0.0 copy-start.5
  0.7 1.2 %head.1 = (bf16[128,512]{1,0:T(8,128)(2,1)S(1)}, bf16[128,512]{1,0:T(8,128)(2,1)S(1)}, s32[8,256]{1,0:T(8,128)S(1)}, s32[2,128]{1,0:T(2,128)S(1)}) custom-call(bf16[256,512]{1,0:T(8,128)(2,1)} %feat_ref.1, s32[8,256]{1,0:T(8,128)} %bitcast.10, s32[2,128]{1,0:T(2,128)} %bitcast.11), custom_call_target="tpu_custom_call" | custom-call | flops 999999995904 | tf_op jit(solution)/shard_map/head/pallas_call | solution.py:240
  1.9 0.7 %collective-permute-start = (bf16[128,512]{1,0:T(8,128)(2,1)S(1)}, bf16[128,512]{1,0:T(8,128)(2,1)S(1)}, u32[]{:S(2)}, u32[]{:S(2)}) collective-permute-start(bf16[128,512]{1,0:T(8,128)(2,1)S(1)} %get-tuple-element.23), channel_id=1, source_target_pairs={{0,1},{1,0},{2,3},{3,2},{4,5},{5,4},{6,7},{7,6},{8,9},{9,8},{10,11... | collective-permute-start | bytes 393224 | tf_op jit(solution)/shard_map/ppermute | solution.py:277
  2.6 1.2 %collective-permute-start.2 = (bf16[128,512]{1,0:T(8,128)(2,1)S(1)}, bf16[128,512]{1,0:T(8,128)(2,1)S(1)}, u32[]{:S(2)}, u32[]{:S(2)}) collective-permute-start(bf16[128,512]{1,0:T(8,128)(2,1)S(1)} %get-tuple-element.27), channel_id=1, source_target_pairs={{1,2},{2,1},{3,4},{4,3},{13,14},{14,13},{15,16},{16,15},{17,18},{1... | collective-permute-start | bytes 393224 | tf_op jit(solution)/shard_map/ppermute | solution.py:275
  3.8 0.4 %collective-permute-start.1 = (bf16[128,512]{1,0:T(8,128)(2,1)S(1)}, bf16[128,512]{1,0:T(8,128)(2,1)S(1)}, u32[]{:S(2)}, u32[]{:S(2)}) collective-permute-start(bf16[128,512]{1,0:T(8,128)(2,1)S(1)} %get-tuple-element.27), channel_id=1, source_target_pairs={{5,6},{6,5},{7,8},{8,7},{9,10},{10,9},{11,12},{12,11},{21,22},{22,... | collective-permute-start | bytes 393224 | tf_op jit(solution)/shard_map/ppermute | solution.py:276
  4.3 1.4 %front.1 = (bf16[1024,512]{1,0:T(8,128)(2,1)S(1)}, bf16[1024,512]{1,0:T(8,128)(2,1)S(1)}, bf16[1024,512]{1,0:T(8,128)(2,1)S(1)}, bf16[1024,512]{1,0:T(8,128)(2,1...) custom-call(s32[8,256]{1,0:T(8,128)S(1)} %get-tuple-element.21.nbr_ref, ...), custom_call_target="tpu_custom_call" | custom-call | tf_op jit(solution)/shard_map/front/pallas_call | solution.py:240
  5.6 0.0 collective-permute-done.near_ref
  5.6 2.1 %near.1 = (bf16[1024,512]{1,0:T(8,128)(2,1)S(1)}, bf16[1024,512]{1,0:T(8,128)(2,1)S(1)}, bf16[128,512]{1,0:T(8,128)(2,1)S(1)}, bf16[1024,512]{1,0:T(8,128)(2,1)S(1)}) custom-call(s32[8,256]{1,0:T(8,128)S(1)} %get-tuple-element.21.nbr_ref, s32[2,128]{1,0:T(2,128)S(1)} %get-tuple-element.22.cnt_ref, bf16[2048,128]{1,0:T(8,128)(2,1)S(1)} %bitcast.8, ...), custom_call_target="tpu_custom_call" | custom-call | tf_op jit(solution)/shard_map/near/pallas_call | solution.py:240
  7.7 0.1 collective-permute-start.5
  7.8 1.4 %collective-permute-done.2.first_ref = bf16[128,512]{1,0:T(8,128)(2,1)S(1)} collective-permute-done((bf16[128,512]{1,0:T(8,128)(2,1)S(1)}, bf16[128,512]{1,0:T(8,128)(2,1)S(1)}, u32[]{:S(2)}, u32[]{:S(2)}) %collective-permute-start.2) | collective-permute-done | bytes 131104 | tf_op jit(solution)/shard_map/ppermute | solution.py:275
  9.2 0.0 collective-permute-done.1.second_ref
  9.2 1.2 %far.1 = (bf16[1024,512]{1,0:T(8,128)(2,1)S(1)}, bf16[1024,512]{1,0:T(8,128)(2,1)S(1)}, bf16[128,512]{1,0:T(8,128)(2,1)S(1)}) custom-call(bf16[128,512]{1,0:T(8,128)(2,1)S(1)} %collective-permute-done.1.second_ref, bf16[128,512]{1,0:T(8,128)(2,1)S(1)} %collective-permute-done.2.first_ref, bf16[512,512]{1,0:T(8,128)(2,1)S(1)} %copy-done, ...), custom_call_target="tpu_custom_call" | custom-call | tf_op jit(solution)/shard_map/far/pallas_call | solution.py:240
  10.4 0.1 collective-permute-start.4
  10.5 1.6 %collective-permute-start.3 = (bf16[128,512]{1,0:T(8,128)(2,1)S(1)}, bf16[128,512]{1,0:T(8,128)(2,1)S(1)}, u32[]{:S(2)}, u32[]{:S(2)}) collective-permute-start(bf16[128,512]{1,0:T(8,128)(2,1)S(1)} %get-tuple-element.37), channel_id=1, source_target_pairs={{5,6},{6,5},{7,8},{8,7},{9,10},{10,9},{11,12},{12,11},{21,22},{22,... | collective-permute-start | bytes 393224 | tf_op jit(solution)/shard_map/ppermute | solution.py:307
  12.1 2.1 %own.1 = (bf16[2048,256]{1,0:T(8,128)(2,1)}, f32[256,512]{1,0:T(8,128)S(1)}) custom-call(bf16[1024,512]{1,0:T(8,128)(2,1)S(1)} %get-tuple-element.26.order_ref.nearmsg_ref, bf16[1024,512]{1,0:T(8,128)(2,1)S(1)} %get-tuple-element.32.farmsg_ref, bf16[1024,512]{1,0:T(8,128)(2,1)S(1)} %get-tuple-element.33.nearadj_ref, ...), custom_call_target="tpu_custom_call" | custom-call | tf_op jit(solution)/shard_map/own/pallas_call | solution.py:240
  14.2 0.0 collective-permute-done.5.near_ref
  14.2 3.1 %collective-permute-done.4.first_ref = bf16[128,512]{1,0:T(8,128)(2,1)S(1)} collective-permute-done((bf16[128,512]{1,0:T(8,128)(2,1)S(1)}, bf16[128,512]{1,0:T(8,128)(2,1)S(1)}, u32[]{:S(2)}, u32[]{:S(2)}) %collective-permute-start.4) | collective-permute-done | bytes 131104 | tf_op jit(solution)/shard_map/ppermute | solution.py:308
  17.3 0.0 collective-permute-done.3.second_ref
  17.3 1.1 %last.1 = bf16[256,512]{1,0:T(8,128)(2,1)} custom-call(bf16[128,512]{1,0:T(8,128)(2,1)S(1)} %collective-permute-done.3.second_ref, bf16[128,512]{1,0:T(8,128)(2,1)S(1)} %collective-permute-done.4.first_ref, bf16[128,512]{1,0:T(8,128)(2,1)S(1)} %collective-permute-done.5.near_ref, f32[256,512]{1,0:T(8,128)S(1)} %get-tuple-element.39.grad_ref, ...), custom_call_target="tpu_custom_call" | custom-call | tf_op jit(solution)/shard_map/last/pallas_call | solution.py:240
  (8 shorter events, 0.0 us)
Async XLA Ops:
  0.6 3.6 %copy-start = (bf16[512,512]{1,0:T(8,128)(2,1)S(1)}, bf16[512,512]{1,0:T(8,128)(2,1)}, u32[]{:S(2)}) copy-start(bf16[512,512]{1,0:T(8,128)(2,1)} %wnbr_ref.9) | copy-start | bytes 1572868
  0.6 3.6 %copy-start.1 = (bf16[256,8,256]{2,1,0:T(8,128)(2,1)S(1)}, bf16[256,8,256]{2,1,0:T(8,128)(2,1)}, u32[]{:S(2)}) copy-start(bf16[256,8,256]{2,1,0:T(8,128)(2,1)} %param.13) | copy-start | bytes 3145732
  0.7 3.6 %copy-start.2 = (bf16[512,256]{1,0:T(8,128)(2,1)S(1)}, bf16[512,256]{1,0:T(8,128)(2,1)}, u32[]{:S(2)}) copy-start(bf16[512,256]{1,0:T(8,128)(2,1)} %wblk_ref.5) | copy-start | bytes 786436
  0.7 3.6 %copy-start.3 = (bf16[256,8,128]{2,1,0:T(8,128)(2,1)S(1)}, bf16[256,8,128]{2,1,0:T(8,128)(2,1)}, u32[]{:S(2)}) copy-start(bf16[256,8,128]{2,1,0:T(8,128)(2,1)} %param.10) | copy-start | bytes 1572868
  0.7 3.6 %copy-start.4 = (bf16[512,512]{1,0:T(8,128)(2,1)S(1)}, bf16[512,512]{1,0:T(8,128)(2,1)}, u32[]{:S(2)}) copy-start(bf16[512,512]{1,0:T(8,128)(2,1)} %wself_ref.3) | copy-start | bytes 1572868
  0.7 3.6 %copy-start.5 = (bf16[128,512]{1,0:T(8,128)(2,1)S(1)}, bf16[128,512]{1,0:T(8,128)(2,1)}, u32[]{:S(2)}) copy-start(bf16[128,512]{1,0:T(8,128)(2,1)} %wrad_ref.3) | copy-start | bytes 393220
  0.7 3.6 %copy-start.6 = (bf16[256,512]{1,0:T(8,128)(2,1)S(1)}, bf16[256,512]{1,0:T(8,128)(2,1)}, u32[]{:S(2)}) copy-start(bf16[256,512]{1,0:T(8,128)(2,1)} %feat_ref.1) | copy-start | bytes 786436
  1.9 3.8 %collective-permute-start = (bf16[128,512]{1,0:T(8,128)(2,1)S(1)}, bf16[128,512]{1,0:T(8,128)(2,1)S(1)}, u32[]{:S(2)}, u32[]{:S(2)}) collective-permute-start(bf16[128,512]{1,0:T(8,128)(2,1)S(1)} %get-tuple-element.23), channel_id=1, source_target_pairs={{0,1},{1,0},{2,3},{3,2},{4,5},{5,4},{6,7},{7,6},{8,9},{9,8},{10,11... | collective-permute-start | bytes 393224 | tf_op jit(solution)/shard_map/ppermute | solution.py:277
  2.6 6.6 %collective-permute-start.2 = (bf16[128,512]{1,0:T(8,128)(2,1)S(1)}, bf16[128,512]{1,0:T(8,128)(2,1)S(1)}, u32[]{:S(2)}, u32[]{:S(2)}) collective-permute-start(bf16[128,512]{1,0:T(8,128)(2,1)S(1)} %get-tuple-element.27), channel_id=1, source_target_pairs={{1,2},{2,1},{3,4},{4,3},{13,14},{14,13},{15,16},{16,15},{17,18},{1... | collective-permute-start | bytes 393224 | tf_op jit(solution)/shard_map/ppermute | solution.py:275
  3.8 5.4 %collective-permute-start.1 = (bf16[128,512]{1,0:T(8,128)(2,1)S(1)}, bf16[128,512]{1,0:T(8,128)(2,1)S(1)}, u32[]{:S(2)}, u32[]{:S(2)}) collective-permute-start(bf16[128,512]{1,0:T(8,128)(2,1)S(1)} %get-tuple-element.27), channel_id=1, source_target_pairs={{5,6},{6,5},{7,8},{8,7},{9,10},{10,9},{11,12},{12,11},{21,22},{22,... | collective-permute-start | bytes 393224 | tf_op jit(solution)/shard_map/ppermute | solution.py:276
  7.7 6.5 %collective-permute-start.5 = (bf16[128,512]{1,0:T(8,128)(2,1)S(1)}, bf16[128,512]{1,0:T(8,128)(2,1)S(1)}, u32[]{:S(2)}, u32[]{:S(2)}) collective-permute-start(bf16[128,512]{1,0:T(8,128)(2,1)S(1)} %get-tuple-element.38), channel_id=1, source_target_pairs={{0,1},{1,0},{2,3},{3,2},{4,5},{5,4},{6,7},{7,6},{8,9},{9,8},{10,11... | collective-permute-start | bytes 393224 | tf_op jit(solution)/shard_map/ppermute | solution.py:299
  10.4 6.9 %collective-permute-start.4 = (bf16[128,512]{1,0:T(8,128)(2,1)S(1)}, bf16[128,512]{1,0:T(8,128)(2,1)S(1)}, u32[]{:S(2)}, u32[]{:S(2)}) collective-permute-start(bf16[128,512]{1,0:T(8,128)(2,1)S(1)} %get-tuple-element.37), channel_id=1, source_target_pairs={{1,2},{2,1},{3,4},{4,3},{13,14},{14,13},{15,16},{16,15},{17,18},{1... | collective-permute-start | bytes 393224 | tf_op jit(solution)/shard_map/ppermute | solution.py:308
  10.5 6.8 %collective-permute-start.3 = (bf16[128,512]{1,0:T(8,128)(2,1)S(1)}, bf16[128,512]{1,0:T(8,128)(2,1)S(1)}, u32[]{:S(2)}, u32[]{:S(2)}) collective-permute-start(bf16[128,512]{1,0:T(8,128)(2,1)S(1)} %get-tuple-element.37), channel_id=1, source_target_pairs={{5,6},{6,5},{7,8},{8,7},{9,10},{10,9},{11,12},{12,11},{21,22},{22,... | collective-permute-start | bytes 393224 | tf_op jit(solution)/shard_map/ppermute | solution.py:307

commit v7 on v5

--- a/solution.py
+++ b/solution.py
@@ -180,7 +180,7 @@
 
 def own_kernel(
     nearmsg_ref, farmsg_ref, nearadj_ref, faradj_ref, nearpick_ref, farpick_ref, wself_ref, wnbr_ref, wblk_ref,
-    blocks_hbm, grad_ref,
+    blocks_hbm, grad_ref, turned_ref,
     nearblk_ref, farblk_ref, selfsum_ref, sems,
 ):
     edges = farmsg_ref.shape[0]
@@ -206,19 +206,20 @@
         selfsum_ref[pl.ds(far_off, half), :] = far_back[atoms:].astype(BF)
         total = (near_back[:atoms] + far_back[:atoms]).astype(BF)
         grad_ref[...] = mm_nt(total, wnbr_ref[...]) + mm_nt(selfsum_ref[...], wself_ref[...])
+        turned_ref[...] = wnbr_ref[...].T
 
     near_copy.wait()
     far_copy.wait()
 
 
-def last_kernel(second_ref, first_ref, near_ref, grad_ref, wnbr_ref, out_hbm, out_ref, sem, *, count):
+def last_kernel(second_ref, first_ref, near_ref, grad_ref, turned_ref, out_hbm, out_ref, sem, *, count):
     half = near_ref.shape[0]
     _, _, near_off, far_off = halves(half)
     rims = jnp.concatenate([from_across(count, first_ref, second_ref), near_ref[...]], axis=0)
     grads = jnp.concatenate(
         [grad_ref[pl.ds(far_off, half), :], grad_ref[pl.ds(near_off, half), :]], axis=0
     )
-    total = (grads + mm_nt(rims, wnbr_ref[...])).astype(BF)
+    total = (grads + mm(rims, turned_ref[...])).astype(BF)
     out_ref[pl.ds(far_off, half), :] = total[:half]
     out_ref[pl.ds(near_off, half), :] = total[half:]
     copy = pltpu.make_async_copy(out_ref, out_hbm, sem)
@@ -305,11 +306,11 @@
     )
     far_back_second = lax.ppermute(far_rim, "cell", second)
     far_back_first = lax.ppermute(far_rim, "cell", first)
-    blocks, grad = call(
+    blocks, grad, turned = call(
         own_kernel,
         "own",
         (near_msg, far_msg, near_adj, far_adj, near_pick, far_pick, w_self, w_neighbour, w_block),
-        [((2 * edges, entries), BF), ((atoms, width), F32)],
+        [((2 * edges, entries), BF), ((atoms, width), F32), ((width, width), BF)],
         16,
         scratch=[
             pltpu.VMEM((edges, entries), BF),
@@ -317,12 +318,12 @@
             pltpu.VMEM((atoms, width), BF),
             dma((2,)),
         ],
-        out_specs=[HB, VM],
+        out_specs=[HB, VM, VM],
     )
     (feat_grad,) = call(
         functools.partial(last_kernel, count=count),
         "last",
-        (far_back_second, far_back_first, near_back, grad, w_neighbour),
+        (far_back_second, far_back_first, near_back, grad, turned),
         [grad_t],
         4,
         scratch=[pltpu.VMEM((atoms, width), BF), dma],

time: 18.4 us -> 18.3 us (level)
  no operation moved by 1% of the time
where the time goes in v7:
time: 18.3 us; the launch traced here: 18.2 us
  Pallas kernels  8.63 us (47%)
  waiting for transfers between devices  4.65 us (25%)
  starting transfers between devices  4.09 us (22%)
  between operations  0.78 us (4%)
    pallas_call x6, Pallas kernels, call(): pl.pallas_call(kernel, name=name, out_shape=[jax.ShapeDtypeStruct(shape,...  8.63 us
    ppermute x1, waiting for transfers between devices, body(): far_back_first = lax.ppermute(far_rim, 'cell', first)  3.12 us
    ppermute x1, starting transfers between devices, body(): far_back_second = lax.ppermute(far_rim, 'cell', second)  1.57 us
    ppermute x1, waiting for transfers between devices, body(): far_first = lax.ppermute(far_send, 'cell', first)  1.52 us
    ppermute x1, starting transfers between devices, body(): far_first = lax.ppermute(far_send, 'cell', first)  1.17 us
    ppermute x1, starting transfers between devices, body(): near = lax.ppermute(near_send, 'cell', inside)  0.74 us
    ppermute x1, starting transfers between devices, body(): far_second = lax.ppermute(far_send, 'cell', second)  0.43 us
  transfers between devices with their start and end apart: 6, of which 2 were waited for; matrix products, arithmetic and copies ran while one was open for 0% of the time, Pallas kernels for 35%

profile of v7, /device:TPU:29, one launch (start us, length us, event | category | flops | bytes accessed | tf_op | source)
XLA Modules:
  0.0 18.2 jit_solution(11228513030567140151)
XLA Ops:
  0.6 0.0 copy-start
  0.6 0.0 copy-start.1
  0.7 1.2 %head.1 = (bf16[128,512]{1,0:T(8,128)(2,1)S(1)}, bf16[128,512]{1,0:T(8,128)(2,1)S(1)}, s32[8,256]{1,0:T(8,128)S(1)}, s32[2,128]{1,0:T(2,128)S(1)}) custom-call(bf16[256,512]{1,0:T(8,128)(2,1)} %feat_ref.1, s32[8,256]{1,0:T(8,128)} %bitcast.10, s32[2,128]{1,0:T(2,128)} %bitcast.11), custom_call_target="tpu_custom_call" | custom-call | flops 999999995904 | tf_op jit(solution)/shard_map/head/pallas_call | solution.py:240
  1.9 0.7 %collective-permute-start = (bf16[128,512]{1,0:T(8,128)(2,1)S(1)}, bf16[128,512]{1,0:T(8,128)(2,1)S(1)}, u32[]{:S(2)}, u32[]{:S(2)}) collective-permute-start(bf16[128,512]{1,0:T(8,128)(2,1)S(1)} %get-tuple-element.24), channel_id=1, source_target_pairs={{0,1},{1,0},{2,3},{3,2},{4,5},{5,4},{6,7},{7,6},{8,9},{9,8},{10,11... | collective-permute-start | bytes 393224 | tf_op jit(solution)/shard_map/ppermute | solution.py:277
  2.6 1.2 %collective-permute-start.2 = (bf16[128,512]{1,0:T(8,128)(2,1)S(1)}, bf16[128,512]{1,0:T(8,128)(2,1)S(1)}, u32[]{:S(2)}, u32[]{:S(2)}) collective-permute-start(bf16[128,512]{1,0:T(8,128)(2,1)S(1)} %get-tuple-element.28), channel_id=1, source_target_pairs={{1,2},{2,1},{3,4},{4,3},{13,14},{14,13},{15,16},{16,15},{17,18},{1... | collective-permute-start | bytes 393224 | tf_op jit(solution)/shard_map/ppermute | solution.py:275
  3.8 0.4 %collective-permute-start.1 = (bf16[128,512]{1,0:T(8,128)(2,1)S(1)}, bf16[128,512]{1,0:T(8,128)(2,1)S(1)}, u32[]{:S(2)}, u32[]{:S(2)}) collective-permute-start(bf16[128,512]{1,0:T(8,128)(2,1)S(1)} %get-tuple-element.28), channel_id=1, source_target_pairs={{5,6},{6,5},{7,8},{8,7},{9,10},{10,9},{11,12},{12,11},{21,22},{22,... | collective-permute-start | bytes 393224 | tf_op jit(solution)/shard_map/ppermute | solution.py:276
  4.2 0.0 copy-done.3
  4.2 0.0 copy-done.4
  4.2 0.0 copy-done.5
  4.3 0.0 copy-done.6
  4.3 1.4 %front.1 = (bf16[1024,512]{1,0:T(8,128)(2,1)S(1)}, bf16[1024,512]{1,0:T(8,128)(2,1)S(1)}, bf16[1024,512]{1,0:T(8,128)(2,1)S(1)}, bf16[1024,512]{1,0:T(8,128)(2,1...) custom-call(s32[8,256]{1,0:T(8,128)S(1)} %get-tuple-element.22.nbr_ref, ...), custom_call_target="tpu_custom_call" | custom-call | tf_op jit(solution)/shard_map/front/pallas_call | solution.py:240
  5.6 0.0 collective-permute-done.near_ref
  5.6 1.9 %near.1 = (bf16[1024,512]{1,0:T(8,128)(2,1)S(1)}, bf16[1024,512]{1,0:T(8,128)(2,1)S(1)}, bf16[128,512]{1,0:T(8,128)(2,1)S(1)}, bf16[1024,512]{1,0:T(8,128)(2,1)S(1)}) custom-call(s32[8,256]{1,0:T(8,128)S(1)} %get-tuple-element.22.nbr_ref, s32[2,128]{1,0:T(2,128)S(1)} %get-tuple-element.23.cnt_ref, bf16[2048,128]{1,0:T(8,128)(2,1)S(1)} %bitcast.8, ...), custom_call_target="tpu_custom_call" | custom-call | tf_op jit(solution)/shard_map/near/pallas_call | solution.py:240
  7.6 0.1 collective-permute-start.5
  7.7 1.5 %collective-permute-done.2.first_ref = bf16[128,512]{1,0:T(8,128)(2,1)S(1)} collective-permute-done((bf16[128,512]{1,0:T(8,128)(2,1)S(1)}, bf16[128,512]{1,0:T(8,128)(2,1)S(1)}, u32[]{:S(2)}, u32[]{:S(2)}) %collective-permute-start.2) | collective-permute-done | bytes 131104 | tf_op jit(solution)/shard_map/ppermute | solution.py:275
  9.2 0.0 collective-permute-done.1.second_ref
  9.2 1.0 %far.1 = (bf16[1024,512]{1,0:T(8,128)(2,1)S(1)}, bf16[1024,512]{1,0:T(8,128)(2,1)S(1)}, bf16[128,512]{1,0:T(8,128)(2,1)S(1)}) custom-call(bf16[128,512]{1,0:T(8,128)(2,1)S(1)} %collective-permute-done.1.second_ref, bf16[128,512]{1,0:T(8,128)(2,1)S(1)} %collective-permute-done.2.first_ref, bf16[512,512]{1,0:T(8,128)(2,1)S(1)} %copy-done, ...), custom_call_target="tpu_custom_call" | custom-call | tf_op jit(solution)/shard_map/far/pallas_call | solution.py:240
  10.3 0.1 collective-permute-start.4
  10.3 1.6 %collective-permute-start.3 = (bf16[128,512]{1,0:T(8,128)(2,1)S(1)}, bf16[128,512]{1,0:T(8,128)(2,1)S(1)}, u32[]{:S(2)}, u32[]{:S(2)}) collective-permute-start(bf16[128,512]{1,0:T(8,128)(2,1)S(1)} %get-tuple-element.38), channel_id=1, source_target_pairs={{5,6},{6,5},{7,8},{8,7},{9,10},{10,9},{11,12},{12,11},{21,22},{22,... | collective-permute-start | bytes 393224 | tf_op jit(solution)/shard_map/ppermute | solution.py:307
  11.9 2.1 %own.1 = (bf16[2048,256]{1,0:T(8,128)(2,1)}, f32[256,512]{1,0:T(8,128)S(1)}, bf16[512,512]{1,0:T(8,128)(2,1)S(1)}) custom-call(bf16[1024,512]{1,0:T(8,128)(2,1)S(1)} %get-tuple-element.27.order_ref.nearmsg_ref, bf16[1024,512]{1,0:T(8,128)(2,1)S(1)} %get-tuple-element.33.farmsg_ref, bf16[1024,512]{1,0:T(8,128)(2,1)S(1)} %get-tuple-element.34.nearadj_ref, ...), custom_call_target="tpu_custom_call" | custom-call | tf_op jit(solution)/shard_map/own/pallas_call | solution.py:240
  14.0 0.0 collective-permute-done.5.near_ref
  14.0 3.1 %collective-permute-done.4.first_ref = bf16[128,512]{1,0:T(8,128)(2,1)S(1)} collective-permute-done((bf16[128,512]{1,0:T(8,128)(2,1)S(1)}, bf16[128,512]{1,0:T(8,128)(2,1)S(1)}, u32[]{:S(2)}, u32[]{:S(2)}) %collective-permute-start.4) | collective-permute-done | bytes 131104 | tf_op jit(solution)/shard_map/ppermute | solution.py:308
  17.2 0.0 collective-permute-done.3.second_ref
  17.2 1.0 %last.1 = bf16[256,512]{1,0:T(8,128)(2,1)} custom-call(bf16[128,512]{1,0:T(8,128)(2,1)S(1)} %collective-permute-done.3.second_ref, bf16[128,512]{1,0:T(8,128)(2,1)S(1)} %collective-permute-done.4.first_ref, bf16[128,512]{1,0:T(8,128)(2,1)S(1)} %collective-permute-done.5.near_ref, f32[256,512]{1,0:T(8,128)S(1)} %get-tuple-element.40.grad_ref, ...), custom_call_target="tpu_custom_call" | custom-call | tf_op jit(solution)/shard_map/last/pallas_call | solution.py:240
  (8 shorter events, 0.0 us)
Async XLA Ops:
  0.6 3.6 %copy-start = (bf16[512,512]{1,0:T(8,128)(2,1)S(1)}, bf16[512,512]{1,0:T(8,128)(2,1)}, u32[]{:S(2)}) copy-start(bf16[512,512]{1,0:T(8,128)(2,1)} %wnbr_ref.7) | copy-start | bytes 1572868
  0.6 3.6 %copy-start.1 = (bf16[256,8,256]{2,1,0:T(8,128)(2,1)S(1)}, bf16[256,8,256]{2,1,0:T(8,128)(2,1)}, u32[]{:S(2)}) copy-start(bf16[256,8,256]{2,1,0:T(8,128)(2,1)} %param.13) | copy-start | bytes 3145732
  0.7 3.6 %copy-start.2 = (bf16[512,256]{1,0:T(8,128)(2,1)S(1)}, bf16[512,256]{1,0:T(8,128)(2,1)}, u32[]{:S(2)}) copy-start(bf16[512,256]{1,0:T(8,128)(2,1)} %wblk_ref.5) | copy-start | bytes 786436
  0.7 3.6 %copy-start.3 = (bf16[256,8,128]{2,1,0:T(8,128)(2,1)S(1)}, bf16[256,8,128]{2,1,0:T(8,128)(2,1)}, u32[]{:S(2)}) copy-start(bf16[256,8,128]{2,1,0:T(8,128)(2,1)} %param.10) | copy-start | bytes 1572868
  0.7 3.6 %copy-start.4 = (bf16[512,512]{1,0:T(8,128)(2,1)S(1)}, bf16[512,512]{1,0:T(8,128)(2,1)}, u32[]{:S(2)}) copy-start(bf16[512,512]{1,0:T(8,128)(2,1)} %wself_ref.3) | copy-start | bytes 1572868
  0.7 3.6 %copy-start.5 = (bf16[128,512]{1,0:T(8,128)(2,1)S(1)}, bf16[128,512]{1,0:T(8,128)(2,1)}, u32[]{:S(2)}) copy-start(bf16[128,512]{1,0:T(8,128)(2,1)} %wrad_ref.3) | copy-start | bytes 393220
  0.7 3.6 %copy-start.6 = (bf16[256,512]{1,0:T(8,128)(2,1)S(1)}, bf16[256,512]{1,0:T(8,128)(2,1)}, u32[]{:S(2)}) copy-start(bf16[256,512]{1,0:T(8,128)(2,1)} %feat_ref.1) | copy-start | bytes 786436
  1.9 3.8 %collective-permute-start = (bf16[128,512]{1,0:T(8,128)(2,1)S(1)}, bf16[128,512]{1,0:T(8,128)(2,1)S(1)}, u32[]{:S(2)}, u32[]{:S(2)}) collective-permute-start(bf16[128,512]{1,0:T(8,128)(2,1)S(1)} %get-tuple-element.24), channel_id=1, source_target_pairs={{0,1},{1,0},{2,3},{3,2},{4,5},{5,4},{6,7},{7,6},{8,9},{9,8},{10,11... | collective-permute-start | bytes 393224 | tf_op jit(solution)/shard_map/ppermute | solution.py:277
  2.6 6.6 %collective-permute-start.2 = (bf16[128,512]{1,0:T(8,128)(2,1)S(1)}, bf16[128,512]{1,0:T(8,128)(2,1)S(1)}, u32[]{:S(2)}, u32[]{:S(2)}) collective-permute-start(bf16[128,512]{1,0:T(8,128)(2,1)S(1)} %get-tuple-element.28), channel_id=1, source_target_pairs={{1,2},{2,1},{3,4},{4,3},{13,14},{14,13},{15,16},{16,15},{17,18},{1... | collective-permute-start | bytes 393224 | tf_op jit(solution)/shard_map/ppermute | solution.py:275
  3.8 5.4 %collective-permute-start.1 = (bf16[128,512]{1,0:T(8,128)(2,1)S(1)}, bf16[128,512]{1,0:T(8,128)(2,1)S(1)}, u32[]{:S(2)}, u32[]{:S(2)}) collective-permute-start(bf16[128,512]{1,0:T(8,128)(2,1)S(1)} %get-tuple-element.28), channel_id=1, source_target_pairs={{5,6},{6,5},{7,8},{8,7},{9,10},{10,9},{11,12},{12,11},{21,22},{22,... | collective-permute-start | bytes 393224 | tf_op jit(solution)/shard_map/ppermute | solution.py:276
  7.6 6.4 %collective-permute-start.5 = (bf16[128,512]{1,0:T(8,128)(2,1)S(1)}, bf16[128,512]{1,0:T(8,128)(2,1)S(1)}, u32[]{:S(2)}, u32[]{:S(2)}) collective-permute-start(bf16[128,512]{1,0:T(8,128)(2,1)S(1)} %get-tuple-element.39), channel_id=1, source_target_pairs={{0,1},{1,0},{2,3},{3,2},{4,5},{5,4},{6,7},{7,6},{8,9},{9,8},{10,11... | collective-permute-start | bytes 393224 | tf_op jit(solution)/shard_map/ppermute | solution.py:299
  10.3 6.9 %collective-permute-start.4 = (bf16[128,512]{1,0:T(8,128)(2,1)S(1)}, bf16[128,512]{1,0:T(8,128)(2,1)S(1)}, u32[]{:S(2)}, u32[]{:S(2)}) collective-permute-start(bf16[128,512]{1,0:T(8,128)(2,1)S(1)} %get-tuple-element.38), channel_id=1, source_target_pairs={{1,2},{2,1},{3,4},{4,3},{13,14},{14,13},{15,16},{16,15},{17,18},{1... | collective-permute-start | bytes 393224 | tf_op jit(solution)/shard_map/ppermute | solution.py:308
  10.3 6.8 %collective-permute-start.3 = (bf16[128,512]{1,0:T(8,128)(2,1)S(1)}, bf16[128,512]{1,0:T(8,128)(2,1)S(1)}, u32[]{:S(2)}, u32[]{:S(2)}) collective-permute-start(bf16[128,512]{1,0:T(8,128)(2,1)S(1)} %get-tuple-element.38), channel_id=1, source_target_pairs={{5,6},{6,5},{7,8},{8,7},{9,10},{10,9},{11,12},{12,11},{21,22},{22,... | collective-permute-start | bytes 393224 | tf_op jit(solution)/shard_map/ppermute | solution.py:307

commit v8 on v7

--- a/solution.py
+++ b/solution.py
@@ -100,7 +100,7 @@
     ]
     copies = [pltpu.make_async_copy(src, dst, sems.at[n]) for n, (src, dst) in enumerate(pairs)]
     for copy in copies:
-        copy.start()
+        copy.start(priority=1)
     for copy in copies:
         copy.wait()
 

time: 18.3 us -> 18.3 us (level)
  no operation moved by 1% of the time
where the time goes in v8:
time: 18.3 us; the launch traced here: 18.2 us
  Pallas kernels  8.63 us (47%)
  waiting for transfers between devices  4.65 us (25%)
  starting transfers between devices  4.09 us (22%)
  between operations  0.78 us (4%)
    pallas_call x6, Pallas kernels, call(): pl.pallas_call(kernel, name=name, out_shape=[jax.ShapeDtypeStruct(shape,...  8.63 us
    ppermute x1, waiting for transfers between devices, body(): far_back_first = lax.ppermute(far_rim, 'cell', first)  3.12 us
    ppermute x1, starting transfers between devices, body(): far_back_second = lax.ppermute(far_rim, 'cell', second)  1.57 us
    ppermute x1, waiting for transfers between devices, body(): far_first = lax.ppermute(far_send, 'cell', first)  1.52 us
    ppermute x1, starting transfers between devices, body(): far_first = lax.ppermute(far_send, 'cell', first)  1.17 us
    ppermute x1, starting transfers between devices, body(): near = lax.ppermute(near_send, 'cell', inside)  0.74 us
    ppermute x1, starting transfers between devices, body(): far_second = lax.ppermute(far_send, 'cell', second)  0.43 us
  transfers between devices with their start and end apart: 6, of which 2 were waited for; matrix products, arithmetic and copies ran while one was open for 0% of the time, Pallas kernels for 35%

profile of v8, /device:TPU:29, one launch (start us, length us, event | category | flops | bytes accessed | tf_op | source)
XLA Modules:
  0.0 18.2 jit_solution(14385785110529794527)
XLA Ops:
  0.6 0.0 copy-start
  0.6 0.0 copy-start.1
  0.7 1.2 %head.1 = (bf16[128,512]{1,0:T(8,128)(2,1)S(1)}, bf16[128,512]{1,0:T(8,128)(2,1)S(1)}, s32[8,256]{1,0:T(8,128)S(1)}, s32[2,128]{1,0:T(2,128)S(1)}) custom-call(bf16[256,512]{1,0:T(8,128)(2,1)} %feat_ref.1, s32[8,256]{1,0:T(8,128)} %bitcast.10, s32[2,128]{1,0:T(2,128)} %bitcast.11), custom_call_target="tpu_custom_call" | custom-call | flops 999999995904 | tf_op jit(solution)/shard_map/head/pallas_call | solution.py:240
  1.9 0.7 %collective-permute-start = (bf16[128,512]{1,0:T(8,128)(2,1)S(1)}, bf16[128,512]{1,0:T(8,128)(2,1)S(1)}, u32[]{:S(2)}, u32[]{:S(2)}) collective-permute-start(bf16[128,512]{1,0:T(8,128)(2,1)S(1)} %get-tuple-element.24), channel_id=1, source_target_pairs={{0,1},{1,0},{2,3},{3,2},{4,5},{5,4},{6,7},{7,6},{8,9},{9,8},{10,11... | collective-permute-start | bytes 393224 | tf_op jit(solution)/shard_map/ppermute | solution.py:277
  2.6 1.2 %collective-permute-start.2 = (bf16[128,512]{1,0:T(8,128)(2,1)S(1)}, bf16[128,512]{1,0:T(8,128)(2,1)S(1)}, u32[]{:S(2)}, u32[]{:S(2)}) collective-permute-start(bf16[128,512]{1,0:T(8,128)(2,1)S(1)} %get-tuple-element.28), channel_id=1, source_target_pairs={{1,2},{2,1},{3,4},{4,3},{13,14},{14,13},{15,16},{16,15},{17,18},{1... | collective-permute-start | bytes 393224 | tf_op jit(solution)/shard_map/ppermute | solution.py:275
  3.8 0.4 %collective-permute-start.1 = (bf16[128,512]{1,0:T(8,128)(2,1)S(1)}, bf16[128,512]{1,0:T(8,128)(2,1)S(1)}, u32[]{:S(2)}, u32[]{:S(2)}) collective-permute-start(bf16[128,512]{1,0:T(8,128)(2,1)S(1)} %get-tuple-element.28), channel_id=1, source_target_pairs={{5,6},{6,5},{7,8},{8,7},{9,10},{10,9},{11,12},{12,11},{21,22},{22,... | collective-permute-start | bytes 393224 | tf_op jit(solution)/shard_map/ppermute | solution.py:276
  4.2 0.0 copy-done.3
  4.2 0.0 copy-done.4
  4.2 0.0 copy-done.5
  4.3 0.0 copy-done.6
  4.3 1.4 %front.1 = (bf16[1024,512]{1,0:T(8,128)(2,1)S(1)}, bf16[1024,512]{1,0:T(8,128)(2,1)S(1)}, bf16[1024,512]{1,0:T(8,128)(2,1)S(1)}, bf16[1024,512]{1,0:T(8,128)(2,1...) custom-call(s32[8,256]{1,0:T(8,128)S(1)} %get-tuple-element.22.nbr_ref, ...), custom_call_target="tpu_custom_call" | custom-call | tf_op jit(solution)/shard_map/front/pallas_call | solution.py:240
  5.6 0.0 collective-permute-done.near_ref
  5.6 1.9 %near.1 = (bf16[1024,512]{1,0:T(8,128)(2,1)S(1)}, bf16[1024,512]{1,0:T(8,128)(2,1)S(1)}, bf16[128,512]{1,0:T(8,128)(2,1)S(1)}, bf16[1024,512]{1,0:T(8,128)(2,1)S(1)}) custom-call(s32[8,256]{1,0:T(8,128)S(1)} %get-tuple-element.22.nbr_ref, s32[2,128]{1,0:T(2,128)S(1)} %get-tuple-element.23.cnt_ref, bf16[2048,128]{1,0:T(8,128)(2,1)S(1)} %bitcast.8, ...), custom_call_target="tpu_custom_call" | custom-call | tf_op jit(solution)/shard_map/near/pallas_call | solution.py:240
  7.6 0.1 collective-permute-start.5
  7.7 1.5 %collective-permute-done.2.first_ref = bf16[128,512]{1,0:T(8,128)(2,1)S(1)} collective-permute-done((bf16[128,512]{1,0:T(8,128)(2,1)S(1)}, bf16[128,512]{1,0:T(8,128)(2,1)S(1)}, u32[]{:S(2)}, u32[]{:S(2)}) %collective-permute-start.2) | collective-permute-done | bytes 131104 | tf_op jit(solution)/shard_map/ppermute | solution.py:275
  9.2 0.0 collective-permute-done.1.second_ref
  9.2 1.0 %far.1 = (bf16[1024,512]{1,0:T(8,128)(2,1)S(1)}, bf16[1024,512]{1,0:T(8,128)(2,1)S(1)}, bf16[128,512]{1,0:T(8,128)(2,1)S(1)}) custom-call(bf16[128,512]{1,0:T(8,128)(2,1)S(1)} %collective-permute-done.1.second_ref, bf16[128,512]{1,0:T(8,128)(2,1)S(1)} %collective-permute-done.2.first_ref, bf16[512,512]{1,0:T(8,128)(2,1)S(1)} %copy-done, ...), custom_call_target="tpu_custom_call" | custom-call | tf_op jit(solution)/shard_map/far/pallas_call | solution.py:240
  10.3 0.1 collective-permute-start.4
  10.3 1.6 %collective-permute-start.3 = (bf16[128,512]{1,0:T(8,128)(2,1)S(1)}, bf16[128,512]{1,0:T(8,128)(2,1)S(1)}, u32[]{:S(2)}, u32[]{:S(2)}) collective-permute-start(bf16[128,512]{1,0:T(8,128)(2,1)S(1)} %get-tuple-element.38), channel_id=1, source_target_pairs={{5,6},{6,5},{7,8},{8,7},{9,10},{10,9},{11,12},{12,11},{21,22},{22,... | collective-permute-start | bytes 393224 | tf_op jit(solution)/shard_map/ppermute | solution.py:307
  11.9 2.1 %own.1 = (bf16[2048,256]{1,0:T(8,128)(2,1)}, f32[256,512]{1,0:T(8,128)S(1)}, bf16[512,512]{1,0:T(8,128)(2,1)S(1)}) custom-call(bf16[1024,512]{1,0:T(8,128)(2,1)S(1)} %get-tuple-element.27.order_ref.nearmsg_ref, bf16[1024,512]{1,0:T(8,128)(2,1)S(1)} %get-tuple-element.33.farmsg_ref, bf16[1024,512]{1,0:T(8,128)(2,1)S(1)} %get-tuple-element.34.nearadj_ref, ...), custom_call_target="tpu_custom_call" | custom-call | tf_op jit(solution)/shard_map/own/pallas_call | solution.py:240
  14.0 0.0 collective-permute-done.5.near_ref
  14.0 3.1 %collective-permute-done.4.first_ref = bf16[128,512]{1,0:T(8,128)(2,1)S(1)} collective-permute-done((bf16[128,512]{1,0:T(8,128)(2,1)S(1)}, bf16[128,512]{1,0:T(8,128)(2,1)S(1)}, u32[]{:S(2)}, u32[]{:S(2)}) %collective-permute-start.4) | collective-permute-done | bytes 131104 | tf_op jit(solution)/shard_map/ppermute | solution.py:308
  17.2 0.0 collective-permute-done.3.second_ref
  17.2 1.0 %last.1 = bf16[256,512]{1,0:T(8,128)(2,1)} custom-call(bf16[128,512]{1,0:T(8,128)(2,1)S(1)} %collective-permute-done.3.second_ref, bf16[128,512]{1,0:T(8,128)(2,1)S(1)} %collective-permute-done.4.first_ref, bf16[128,512]{1,0:T(8,128)(2,1)S(1)} %collective-permute-done.5.near_ref, f32[256,512]{1,0:T(8,128)S(1)} %get-tuple-element.40.grad_ref, ...), custom_call_target="tpu_custom_call" | custom-call | tf_op jit(solution)/shard_map/last/pallas_call | solution.py:240
  (8 shorter events, 0.0 us)
Async XLA Ops:
  0.6 3.6 %copy-start = (bf16[512,512]{1,0:T(8,128)(2,1)S(1)}, bf16[512,512]{1,0:T(8,128)(2,1)}, u32[]{:S(2)}) copy-start(bf16[512,512]{1,0:T(8,128)(2,1)} %wnbr_ref.7) | copy-start | bytes 1572868
  0.6 3.6 %copy-start.1 = (bf16[256,8,256]{2,1,0:T(8,128)(2,1)S(1)}, bf16[256,8,256]{2,1,0:T(8,128)(2,1)}, u32[]{:S(2)}) copy-start(bf16[256,8,256]{2,1,0:T(8,128)(2,1)} %param.13) | copy-start | bytes 3145732
  0.7 3.6 %copy-start.2 = (bf16[512,256]{1,0:T(8,128)(2,1)S(1)}, bf16[512,256]{1,0:T(8,128)(2,1)}, u32[]{:S(2)}) copy-start(bf16[512,256]{1,0:T(8,128)(2,1)} %wblk_ref.5) | copy-start | bytes 786436
  0.7 3.6 %copy-start.3 = (bf16[256,8,128]{2,1,0:T(8,128)(2,1)S(1)}, bf16[256,8,128]{2,1,0:T(8,128)(2,1)}, u32[]{:S(2)}) copy-start(bf16[256,8,128]{2,1,0:T(8,128)(2,1)} %param.10) | copy-start | bytes 1572868
  0.7 3.6 %copy-start.4 = (bf16[512,512]{1,0:T(8,128)(2,1)S(1)}, bf16[512,512]{1,0:T(8,128)(2,1)}, u32[]{:S(2)}) copy-start(bf16[512,512]{1,0:T(8,128)(2,1)} %wself_ref.3) | copy-start | bytes 1572868
  0.7 3.6 %copy-start.5 = (bf16[128,512]{1,0:T(8,128)(2,1)S(1)}, bf16[128,512]{1,0:T(8,128)(2,1)}, u32[]{:S(2)}) copy-start(bf16[128,512]{1,0:T(8,128)(2,1)} %wrad_ref.3) | copy-start | bytes 393220
  0.7 3.6 %copy-start.6 = (bf16[256,512]{1,0:T(8,128)(2,1)S(1)}, bf16[256,512]{1,0:T(8,128)(2,1)}, u32[]{:S(2)}) copy-start(bf16[256,512]{1,0:T(8,128)(2,1)} %feat_ref.1) | copy-start | bytes 786436
  1.9 3.8 %collective-permute-start = (bf16[128,512]{1,0:T(8,128)(2,1)S(1)}, bf16[128,512]{1,0:T(8,128)(2,1)S(1)}, u32[]{:S(2)}, u32[]{:S(2)}) collective-permute-start(bf16[128,512]{1,0:T(8,128)(2,1)S(1)} %get-tuple-element.24), channel_id=1, source_target_pairs={{0,1},{1,0},{2,3},{3,2},{4,5},{5,4},{6,7},{7,6},{8,9},{9,8},{10,11... | collective-permute-start | bytes 393224 | tf_op jit(solution)/shard_map/ppermute | solution.py:277
  2.6 6.6 %collective-permute-start.2 = (bf16[128,512]{1,0:T(8,128)(2,1)S(1)}, bf16[128,512]{1,0:T(8,128)(2,1)S(1)}, u32[]{:S(2)}, u32[]{:S(2)}) collective-permute-start(bf16[128,512]{1,0:T(8,128)(2,1)S(1)} %get-tuple-element.28), channel_id=1, source_target_pairs={{1,2},{2,1},{3,4},{4,3},{13,14},{14,13},{15,16},{16,15},{17,18},{1... | collective-permute-start | bytes 393224 | tf_op jit(solution)/shard_map/ppermute | solution.py:275
  3.8 5.4 %collective-permute-start.1 = (bf16[128,512]{1,0:T(8,128)(2,1)S(1)}, bf16[128,512]{1,0:T(8,128)(2,1)S(1)}, u32[]{:S(2)}, u32[]{:S(2)}) collective-permute-start(bf16[128,512]{1,0:T(8,128)(2,1)S(1)} %get-tuple-element.28), channel_id=1, source_target_pairs={{5,6},{6,5},{7,8},{8,7},{9,10},{10,9},{11,12},{12,11},{21,22},{22,... | collective-permute-start | bytes 393224 | tf_op jit(solution)/shard_map/ppermute | solution.py:276
  7.6 6.4 %collective-permute-start.5 = (bf16[128,512]{1,0:T(8,128)(2,1)S(1)}, bf16[128,512]{1,0:T(8,128)(2,1)S(1)}, u32[]{:S(2)}, u32[]{:S(2)}) collective-permute-start(bf16[128,512]{1,0:T(8,128)(2,1)S(1)} %get-tuple-element.39), channel_id=1, source_target_pairs={{0,1},{1,0},{2,3},{3,2},{4,5},{5,4},{6,7},{7,6},{8,9},{9,8},{10,11... | collective-permute-start | bytes 393224 | tf_op jit(solution)/shard_map/ppermute | solution.py:299
  10.3 6.9 %collective-permute-start.4 = (bf16[128,512]{1,0:T(8,128)(2,1)S(1)}, bf16[128,512]{1,0:T(8,128)(2,1)S(1)}, u32[]{:S(2)}, u32[]{:S(2)}) collective-permute-start(bf16[128,512]{1,0:T(8,128)(2,1)S(1)} %get-tuple-element.38), channel_id=1, source_target_pairs={{1,2},{2,1},{3,4},{4,3},{13,14},{14,13},{15,16},{16,15},{17,18},{1... | collective-permute-start | bytes 393224 | tf_op jit(solution)/shard_map/ppermute | solution.py:308
  10.3 6.8 %collective-permute-start.3 = (bf16[128,512]{1,0:T(8,128)(2,1)S(1)}, bf16[128,512]{1,0:T(8,128)(2,1)S(1)}, u32[]{:S(2)}, u32[]{:S(2)}) collective-permute-start(bf16[128,512]{1,0:T(8,128)(2,1)S(1)} %get-tuple-element.38), channel_id=1, source_target_pairs={{5,6},{6,5},{7,8},{8,7},{9,10},{10,9},{11,12},{12,11},{21,22},{22,... | collective-permute-start | bytes 393224 | tf_op jit(solution)/shard_map/ppermute | solution.py:307
